TPU v7x, 32 devices: a whole 2x2x4 slice. The times are simulated.
32 devices in a mesh: comp: 2 (over x), mr: 16 (over z, y, core).
Axes of the slice: x: 2, y: 2, z: 4, core: 2. Of those that a mesh axis runs over, the one named last changes fastest.
Arguments:
- spectrum: float32 [2, 1024, 2, 64, 512], P('comp', 'mr'), may hold values from -6 to 6
- radial_basis: bfloat16 [1024, 1024, 512], P('mr'), may hold values from -0.25 to 0.25
- cutoff: int32 [1024], P('mr'), may hold values from 128 to 512, as said below
- couplings: float32 [2, 2], replicated, may hold values from 0.5 to 1.5
- trap_potential: float32 [1024], replicated, may hold values from 0 to 2
- weights: float32 [1024], replicated, may hold values from 0.25 to 0.75
Outputs:
- evolved: float32 [2, 1024, 2, 64, 512], P('comp', 'mr')
Inputs may be any that keep to these rules, and one draw needn't show every extreme that they name: cutoff[m] is the number of Laguerre degrees kept for angular mode m; degrees from cutoff[m] on are dropped.
All inputs are finite; a program needn't handle non-finite values.
Results may differ from a plain program's by a relative error of at most 0.0089.
Values may be sent and summed in bfloat16 or wider, within the bound.
No kernel may reach another device: no remote copies, remote signals or barrier semaphores. Data moves between devices by JAX's collectives and lax.ppermute only.
A program may use at most 320 MiB of HBM per device.

v0:
```python
import math

import jax
import jax.numpy as jnp
from jax import lax
from jax.sharding import PartitionSpec as P

TIMESTEP = 0.5
ROTATION = 0.7


def spectral_tables(mode_total):
    ordinal = jnp.arange(mode_total, dtype=jnp.int32)
    product = ordinal[:, None] * ordinal[None, :] % mode_total
    angles = product.astype(jnp.float32) * (2.0 * math.pi / mode_total)
    normalizer = 1.0 / math.sqrt(mode_total)
    return (
        (jnp.cos(angles) * normalizer).astype(jnp.bfloat16),
        (jnp.sin(angles) * normalizer).astype(jnp.bfloat16),
    )


def rotate(real_part, imag_part, phase_angle):
    cosine = jnp.cos(phase_angle)
    sine_value = jnp.sin(phase_angle)
    return (
        real_part * cosine + imag_part * sine_value,
        imag_part * cosine - real_part * sine_value,
    )


def forward_modes(cosine_table, sine_table, radial, planes):
    cosine_term = jnp.einsum(
        "am,rmk->rak", cosine_table, radial, preferred_element_type=jnp.float32
    )
    sine_term = jnp.einsum("am,rmk->rak", sine_table, radial, preferred_element_type=jnp.float32)
    real_part = cosine_term[..., :planes] - sine_term[..., planes:]
    imag_part = sine_term[..., :planes] + cosine_term[..., planes:]
    return (real_part, imag_part)


def inverse_modes(cosine_table, sine_table, kicked, planes):
    cosine_back = jnp.einsum(
        "am,rak->rmk", cosine_table, kicked, preferred_element_type=jnp.float32
    )
    sine_back = jnp.einsum("am,rak->rmk", sine_table, kicked, preferred_element_type=jnp.float32)
    back_real = cosine_back[..., :planes] + sine_back[..., planes:]
    back_imag = cosine_back[..., planes:] - sine_back[..., :planes]
    return jnp.concatenate([back_real, back_imag], -1)


def on_device(spectrum, radial_basis, cutoff, couplings, trap_potential, weights):
    local_modes = spectrum.shape[1]
    planes = spectrum.shape[3]
    degrees = spectrum.shape[4]
    radius_count = radial_basis.shape[1]
    mode_width = lax.axis_size("mr")
    mode_total = local_modes * mode_width
    first_mode = lax.axis_index("mr") * local_modes
    mode_ids = first_mode + jnp.arange(local_modes, dtype=jnp.int32)
    signed = jnp.where(mode_ids < mode_total // 2, mode_ids, mode_ids - mode_total).astype(
        jnp.float32
    )
    degree_ids = jnp.arange(degrees, dtype=jnp.int32)
    energy = (
        2.0 * degree_ids.astype(jnp.float32)[None, :]
        + (jnp.abs(signed) + 1.0 - ROTATION * signed)[:, None]
    )
    kinetic_phase = TIMESTEP * energy
    kept_mask = (degree_ids[None, :] < cutoff[:, None]).astype(jnp.float32)
    spin_real, spin_imag = rotate(spectrum[0, :, 0], spectrum[0, :, 1], kinetic_phase[:, None, :])
    coeffs = jnp.concatenate(
        [spin_real * kept_mask[:, None, :], spin_imag * kept_mask[:, None, :]], axis=1
    ).astype(jnp.bfloat16)
    synthesized = jnp.einsum(
        "mkn,mrn->rmk", coeffs, radial_basis, preferred_element_type=jnp.float32
    ).astype(jnp.bfloat16)
    cosine_table, sine_table = spectral_tables(mode_total)
    row_count = radius_count // (2 * mode_width)
    first_row = (lax.axis_index("comp") * mode_width + lax.axis_index("mr")) * row_count
    trap_rows = lax.dynamic_slice_in_dim(trap_potential, first_row, row_count)
    weight_rows = lax.dynamic_slice_in_dim(weights, first_row, row_count)
    radial = lax.all_to_all(synthesized, ("comp", "mr"), split_axis=0, concat_axis=1, tiled=True)
    paired = radial.reshape(row_count * 2, mode_total, 2 * planes)
    real_part, imag_part = forward_modes(cosine_table, sine_table, paired, planes)
    real_part = real_part.reshape(row_count, 2, mode_total, planes)
    imag_part = imag_part.reshape(row_count, 2, mode_total, planes)
    density = real_part * real_part + imag_part * imag_part
    partner = density[:, ::-1]
    self_strength = couplings[:, 0][None, :, None, None]
    cross_strength = couplings[:, 1][None, :, None, None]
    phase_angle = TIMESTEP * (
        self_strength * density + cross_strength * partner + trap_rows[:, None, None, None]
    )
    kick_real, kick_imag = rotate(real_part, imag_part, phase_angle)
    kicked = (
        jnp.concatenate([kick_real, kick_imag], -1)
        .astype(jnp.bfloat16)
        .reshape(row_count * 2, mode_total, 2 * planes)
    )
    weighted = (
        inverse_modes(cosine_table, sine_table, kicked, planes).reshape(
            row_count, 2, mode_total, 2 * planes
        )
        * weight_rows[:, None, None, None]
    )
    analysis_input = weighted.astype(jnp.bfloat16).reshape(row_count, 2 * mode_total, 2 * planes)
    gathered_modes = lax.all_to_all(
        analysis_input, ("comp", "mr"), split_axis=1, concat_axis=0, tiled=True
    )
    evolved = (
        jnp.einsum("rmk,mrn->mkn", gathered_modes, radial_basis, preferred_element_type=jnp.float32)
        * kept_mask[:, None, :]
    )
    return evolved.reshape(1, local_modes, 2, planes, degrees)


def solution(mesh):
    in_specs = (P("comp", "mr", None, None, None), P("mr", None, None), P("mr"), P(), P(), P())
    out_specs = P("comp", "mr", None, None, None)
    return jax.shard_map(
        on_device, mesh=mesh, in_specs=in_specs, out_specs=out_specs, check_vma=False
    )
```

profile of v0, /device:TPU:0, one launch (start us, length us, event | category | flops | bytes accessed | tf_op | source)
XLA Modules:
  0.0 1249.6 jit_solution(6855612835412474267)
XLA Ops:
  1.3 9.6 fusion.13
  11.0 36.1 %convert_bitcast_fusion = bf16[1024,64,128]{0,2,1:T(8,128)(2,1)} fusion(bf16[64,1024,512]{2,1,0:T(8,128)(2,1)} %param.7, bf16[64,64,512]{2,1,0:T(8,128)(2,1)} %get-tuple-element.14, bf16[64,64,512]{2,1,0:T(8,128)(2,1)} %get-tuple-element.13), kind=kOutput, calls=%fused_computation.14 | convolution fusion | flops 8615100416 | bytes 92274688 | tf_op jit(solution)/shard_map/mkn,mrn->rmk/dot_general | solution.py:75
  47.0 22.7 %copy.20 = bf16[1024,64,128]{2,1,0:T(8,128)(2,1)} copy(bf16[1024,64,128]{0,2,1:T(8,128)(2,1)} %convert_bitcast_fusion) | data formatting | bytes 33554432 | tf_op jit(solution)/shard_map/convert_element_type | solution.py:77
  69.7 7.7 all-to-all-start
  79.6 16.5 %fusion.71 = bf16[1024,1024,1]{1,0,2:T(8,128)(2,1)} fusion(), kind=kLoop, calls=%fused_computation.46.clone.clone.2 | loop fusion | flops 16777216 | bytes 2097152 | tf_op jit(solution)/shard_map/am,rak->rmk/dot_general | solution.py:43
  96.1 16.5 %fusion.69 = bf16[1024,1024,1]{1,0,2:T(8,128)(2,1)} fusion(), kind=kLoop, calls=%fused_computation.47.clone.clone.2 | loop fusion | flops 16777216 | bytes 2097152 | tf_op jit(solution)/shard_map/am,rak->rmk/dot_general | solution.py:46
  112.6 331.1 %all-to-all-done = bf16[1024,64,128]{2,1,0:T(8,128)(2,1)} async-done(((bf16[1024,64,128]{2,1,0:T(8,128)(2,1)}), bf16[1024,64,128]{2,1,0:T(8,128)(2,1)}, u32[]{:S(2)}, u32[]{:S(2)}) %all-to-all-start) | async-done | bytes 16777248 | tf_op jit(solution)/shard_map/all_to_all | solution.py:83
  443.7 8.3 copy.21
  452.0 30.1 %convolution_bitcast_fusion.2 = f32[64,1024,128]{1,2,0:T(8,128)} fusion(bf16[64,1024,128]{2,1,0:T(8,128)(2,1)S(1)} %bitcast.91), kind=kOutput, calls=%fused_computation.17 | convolution fusion | flops 17196646400 | bytes 50331648 | tf_op jit(solution)/shard_map/am,rmk->rak/dot_general | solution.py:36
  482.2 30.5 %convolution_bitcast_fusion.3 = f32[64,1024,128]{1,2,0:T(8,128)} fusion(bf16[64,1024,128]{2,1,0:T(8,128)(2,1)S(1)} %bitcast.92), kind=kOutput, calls=%fused_computation.18 | convolution fusion | flops 17196646400 | bytes 50331648 | tf_op jit(solution)/shard_map/am,rmk->rak/dot_general | solution.py:33
  512.6 34.1 %slice_add_fusion.1 = (f32[64,1024,64]{1,2,0:T(8,128)}, f32[64,1024,64]{1,2,0:T(8,128)}) fusion(f32[64,1024,128]{1,2,0:T(8,128)} %convolution_bitcast_fusion.3, f32[64,1024,128]{1,2,0:T(8,128)} %convolution_bitcast_fusion.2), kind=kLoop, calls=%fused_computation.5 | loop fusion | flops 8388608 | bytes 100663296 | tf_op jit(solution)/shard_map/add | solution.py:38
  546.7 18.3 %multiply_add_fusion = f32[32,2,1024,64]{2,3,1,0:T(8,128)} fusion(f32[32,2,1024,64]{2,3,1,0:T(8,128)} %bitcast.82, f32[32,2,1024,64]{2,3,1,0:T(8,128)} %bitcast.86), kind=kLoop, calls=%fused_computation.13 | loop fusion | flops 12582912 | bytes 50331648 | tf_op jit(solution)/shard_map/add | solution.py:88
  565.4 1.7 slice-done.2
  568.2 72.4 %add_convert_fusion = (bf16[32,2,1024,64]{2,3,1,0:T(8,128)(2,1)}, bf16[32,2,1024,64]{2,3,1,0:T(8,128)(2,1)}) fusion(f32[32,2,1024,64]{2,3,1,0:T(8,128)S(1)} %bitcast.85, f32[32,2,1024,64]{2,3,1,0:T(8,128)} %bitcast.87, f32[32,2,1024,64]{2,3,1,0:T(8,128)} %multiply_add_fusion, f32[32]{0:T(128)S(1)} %dynamic_slice.6, f32[2]{0:T(128)S(1)} %get-tuple-element.6, ...), kind=kLoop, calls=%fused_computation.11 | loop fusion | flops 54525952 | bytes 67109008 | tf_op jit(solution)/shard_map/convert.3
  640.7 25.6 %convolution_bitcast_fusion.1 = f32[64,1024,128]{1,2,0:T(8,128)} fusion(bf16[64,1024,64]{1,2,0:T(8,128)(2,1)} %bitcast.95, bf16[64,1024,64]{1,2,0:T(8,128)(2,1)} %bitcast.93, bf16[1024,1024,1]{1,0,2:T(8,128)(2,1)S(1)} %copy-done.1), kind=kOutput, calls=%fused_computation.16 | convolution fusion | flops 17213423616 | bytes 52428800 | tf_op jit(solution)/shard_map/am,rak->rmk/dot_general | solution.py:43
  666.2 25.6 %convolution_bitcast_fusion = f32[64,1024,128]{1,2,0:T(8,128)} fusion(bf16[64,1024,64]{1,2,0:T(8,128)(2,1)} %bitcast.96, bf16[64,1024,64]{1,2,0:T(8,128)(2,1)} %bitcast.94, bf16[1024,1024,1]{1,0,2:T(8,128)(2,1)S(1)} %copy-done), kind=kOutput, calls=%fused_computation.15 | convolution fusion | flops 17213423616 | bytes 52428800 | tf_op jit(solution)/shard_map/am,rak->rmk/dot_general | solution.py:46
  691.8 34.1 %slice_add_fusion = (f32[64,1024,64]{1,2,0:T(8,128)}, f32[64,1024,64]{1,2,0:T(8,128)}) fusion(f32[64,1024,128]{1,2,0:T(8,128)} %convolution_bitcast_fusion, f32[64,1024,128]{1,2,0:T(8,128)} %convolution_bitcast_fusion.1), kind=kLoop, calls=%fused_computation.4 | loop fusion | flops 8388608 | bytes 100663296 | tf_op jit(solution)/shard_map/add | solution.py:47
  725.9 23.5 %pad_maximum_fusion = f32[64,1024,128]{1,2,0:T(8,128)} fusion(f32[64,1024,64]{1,2,0:T(8,128)} %get-tuple-element.8, f32[64,1024,64]{1,2,0:T(8,128)} %get-tuple-element.7), kind=kLoop, calls=%fused_computation | loop fusion | flops 8388608 | bytes 67108864 | tf_op jit(solution)/shard_map/concatenate | solution.py:49
  749.4 33.4 %copy.24 = f32[64,1024,128]{2,1,0:T(8,128)} copy(f32[64,1024,128]{1,2,0:T(8,128)} %pad_maximum_fusion) | data formatting | bytes 67108864 | tf_op jit(solution)/shard_map/concatenate | solution.py:49
  782.8 12.4 fusion
  795.2 42.8 %copy.25 = bf16[32,2048,128]{2,0,1:T(8,128)(2,1)S(1)} copy(bf16[32,2048,128]{2,1,0:T(8,128)(2,1)S(1)} %fusion) | data formatting | bytes 33554432 | tf_op jit(solution)/shard_map/convert_element_type | solution.py:107
  838.1 366.6 %all_to_all.33 = bf16[32,2048,128]{2,0,1:T(8,128)(2,1)S(1)} all-to-all(bf16[32,2048,128]{2,0,1:T(8,128)(2,1)S(1)} %copy.25), channel_id=1, replica_groups=mesh['comp'=2,'mr'=16] {'comp','mr'}, dimensions={1} | all-to-all | bytes 33554432 | tf_op jit(solution)/shard_map/all_to_all | solution.py:108
  1204.7 8.9 copy.27
  1213.6 35.7 %fusion.5 = f32[64,128,512]{2,1,0:T(8,128)} fusion(bf16[64,1024,512]{2,1,0:T(8,128)(2,1)} %param.7, bf16[1024,64,128]{2,1,0:T(8,128)(2,1)} %bitcast.89, f32[64,512]{1,0:T(8,128)S(1)} %copy-done.3), kind=kOutput, calls=%fused_computation.21 | convolution fusion | flops 8594128896 | bytes 100794368 | tf_op jit(solution)/shard_map/rmk,mrn->mkn/dot_general | solution.py:112
  (27 shorter events, 5.1 us)
Async XLA Ops:
  0.8 10.2 copy-start.2
  69.7 9.7 copy-start.4
  69.7 374.1 %all-to-all-start = ((bf16[1024,64,128]{2,1,0:T(8,128)(2,1)}), bf16[1024,64,128]{2,1,0:T(8,128)(2,1)}, u32[]{:S(2)}, u32[]{:S(2)}) async-start(bf16[1024,64,128]{2,1,0:T(8,128)(2,1)} %copy.20), calls=%async_computation | async-start | bytes 33554432 | tf_op jit(solution)/shard_map/all_to_all | solution.py:83
  546.7 18.3 %slice-start = ((s8[16777216]{0:T(1024)(128)(4,1)}), s8[4194304]{0:T(1024)(128)(4,1)S(1)}, s32[]{:S(2)}) async-start(s8[16777216]{0:T(1024)(128)(4,1)} %bitcast.83), calls=%async_computation.2 | async-start | bytes 8388608
  546.7 18.7 %slice-start.1 = ((s8[16777216]{0:T(1024)(128)(4,1)}), s8[4194304]{0:T(1024)(128)(4,1)S(1)}, s32[]{:S(2)}) async-start(s8[16777216]{0:T(1024)(128)(4,1)} %bitcast.83), calls=%async_computation.3 | async-start | bytes 8388608
  546.7 20.3 %slice-start.2 = ((s8[16777216]{0:T(1024)(128)(4,1)}), s8[4194304]{0:T(1024)(128)(4,1)S(1)}, s32[]{:S(2)}) async-start(s8[16777216]{0:T(1024)(128)(4,1)} %bitcast.83), calls=%async_computation.4 | async-start | bytes 8388608
  546.7 21.5 %slice-start.3 = ((s8[16777216]{0:T(1024)(128)(4,1)}), s8[4194304]{0:T(1024)(128)(4,1)S(1)}, s32[]{:S(2)}) async-start(s8[16777216]{0:T(1024)(128)(4,1)} %bitcast.83), calls=%async_computation.5 | async-start | bytes 8388608
  568.2 72.4 %copy-start.1 = (bf16[1024,1024,1]{1,0,2:T(8,128)(2,1)S(1)}, bf16[1024,1024,1]{1,0,2:T(8,128)(2,1)}, u32[]{:S(2)}) copy-start(bf16[1024,1024,1]{1,0,2:T(8,128)(2,1)} %fusion.71) | copy-start | bytes 6291460
  640.7 25.6 %copy-start = (bf16[1024,1024,1]{1,0,2:T(8,128)(2,1)S(1)}, bf16[1024,1024,1]{1,0,2:T(8,128)(2,1)}, u32[]{:S(2)}) copy-start(bf16[1024,1024,1]{1,0,2:T(8,128)(2,1)} %fusion.69) | copy-start | bytes 6291460
  749.4 33.4 %copy-start.5 = (f32[32]{0:T(128)S(1)}, f32[32]{0:T(128)}, u32[]{:S(2)}) copy-start(f32[32]{0:T(128)} %dynamic_slice.7) | copy-start | bytes 388
  1204.7 8.9 copy-start.3
where the time goes:
time: 1260 us; the launch traced here: 1250 us
  blocking collectives  367 us (29%)
  waiting for transfers between devices  331 us (26%)
  other arithmetic  239 us (19%)
  matrix products  184 us (15%)
  local copies, waits for them, and re-layouts  122 us (10%)
    all_to_all x1, blocking collectives, on_device(): lax.all_to_all(analysis_input, ('comp', 'mr'), split_axis=1, concat_axis=...  367 us
    all_to_all x1, waiting for transfers between devices, on_device(): lax.all_to_all(synthesized, ('comp', 'mr'), split_axis=0, concat_axis=1,...  331 us
    another operation x2, other arithmetic  82.1 us
    convert_element_type x1, local copies, waits for them, and re-layouts, on_device(): weighted.astype(jnp.bfloat16).reshape(row_count, 2 * mode_total, 2 * planes)  42.8 us
    dot_general x1, matrix products, on_device(): jnp.einsum('mkn,mrn->rmk', coeffs, radial_basis, preferred_element_type=j...  36.1 us
    dot_general x1, matrix products, on_device(): jnp.einsum('rmk,mrn->mkn', gathered_modes, radial_basis, preferred_elemen...  35.7 us
    add x1, other arithmetic, inverse_modes(): back_real = cosine_back[..., :planes] + sine_back[..., planes:]  34.1 us
    add x1, other arithmetic, forward_modes(): imag_part = sine_term[..., :planes] + cosine_term[..., planes:]  34.1 us
  transfers between devices with their start and end apart: 1, of which 1 were waited for; matrix products, arithmetic and copies ran while one was open for 3% of the time, Pallas kernels for 0%

commit v1 on v0

v1 whole, which is shorter than its diff:
```python
import functools
import math

import jax
import jax.numpy as jnp
import numpy as np
from jax import lax
from jax.experimental import pallas as pl
from jax.experimental.pallas import tpu as pltpu
from jax.sharding import PartitionSpec as P

TIMESTEP = 0.5
ROTATION = 0.7
VMEM_LIMIT = 56 * 1024 * 1024
CHUNK_EIGHTHS = (2, 2, 2, 2)
MODE_BLOCK = 16


def spectral_tables(mode_total):
    ordinal = jnp.arange(mode_total, dtype=jnp.int32)
    product = ordinal[:, None] * ordinal[None, :] % mode_total
    angles = product.astype(jnp.float32) * (2.0 * math.pi / mode_total)
    normalizer = 1.0 / math.sqrt(mode_total)
    cosine = (jnp.cos(angles) * normalizer).astype(jnp.bfloat16)
    sine = (jnp.sin(angles) * normalizer).astype(jnp.bfloat16)
    return jnp.concatenate([cosine, sine], axis=1)


def half_turn_series():
    grid = np.cos(np.linspace(0.0, np.pi, 4001)) * 0.25
    grid = np.sort(np.concatenate([grid + 0.25, -(grid + 0.25)]))
    grid = grid[np.abs(grid) > 1e-9]
    square = grid * grid
    cheb = np.polynomial.chebyshev.Chebyshev
    sine = cheb.fit(square, np.sin(np.pi * grid) / grid, 4, domain=[0.0, 0.25])
    cosine = cheb.fit(square, np.cos(np.pi * grid), 5, domain=[0.0, 0.25])
    poly = np.polynomial.polynomial.Polynomial
    return (
        [float(v) for v in sine.convert(kind=poly).coef],
        [float(v) for v in cosine.convert(kind=poly).coef],
    )


SINE_SERIES, COSINE_SERIES = half_turn_series()


def horner(series, square):
    total = jnp.full_like(square, series[-1])
    for term in reversed(series[:-1]):
        total = total * square + term
    return total


def cos_sin_of_turns(turns):
    rest = turns - jnp.round(turns)
    square = rest * rest
    sine = rest * horner(SINE_SERIES, square)
    cosine = horner(COSINE_SERIES, square)
    twice = sine + sine
    return 1.0 - twice * sine, twice * cosine


def swap_halves(value):
    return pltpu.roll(value, value.shape[-1] // 2, value.ndim - 1)


def first_synthesis_kernel(
    block, planes, spectrum_ref, cos_ref, sin_ref, basis_ref, coeffs_ref, out_ref, stage
):
    radii = basis_ref.shape[1]
    for i in range(block):
        cosine = cos_ref[i : i + 1, :]
        sine = sin_ref[i : i + 1, :]
        real = spectrum_ref[i, 0]
        imag = spectrum_ref[i, 1]
        coeffs = jnp.concatenate(
            [real * cosine + imag * sine, imag * cosine - real * sine], axis=0
        ).astype(jnp.bfloat16)
        coeffs_ref[i] = coeffs
        stage[pl.ds(i, radii, stride=block), :] = lax.dot_general(
            basis_ref[i], coeffs, (((1,), (1,)), ((), ())), preferred_element_type=jnp.float32
        )
    out_ref[...] = stage[...].reshape(radii, block, 2 * planes).astype(jnp.bfloat16)


def synthesis_kernel(block, coeffs_ref, basis_ref, out_ref, stage):
    radii = basis_ref.shape[1]
    for i in range(block):
        stage[pl.ds(i, radii, stride=block), :] = lax.dot_general(
            basis_ref[i],
            coeffs_ref[i],
            (((1,), (1,)), ((), ())),
            preferred_element_type=jnp.float32,
        )
    out_ref[...] = stage[...].reshape(out_ref.shape).astype(jnp.bfloat16)


def physical_kernel(tile, trap_ref, weight_ref, lanes_ref, table_ref, x_ref, out_ref, work, kick):
    row = pl.program_id(0)
    width, local_modes, lanes = x_ref.shape[1], x_ref.shape[3], x_ref.shape[4]
    total = width * local_modes
    half = lanes // 2
    group = tile // local_modes
    first = lax.broadcasted_iota(jnp.int32, (tile, lanes), 1) < half
    for t in range(total // tile):
        rows = pl.ds(t * tile, tile)
        low = x_ref[0, t * group : (t + 1) * group, 0].reshape(tile, lanes).astype(jnp.float32)
        high = x_ref[1, t * group : (t + 1) * group, 0].reshape(tile, lanes).astype(jnp.float32)
        real = jnp.where(first, low, swap_halves(high)).astype(jnp.bfloat16)
        imag = jnp.where(first, swap_halves(low), high)
        work[rows, :lanes] = real
        work[rows, lanes:] = imag.astype(jnp.bfloat16)
        lower_rows = pl.ds(total + t * tile, tile)
        work[lower_rows, :lanes] = (-imag).astype(jnp.bfloat16)
        work[lower_rows, lanes:] = real
    strength = lanes_ref[0:1, :]
    cross = lanes_ref[1:2, :]
    trap = trap_ref[row]
    weight = weight_ref[row]

    for t in range(total // tile):
        rows = pl.ds(t * tile, tile)
        psi = jnp.dot(table_ref[rows, :], work[...], preferred_element_type=jnp.float32)
        real, imag = psi[:, :lanes], psi[:, lanes:]
        density = real * real + imag * imag
        turns = strength * density + cross * swap_halves(density) + trap
        cosine, sine = cos_sin_of_turns(turns)
        kick_real = (real * cosine + imag * sine).astype(jnp.bfloat16)
        kick_imag = imag * cosine - real * sine
        kick[rows, :lanes] = kick_real
        kick[rows, lanes:] = kick_imag.astype(jnp.bfloat16)
        lower_rows = pl.ds(total + t * tile, tile)
        kick[lower_rows, :lanes] = kick_imag.astype(jnp.bfloat16)
        kick[lower_rows, lanes:] = (-(real * cosine + imag * sine)).astype(jnp.bfloat16)

    for t in range(total // tile):
        rows = pl.ds(t * tile, tile)
        back = jnp.dot(table_ref[rows, :], kick[...], preferred_element_type=jnp.float32) * weight
        real, imag = back[:, :lanes], back[:, lanes:]
        low = jnp.where(first, real, swap_halves(imag)).astype(jnp.bfloat16)
        high = jnp.where(first, swap_halves(real), imag).astype(jnp.bfloat16)
        out_ref[0, t * group : (t + 1) * group, 0] = low.reshape(group, local_modes, lanes)
        out_ref[1, t * group : (t + 1) * group, 0] = high.reshape(group, local_modes, lanes)


def analysis_kernel(block, first, last, *refs):
    if first:
        fields_ref, basis_ref, kept_ref, out_ref, stage = refs
        held_ref = None
    else:
        fields_ref, basis_ref, kept_ref, held_ref, out_ref, stage = refs
    radii = basis_ref.shape[1]
    stage[...] = fields_ref[...].astype(jnp.float32).reshape(stage.shape)
    for i in range(block):
        field = stage[pl.ds(i, radii, stride=block), :].astype(jnp.bfloat16)
        part = lax.dot_general(
            field, basis_ref[i], (((0,), (0,)), ((), ())), preferred_element_type=jnp.float32
        )
        if not first:
            part = part + held_ref[i]
        if last:
            part = part * kept_ref[i : i + 1, :]
        out_ref[i] = part


def params():
    return pltpu.CompilerParams(
        vmem_limit_bytes=VMEM_LIMIT, dimension_semantics=("arbitrary",)
    )


def row_parts(row_count):
    parts, done = [], 0
    for share in np.cumsum(CHUNK_EIGHTHS):
        upto = row_count * int(share) // int(np.sum(CHUNK_EIGHTHS))
        if upto > done:
            parts.append((done, upto - done))
            done = upto
    return parts


def on_device(spectrum, radial_basis, cutoff, couplings, trap_potential, weights):
    local_modes, planes, degrees = spectrum.shape[1], spectrum.shape[3], spectrum.shape[4]
    radius_count = radial_basis.shape[1]
    axes = ("comp", "mr")
    components, mode_width = lax.axis_size("comp"), lax.axis_size("mr")
    device_count = components * mode_width
    mode_total = local_modes * mode_width
    lanes = 2 * planes
    block = math.gcd(local_modes, MODE_BLOCK)
    steps = local_modes // block

    mode_ids = lax.axis_index("mr") * local_modes + jnp.arange(local_modes, dtype=jnp.int32)
    signed = jnp.where(mode_ids < mode_total // 2, mode_ids, mode_ids - mode_total).astype(
        jnp.float32
    )
    degree_ids = jnp.arange(degrees, dtype=jnp.int32)
    energy = (
        2.0 * degree_ids.astype(jnp.float32)[None, :]
        + (jnp.abs(signed) + 1.0 - ROTATION * signed)[:, None]
    )
    kinetic_phase = TIMESTEP * energy
    kept_mask = (degree_ids[None, :] < cutoff[:, None]).astype(jnp.float32)
    kinetic_cos = jnp.cos(kinetic_phase) * kept_mask
    kinetic_sin = jnp.sin(kinetic_phase) * kept_mask
    table = spectral_tables(mode_total)
    to_turns = TIMESTEP / (2.0 * math.pi)
    lane_strength = jnp.repeat(couplings.T * to_turns, planes, axis=1)

    me = lax.axis_index(axes)
    parts = row_parts(radius_count // device_count)

    def basis_spec(rows, start):
        radii = rows * device_count
        assert start * device_count % radii == 0
        place = start * device_count // radii
        return pl.BlockSpec((block, radii, degrees), lambda i: (i, place, 0))

    def first_synthesis(start, rows):
        radii = rows * device_count
        return pl.pallas_call(
            functools.partial(first_synthesis_kernel, block, planes),
            grid=(steps,),
            out_shape=(
                jax.ShapeDtypeStruct((local_modes, lanes, degrees), jnp.bfloat16),
                jax.ShapeDtypeStruct((radii, local_modes, lanes), jnp.bfloat16),
            ),
            in_specs=[
                pl.BlockSpec((None, block, 2, planes, degrees), lambda i: (0, i, 0, 0, 0)),
                pl.BlockSpec((block, degrees), lambda i: (i, 0)),
                pl.BlockSpec((block, degrees), lambda i: (i, 0)),
                basis_spec(rows, start),
            ],
            out_specs=(
                pl.BlockSpec((block, lanes, degrees), lambda i: (i, 0, 0)),
                pl.BlockSpec((radii, block, lanes), lambda i: (0, i, 0)),
            ),
            scratch_shapes=[pltpu.VMEM((radii * block, lanes), jnp.float32)],
            compiler_params=params(),
            cost_estimate=pl.CostEstimate(
                flops=2 * local_modes * radii * degrees * lanes,
                bytes_accessed=6 * local_modes * lanes * degrees
                + 2 * local_modes * radii * (degrees + lanes),
                transcendentals=0,
            ),
            name="first_synthesis",
        )(spectrum, kinetic_cos, kinetic_sin, radial_basis)

    def synthesis(coeffs, start, rows):
        radii = rows * device_count
        return pl.pallas_call(
            functools.partial(synthesis_kernel, block),
            grid=(steps,),
            out_shape=jax.ShapeDtypeStruct((radii, local_modes, lanes), jnp.bfloat16),
            in_specs=[
                pl.BlockSpec((block, lanes, degrees), lambda i: (i, 0, 0)),
                basis_spec(rows, start),
            ],
            out_specs=pl.BlockSpec((radii, block, lanes), lambda i: (0, i, 0)),
            scratch_shapes=[pltpu.VMEM((radii * block, lanes), jnp.float32)],
            compiler_params=params(),
            cost_estimate=pl.CostEstimate(
                flops=2 * local_modes * radii * degrees * lanes,
                bytes_accessed=2 * local_modes * (lanes * degrees + radii * (degrees + lanes)),
                transcendentals=0,
            ),
            name="synthesis",
        )(coeffs, radial_basis)

    def physical(radial, start, rows):
        first_radius = start * device_count + me * rows
        trap = lax.dynamic_slice_in_dim(trap_potential, first_radius, rows) * to_turns
        weight = lax.dynamic_slice_in_dim(weights, first_radius, rows)
        shape = (components, mode_width, rows, local_modes, lanes)
        spec = pl.BlockSpec(
            (components, mode_width, 1, local_modes, lanes), lambda i: (0, 0, i, 0, 0)
        )
        tile = max(min(mode_total, 256), local_modes)
        return pl.pallas_call(
            functools.partial(physical_kernel, tile),
            grid=(rows,),
            out_shape=jax.ShapeDtypeStruct(shape, jnp.bfloat16),
            in_specs=[
                pl.BlockSpec(memory_space=pltpu.SMEM),
                pl.BlockSpec(memory_space=pltpu.SMEM),
                pl.BlockSpec((2, lanes), lambda i: (0, 0)),
                pl.BlockSpec((mode_total, 2 * mode_total), lambda i: (0, 0)),
                spec,
            ],
            out_specs=spec,
            scratch_shapes=[
                pltpu.VMEM((2 * mode_total, 2 * lanes), jnp.bfloat16),
                pltpu.VMEM((2 * mode_total, 2 * lanes), jnp.bfloat16),
            ],
            compiler_params=params(),
            cost_estimate=pl.CostEstimate(
                flops=16 * rows * mode_total * mode_total * lanes,
                bytes_accessed=8 * rows * mode_total * lanes + 4 * mode_total * mode_total,
                transcendentals=0,
            ),
            name="physical",
        )(trap, weight, lane_strength, table, radial.reshape(shape)).reshape(radial.shape)

    def analysis(fields, held, start, rows, last):
        radii = rows * device_count
        out_spec = pl.BlockSpec((block, lanes, degrees), lambda i: (i, 0, 0))
        operands = [fields, radial_basis, kept_mask]
        in_specs = [
            pl.BlockSpec((radii, block, lanes), lambda i: (0, i, 0)),
            basis_spec(rows, start),
            pl.BlockSpec((block, degrees), lambda i: (i, 0)),
        ]
        if held is not None:
            operands.append(held)
            in_specs.append(out_spec)
        return pl.pallas_call(
            functools.partial(analysis_kernel, block, held is None, last),
            grid=(steps,),
            out_shape=jax.ShapeDtypeStruct((local_modes, lanes, degrees), jnp.float32),
            in_specs=in_specs,
            out_specs=out_spec,
            scratch_shapes=[pltpu.VMEM((radii * block, lanes), jnp.float32)],
            input_output_aliases={} if held is None else {3: 0},
            compiler_params=params(),
            cost_estimate=pl.CostEstimate(
                flops=2 * local_modes * radii * degrees * lanes,
                bytes_accessed=2 * local_modes * radii * (degrees + lanes)
                + 8 * local_modes * lanes * degrees,
                transcendentals=0,
            ),
            name="analysis",
        )(*operands)

    def exchange(value):
        return lax.all_to_all(value, axes, split_axis=0, concat_axis=0, tiled=True)

    coeffs, synthesized = first_synthesis(*parts[0])
    arrived = []
    for k, part in enumerate(parts):
        if k > 0:
            synthesized = synthesis(coeffs, *part)
        arrived.append(exchange(synthesized))
    evolved = None
    returned = [exchange(physical(arrived[k], *part)) for k, part in enumerate(parts)]
    for k, part in enumerate(parts):
        evolved = analysis(returned[k], evolved, *part, k == len(parts) - 1)
    return evolved.reshape(1, local_modes, 2, planes, degrees)


def solution(mesh):
    in_specs = (P("comp", "mr", None, None, None), P("mr", None, None), P("mr"), P(), P(), P())
    out_specs = P("comp", "mr", None, None, None)
    return jax.shard_map(
        on_device, mesh=mesh, in_specs=in_specs, out_specs=out_specs, check_vma=False
    )
```

time: 1260 us -> 828 us (0.66)
  blocking collectives: 367 us -> 0 us
  Pallas kernels: 0 us -> 245 us
  other arithmetic: 239 us -> 22.9 us
  waiting for transfers between devices: 331 us -> 526 us
  matrix products: 184 us -> 0 us
  local copies, waits for them, and re-layouts: 122 us -> 0.78 us
  starting transfers between devices: 7.65 us -> 33 us
    all_to_all x1 -> x0, blocking collectives: 367 us -> none  [on_device(): lax.all_to_all(analysis_input, ('comp', 'mr'), split_axis=1, concat_axis=...]
    pallas_call x0 -> x12, Pallas kernels: none -> 245 us  [the longest x4 119 us: physical(): pl.pallas_call(functools.partial(physical_kernel, tile), grid=(rows,), ou...]
    all_to_all x1 -> x8, waiting for transfers between devices: 331 us -> 526 us  [exchange(): return lax.all_to_all(value, axes, split_axis=0, concat_axis=0, tiled=True)]
    dot_general x6 -> x0, matrix products: 184 us -> none  [the longest x1 36.1 us: on_device(): jnp.einsum('mkn,mrn->rmk', coeffs, radial_basis, preferred_element_type=j...]
    add x3 -> x0, other arithmetic: 86.4 us -> none  [the longest x1 34.1 us: inverse_modes(): back_real = cosine_back[..., :planes] + sine_back[..., planes:]]
    another operation x2 -> x0, other arithmetic: 82.1 us -> none
    convert_element_type x2 -> x0, local copies, waits for them, and re-layouts: 65.5 us -> none  [the longest x1 42.8 us: on_device(): weighted.astype(jnp.bfloat16).reshape(row_count, 2 * mode_total, 2 * planes)]
    concatenate x1 -> x0, local copies, waits for them, and re-layouts: 33.4 us -> none  [inverse_modes(): return jnp.concatenate([back_real, back_imag], -1)]
  transfers between devices with their start and end apart: 1 -> 8, of which waited for: 1 -> 8; matrix products, arithmetic and copies ran while one was open for 3% -> 3% of each run, Pallas kernels for 0% -> 25%
where the time goes in v1:
time: 828 us
  waiting for transfers between devices  526 us (64%)
  Pallas kernels  245 us (30%)
  starting transfers between devices  33 us (4%)
  other arithmetic  22.9 us (3%)
    all_to_all x8, waiting for transfers between devices, exchange(): return lax.all_to_all(value, axes, split_axis=0, concat_axis=0, tiled=True)  526 us
    pallas_call x4, Pallas kernels, physical(): pl.pallas_call(functools.partial(physical_kernel, tile), grid=(rows,), ou...  119 us
    pallas_call x4, Pallas kernels, analysis(): pl.pallas_call(functools.partial(analysis_kernel, block, held is None, la...  72.6 us
    pallas_call x3, Pallas kernels, synthesis(): pl.pallas_call(functools.partial(synthesis_kernel, block), grid=(steps,),...  37.1 us
    all_to_all x8, starting transfers between devices, exchange(): return lax.all_to_all(value, axes, split_axis=0, concat_axis=0, tiled=True)  33 us
    convert_element_type x1, other arithmetic, spectral_tables(): sine = (jnp.sin(angles) * normalizer).astype(jnp.bfloat16)  17.1 us
  transfers between devices with their start and end apart: 8, of which 8 were waited for; matrix products, arithmetic and copies ran while one was open for 3% of the time, Pallas kernels for 25%

profile of v1, /device:TPU:0, one launch (start us, length us, event | category | flops | bytes accessed | tf_op | source)
XLA Modules:
  0.0 827.8 jit_solution(6040245934112513681)
XLA Ops:
  1.9 16.2 %first_synthesis.1 = (bf16[64,128,512]{2,1,0:T(8,128)(2,1)}, bf16[256,64,128]{2,1,0:T(8,128)(2,1)}) custom-call(f32[1,64,2,64,512]{4,3,2,1,0:T(8,128)} %spectrum_ref.1, f32[64,512]{1,0:T(8,128)} %get-tuple-element.18.cos_ref, f32[64,512]{1,0:T(8,128)} %get-tuple-element.17.sin_ref, bf16[64,1024,512]{2,1,0:T(8,128)(2,1)} %refs_1_.7), custom_call_target="tpu_custom_call" | custom-call | flops 2147483648 | bytes 46137344 | tf_op jit(solution)/shard_map/first_synthesis/pallas_call | solution.py:221
  18.2 7.4 all-to-all-start.6
  25.6 12.4 %synthesis.5 = bf16[256,64,128]{2,1,0:T(8,128)(2,1)} custom-call(bf16[64,128,512]{2,1,0:T(8,128)(2,1)} %get-tuple-element.7.coeffs_ref, bf16[64,1024,512]{2,1,0:T(8,128)(2,1)} %refs_1_.7), custom_call_target="tpu_custom_call" | custom-call | flops 2147483648 | bytes 29360128 | tf_op jit(solution)/shard_map/synthesis/pallas_call | solution.py:251
  38.0 82.3 %all-to-all-done.6 = bf16[256,64,128]{2,1,0:T(8,128)(2,1)} async-done(((bf16[256,64,128]{2,1,0:T(8,128)(2,1)}), bf16[256,64,128]{2,1,0:T(8,128)(2,1)}, u32[]{:S(2)}, u32[]{:S(2)}) %all-to-all-start.6) | async-done | bytes 4194336 | tf_op jit(solution)/shard_map/all_to_all | solution.py:335
  123.8 12.4 %synthesis.3 = bf16[256,64,128]{2,1,0:T(8,128)(2,1)} custom-call(bf16[64,128,512]{2,1,0:T(8,128)(2,1)} %get-tuple-element.7.coeffs_ref, bf16[64,1024,512]{2,1,0:T(8,128)(2,1)} %refs_1_.7), custom_call_target="tpu_custom_call" | custom-call | flops 2147483648 | bytes 29360128 | tf_op jit(solution)/shard_map/synthesis/pallas_call | solution.py:251
  136.2 82.3 %all-to-all-done.4 = bf16[256,64,128]{2,1,0:T(8,128)(2,1)} async-done(((bf16[256,64,128]{2,1,0:T(8,128)(2,1)}), bf16[256,64,128]{2,1,0:T(8,128)(2,1)}, u32[]{:S(2)}, u32[]{:S(2)}) %all-to-all-start.4) | async-done | bytes 4194336 | tf_op jit(solution)/shard_map/all_to_all | solution.py:335
  222.2 12.4 %synthesis.4 = bf16[256,64,128]{2,1,0:T(8,128)(2,1)} custom-call(bf16[64,128,512]{2,1,0:T(8,128)(2,1)} %get-tuple-element.7.coeffs_ref, bf16[64,1024,512]{2,1,0:T(8,128)(2,1)} %refs_1_.7), custom_call_target="tpu_custom_call" | custom-call | flops 2147483648 | bytes 29360128 | tf_op jit(solution)/shard_map/synthesis/pallas_call | solution.py:251
  234.5 82.4 %all-to-all-done = bf16[256,64,128]{2,1,0:T(8,128)(2,1)} async-done(((bf16[256,64,128]{2,1,0:T(8,128)(2,1)}), bf16[256,64,128]{2,1,0:T(8,128)(2,1)}, u32[]{:S(2)}, u32[]{:S(2)}) %all-to-all-start) | async-done | bytes 4194336 | tf_op jit(solution)/shard_map/all_to_all | solution.py:335
  321.9 17.1 %multiply_convert_fusion = (bf16[1024,1024]{1,0:T(8,128)(2,1)S(1)}, bf16[1024,1024]{1,0:T(8,128)(2,1)S(1)}) fusion(), kind=kLoop, calls=%fused_computation.7 | loop fusion | flops 18874368 | bytes 4194304 | tf_op jit(solution)/shard_map/convert_element_type | solution.py:25
  341.5 29.8 %physical.7 = bf16[2,16,8,64,128]{4,3,2,1,0:T(8,128)(2,1)} custom-call(f32[8]{0:T(128)} %get-tuple-element.13.trap_ref, f32[8]{0:T(128)} %get-tuple-element.22.weight_ref, f32[2,128]{1,0:T(2,128)} %reshape.49.lanes_ref, bf16[1024,2048]{1,0:T(8,128)(2,1)} %pad_maximum_fusion.table_ref, bf16[2,16,8,64,128]{4,3,2,1,0:T(8,128)(2,1)} %bitcast.7.x_ref), custom_call_target="tpu_custom_call" | custom-call | flops 17179869184 | bytes 12582912 | tf_op jit(solution)/shard_map/physical/pallas_call | solution.py:279
  371.3 43.8 %all-to-all-done.2 = bf16[256,64,128]{2,1,0:T(8,128)(2,1)} async-done(((bf16[256,64,128]{2,1,0:T(8,128)(2,1)}), bf16[256,64,128]{2,1,0:T(8,128)(2,1)}, u32[]{:S(2)}, u32[]{:S(2)}) %all-to-all-start.2) | async-done | bytes 4194336 | tf_op jit(solution)/shard_map/all_to_all | solution.py:335
  415.2 3.8 all-to-all-start.7
  418.9 29.8 %physical.6 = bf16[2,16,8,64,128]{4,3,2,1,0:T(8,128)(2,1)} custom-call(f32[8]{0:T(128)} %get-tuple-element.16.trap_ref, f32[8]{0:T(128)} %get-tuple-element.19.weight_ref, f32[2,128]{1,0:T(2,128)} %reshape.49.lanes_ref, bf16[1024,2048]{1,0:T(8,128)(2,1)} %pad_maximum_fusion.table_ref, bf16[2,16,8,64,128]{4,3,2,1,0:T(8,128)(2,1)} %bitcast.5.x_ref), custom_call_target="tpu_custom_call" | custom-call | flops 17179869184 | bytes 12582912 | tf_op jit(solution)/shard_map/physical/pallas_call | solution.py:279
  448.7 64.7 %all-to-all-done.7.refs_0_ = bf16[256,64,128]{2,1,0:T(8,128)(2,1)} async-done(((bf16[256,64,128]{2,1,0:T(8,128)(2,1)}), bf16[256,64,128]{2,1,0:T(8,128)(2,1)}, u32[]{:S(2)}, u32[]{:S(2)}) %all-to-all-start.7) | async-done | bytes 4194336 | tf_op jit(solution)/shard_map/all_to_all | solution.py:335
  517.0 29.8 %physical.5 = bf16[2,16,8,64,128]{4,3,2,1,0:T(8,128)(2,1)} custom-call(f32[8]{0:T(128)} %get-tuple-element.14.trap_ref, f32[8]{0:T(128)} %get-tuple-element.21.weight_ref, f32[2,128]{1,0:T(2,128)} %reshape.49.lanes_ref, bf16[1024,2048]{1,0:T(8,128)(2,1)} %pad_maximum_fusion.table_ref, bf16[2,16,8,64,128]{4,3,2,1,0:T(8,128)(2,1)} %bitcast.3.x_ref), custom_call_target="tpu_custom_call" | custom-call | flops 17179869184 | bytes 12582912 | tf_op jit(solution)/shard_map/physical/pallas_call | solution.py:279
  546.9 64.9 %all-to-all-done.5.refs_0_ = bf16[256,64,128]{2,1,0:T(8,128)(2,1)} async-done(((bf16[256,64,128]{2,1,0:T(8,128)(2,1)}), bf16[256,64,128]{2,1,0:T(8,128)(2,1)}, u32[]{:S(2)}, u32[]{:S(2)}) %all-to-all-start.5) | async-done | bytes 4194336 | tf_op jit(solution)/shard_map/all_to_all | solution.py:335
  615.4 29.8 %physical.4 = bf16[2,16,8,64,128]{4,3,2,1,0:T(8,128)(2,1)} custom-call(f32[8]{0:T(128)} %get-tuple-element.15.trap_ref, f32[8]{0:T(128)} %get-tuple-element.20.weight_ref, f32[2,128]{1,0:T(2,128)} %reshape.49.lanes_ref, bf16[1024,2048]{1,0:T(8,128)(2,1)} %pad_maximum_fusion.table_ref, bf16[2,16,8,64,128]{4,3,2,1,0:T(8,128)(2,1)} %bitcast.1.x_ref), custom_call_target="tpu_custom_call" | custom-call | flops 17179869184 | bytes 12582912 | tf_op jit(solution)/shard_map/physical/pallas_call | solution.py:279
  645.1 64.9 %all-to-all-done.3.refs_0_ = bf16[256,64,128]{2,1,0:T(8,128)(2,1)} async-done(((bf16[256,64,128]{2,1,0:T(8,128)(2,1)}), bf16[256,64,128]{2,1,0:T(8,128)(2,1)}, u32[]{:S(2)}, u32[]{:S(2)}) %all-to-all-start.3) | async-done | bytes 4194336 | tf_op jit(solution)/shard_map/all_to_all | solution.py:335
  710.1 3.9 all-to-all-start.1
  714.8 15.0 %analysis.4.refs_3_ = f32[64,128,512]{2,1,0:T(8,128)} custom-call(bf16[256,64,128]{2,1,0:T(8,128)(2,1)} %all-to-all-done.7.refs_0_, bf16[64,1024,512]{2,1,0:T(8,128)(2,1)} %refs_1_.7, f32[64,512]{1,0:T(8,128)} %fusion.6.refs_2_), custom_call_target="tpu_custom_call" | custom-call | flops 2147483648 | bytes 54525952 | tf_op jit(solution)/shard_map/analysis/pallas_call | solution.py:316
  729.8 19.2 %analysis.5.refs_3_ = f32[64,128,512]{2,1,0:T(8,128)} custom-call(bf16[256,64,128]{2,1,0:T(8,128)(2,1)} %all-to-all-done.5.refs_0_, bf16[64,1024,512]{2,1,0:T(8,128)(2,1)} %refs_1_.7, f32[64,512]{1,0:T(8,128)} %fusion.6.refs_2_, f32[64,128,512]{2,1,0:T(8,128)} %analysis.4.refs_3_), custom_call_target="tpu_custom_call", output_to_operand_aliasing={{}: (3, {})} | custom-call | flops 2147483648 | bytes 54525952 | tf_op jit(solution)/shard_map/analysis/pallas_call | solution.py:316
  748.9 19.2 %analysis.6.refs_3_ = f32[64,128,512]{2,1,0:T(8,128)} custom-call(bf16[256,64,128]{2,1,0:T(8,128)(2,1)} %all-to-all-done.3.refs_0_, bf16[64,1024,512]{2,1,0:T(8,128)(2,1)} %refs_1_.7, f32[64,512]{1,0:T(8,128)} %fusion.6.refs_2_, f32[64,128,512]{2,1,0:T(8,128)} %analysis.5.refs_3_), custom_call_target="tpu_custom_call", output_to_operand_aliasing={{}: (3, {})} | custom-call | flops 2147483648 | bytes 54525952 | tf_op jit(solution)/shard_map/analysis/pallas_call | solution.py:316
  768.1 40.4 %all-to-all-done.1.refs_0_ = bf16[256,64,128]{2,1,0:T(8,128)(2,1)} async-done(((bf16[256,64,128]{2,1,0:T(8,128)(2,1)}), bf16[256,64,128]{2,1,0:T(8,128)(2,1)}, u32[]{:S(2)}, u32[]{:S(2)}) %all-to-all-start.1) | async-done | bytes 4194336 | tf_op jit(solution)/shard_map/all_to_all | solution.py:335
  808.5 19.3 %analysis.7 = f32[64,128,512]{2,1,0:T(8,128)} custom-call(bf16[256,64,128]{2,1,0:T(8,128)(2,1)} %all-to-all-done.1.refs_0_, bf16[64,1024,512]{2,1,0:T(8,128)(2,1)} %refs_1_.7, f32[64,512]{1,0:T(8,128)} %fusion.6.refs_2_, f32[64,128,512]{2,1,0:T(8,128)} %analysis.6.refs_3_), custom_call_target="tpu_custom_call", output_to_operand_aliasing={{}: (3, {})} | custom-call | flops 2147483648 | bytes 54525952 | tf_op jit(solution)/shard_map/analysis/pallas_call | solution.py:316
  (23 shorter events, 24.5 us)
Async XLA Ops:
  18.2 102.1 %all-to-all-start.6 = ((bf16[256,64,128]{2,1,0:T(8,128)(2,1)}), bf16[256,64,128]{2,1,0:T(8,128)(2,1)}, u32[]{:S(2)}, u32[]{:S(2)}) async-start(bf16[256,64,128]{2,1,0:T(8,128)(2,1)} %get-tuple-element.8), calls=%async_computation.6 | async-start | bytes 8388608 | tf_op jit(solution)/shard_map/all_to_all | solution.py:335
  120.3 98.3 %all-to-all-start.4 = ((bf16[256,64,128]{2,1,0:T(8,128)(2,1)}), bf16[256,64,128]{2,1,0:T(8,128)(2,1)}, u32[]{:S(2)}, u32[]{:S(2)}) async-start(bf16[256,64,128]{2,1,0:T(8,128)(2,1)} %synthesis.5), calls=%async_computation.4 | async-start | bytes 8388608 | tf_op jit(solution)/shard_map/all_to_all | solution.py:335
  218.6 98.3 %all-to-all-start = ((bf16[256,64,128]{2,1,0:T(8,128)(2,1)}), bf16[256,64,128]{2,1,0:T(8,128)(2,1)}, u32[]{:S(2)}, u32[]{:S(2)}) async-start(bf16[256,64,128]{2,1,0:T(8,128)(2,1)} %synthesis.3), calls=%async_computation | async-start | bytes 8388608 | tf_op jit(solution)/shard_map/all_to_all | solution.py:335
  234.5 86.0 %copy-start.3 = (f32[2,2]{1,0:T(2,128)S(1)}, f32[2,2]{1,0:T(2,128)}, u32[]{:S(2)}) copy-start(f32[2,2]{1,0:T(2,128)} %param.9) | copy-start | bytes 52
  234.5 86.7 %copy-start.1 = (f32[1024]{0:T(1024)S(1)}, f32[1024]{0:T(1024)}, u32[]{:S(2)}) copy-start(f32[1024]{0:T(1024)} %param.10) | copy-start | bytes 12292
  234.5 86.7 %copy-start.2 = (f32[1024]{0:T(1024)S(1)}, f32[1024]{0:T(1024)}, u32[]{:S(2)}) copy-start(f32[1024]{0:T(1024)} %param.11) | copy-start | bytes 12292
  316.9 98.3 %all-to-all-start.2 = ((bf16[256,64,128]{2,1,0:T(8,128)(2,1)}), bf16[256,64,128]{2,1,0:T(8,128)(2,1)}, u32[]{:S(2)}, u32[]{:S(2)}) async-start(bf16[256,64,128]{2,1,0:T(8,128)(2,1)} %synthesis.4), calls=%async_computation.2 | async-start | bytes 8388608 | tf_op jit(solution)/shard_map/all_to_all | solution.py:335
  415.2 98.3 %all-to-all-start.7 = ((bf16[256,64,128]{2,1,0:T(8,128)(2,1)}), bf16[256,64,128]{2,1,0:T(8,128)(2,1)}, u32[]{:S(2)}, u32[]{:S(2)}) async-start(bf16[256,64,128]{2,1,0:T(8,128)(2,1)} %bitcast.13), calls=%async_computation.7 | async-start | bytes 8388608 | tf_op jit(solution)/shard_map/all_to_all | solution.py:335
  513.5 98.3 %all-to-all-start.5 = ((bf16[256,64,128]{2,1,0:T(8,128)(2,1)}), bf16[256,64,128]{2,1,0:T(8,128)(2,1)}, u32[]{:S(2)}, u32[]{:S(2)}) async-start(bf16[256,64,128]{2,1,0:T(8,128)(2,1)} %bitcast.14), calls=%async_computation.5 | async-start | bytes 8388608 | tf_op jit(solution)/shard_map/all_to_all | solution.py:335
  611.8 98.3 %all-to-all-start.3 = ((bf16[256,64,128]{2,1,0:T(8,128)(2,1)}), bf16[256,64,128]{2,1,0:T(8,128)(2,1)}, u32[]{:S(2)}, u32[]{:S(2)}) async-start(bf16[256,64,128]{2,1,0:T(8,128)(2,1)} %bitcast.12), calls=%async_computation.3 | async-start | bytes 8388608 | tf_op jit(solution)/shard_map/all_to_all | solution.py:335
  710.1 3.9 copy-start
  710.1 98.4 %all-to-all-start.1 = ((bf16[256,64,128]{2,1,0:T(8,128)(2,1)}), bf16[256,64,128]{2,1,0:T(8,128)(2,1)}, u32[]{:S(2)}, u32[]{:S(2)}) async-start(bf16[256,64,128]{2,1,0:T(8,128)(2,1)} %bitcast.11), calls=%async_computation.1 | async-start | bytes 8388608 | tf_op jit(solution)/shard_map/all_to_all | solution.py:335

commit v2 on v1

v2 whole, which is shorter than its diff:
```python
import functools
import math

import jax
import jax.numpy as jnp
import numpy as np
from jax import lax
from jax.experimental import pallas as pl
from jax.experimental.pallas import tpu as pltpu
from jax.sharding import PartitionSpec as P

TIMESTEP = 0.5
ROTATION = 0.7
VMEM_LIMIT = 60 * 1024 * 1024
ROW_SHARES = (6, 26)
MODE_BLOCK = 16
MODE_PART = 16


def spectral_tables(mode_total):
    quarter = mode_total // 4
    ordinal = jnp.arange(quarter, dtype=jnp.int32)
    angle_ids = 4 * ordinal[None, :] + jnp.arange(4, dtype=jnp.int32)[:, None]
    product = angle_ids[:, :, None] * ordinal[None, None, :] % mode_total
    angles = product.astype(jnp.float32) * (2.0 * math.pi / mode_total)
    normalizer = 1.0 / math.sqrt(mode_total)
    cosine = (jnp.cos(angles) * normalizer).astype(jnp.bfloat16)
    sine = (jnp.sin(angles) * normalizer).astype(jnp.bfloat16)
    out = jnp.concatenate([cosine, sine], axis=2)
    back = jnp.concatenate([cosine.swapaxes(1, 2), sine.swapaxes(1, 2)], axis=2)
    return out, back


def kinetic_tables(mode_total, degrees):
    mode_ids = np.arange(mode_total)
    signed = np.where(mode_ids < mode_total // 2, mode_ids, mode_ids - mode_total)
    of_mode = TIMESTEP * (np.abs(signed) + 1.0 - ROTATION * signed)
    of_degree = TIMESTEP * 2.0 * np.arange(degrees)
    return tuple(
        jnp.asarray(np.stack([np.cos(angles), np.sin(angles)]), jnp.float32)
        for angles in (of_mode, of_degree)
    )


def half_turn_series():
    grid = np.cos(np.linspace(0.0, np.pi, 4001)) * 0.25
    grid = np.sort(np.concatenate([grid + 0.25, -(grid + 0.25)]))
    grid = grid[np.abs(grid) > 1e-9]
    square = grid * grid
    cheb = np.polynomial.chebyshev.Chebyshev
    sine = cheb.fit(square, np.sin(np.pi * grid) / grid, 4, domain=[0.0, 0.25])
    cosine = cheb.fit(square, np.cos(np.pi * grid), 5, domain=[0.0, 0.25])
    poly = np.polynomial.polynomial.Polynomial
    return (
        [float(v) for v in sine.convert(kind=poly).coef],
        [float(v) for v in cosine.convert(kind=poly).coef],
    )


SINE_SERIES, COSINE_SERIES = half_turn_series()


def horner(series, square):
    total = jnp.full_like(square, series[-1])
    for term in reversed(series[:-1]):
        total = total * square + term
    return total


def cos_sin_of_turns(turns):
    rest = turns - jnp.round(turns)
    square = rest * rest
    sine = rest * horner(SINE_SERIES, square)
    cosine = horner(COSINE_SERIES, square)
    twice = sine + sine
    return 1.0 - twice * sine, twice * cosine


def swap_halves(value):
    return pltpu.roll(value, value.shape[-1] // 2, value.ndim - 1)


def synthesis_kernel(
    planes, first_ref, cutoff_ref, mode_ref, degree_ref, spectrum_ref, basis_ref, out_ref, stage
):
    part, radii, degrees = basis_ref.shape
    block = out_ref.shape[1]
    inner = pl.program_id(1)
    local = pl.program_id(0) * block + inner * part
    degree_ids = lax.broadcasted_iota(jnp.int32, (1, degrees), 1)
    for i in range(part):
        mode = first_ref[0] + local + i
        mode_cos, mode_sin = mode_ref[0, mode], mode_ref[1, mode]
        degree_cos, degree_sin = degree_ref[0:1, :], degree_ref[1:2, :]
        kept = degree_ids < cutoff_ref[local + i]
        cosine = jnp.where(kept, degree_cos * mode_cos - degree_sin * mode_sin, 0.0)
        sine = jnp.where(kept, degree_sin * mode_cos + degree_cos * mode_sin, 0.0)
        real = spectrum_ref[i, 0]
        imag = spectrum_ref[i, 1]
        coeffs = jnp.concatenate(
            [real * cosine + imag * sine, imag * cosine - real * sine], axis=0
        ).astype(jnp.bfloat16)
        stage[pl.ds(inner * part + i, radii, stride=block), :] = lax.dot_general(
            basis_ref[i], coeffs, (((1,), (1,)), ((), ())), preferred_element_type=jnp.float32
        )

    @pl.when(inner == pl.num_programs(1) - 1)
    def _():
        out_ref[...] = stage[...].reshape(out_ref.shape).astype(jnp.bfloat16)


def complex_sum(left, right):
    return left[0] + right[0], left[1] + right[1]


def complex_difference(left, right):
    return left[0] - right[0], left[1] - right[1]


def quarter_turn(value):
    return -value[1], value[0]


def physical_kernel(trap_ref, weight_ref, lanes_ref, table_ref, back_ref, x_ref, *refs):
    *out_refs, work, kick = refs
    row = pl.program_id(0)
    width, local_modes, lanes = x_ref.shape[1], x_ref.shape[3], x_ref.shape[4]
    quarter = width * local_modes // 4
    blocks = width // 4
    first = lax.broadcasted_iota(jnp.int32, (quarter, lanes), 1) < lanes // 2

    parts = []
    for j in range(4):
        own = slice(j * blocks, (j + 1) * blocks)
        low = x_ref[0, own, 0].reshape(quarter, lanes).astype(jnp.float32)
        high = x_ref[1, own, 0].reshape(quarter, lanes).astype(jnp.float32)
        parts.append(
            (
                jnp.where(first, low, swap_halves(high)),
                jnp.where(first, swap_halves(low), high),
            )
        )
    even, odd = complex_sum(parts[0], parts[2]), complex_sum(parts[1], parts[3])
    skew = quarter_turn(complex_difference(parts[1], parts[3]))
    rest = complex_difference(parts[0], parts[2])
    folded = (
        complex_sum(even, odd),
        complex_sum(rest, skew),
        complex_difference(even, odd),
        complex_difference(rest, skew),
    )
    for q, (real, imag) in enumerate(folded):
        real = real.astype(jnp.bfloat16)
        work[q, :quarter, :lanes] = real
        work[q, :quarter, lanes:] = imag.astype(jnp.bfloat16)
        work[q, quarter:, :lanes] = (-imag).astype(jnp.bfloat16)
        work[q, quarter:, lanes:] = real

    strength = lanes_ref[0:1, :]
    cross = lanes_ref[1:2, :]
    trap = trap_ref[row]
    weight = weight_ref[row]
    for q in range(4):
        psi = jnp.dot(table_ref[q], work[q], preferred_element_type=jnp.float32)
        real, imag = psi[:, :lanes], psi[:, lanes:]
        density = real * real + imag * imag
        turns = strength * density + cross * swap_halves(density) + trap
        cosine, sine = cos_sin_of_turns(turns)
        kick_real = real * cosine + imag * sine
        kick_imag = (imag * cosine - real * sine).astype(jnp.bfloat16)
        kick[q, :quarter, :lanes] = kick_real.astype(jnp.bfloat16)
        kick[q, :quarter, lanes:] = kick_imag
        kick[q, quarter:, :lanes] = kick_imag
        kick[q, quarter:, lanes:] = (-kick_real).astype(jnp.bfloat16)

    backs = []
    for q in range(4):
        back = jnp.dot(back_ref[q], kick[q], preferred_element_type=jnp.float32)
        backs.append((back[:, :lanes], back[:, lanes:]))
    even, odd = complex_sum(backs[0], backs[2]), complex_sum(backs[1], backs[3])
    skew = quarter_turn(complex_difference(backs[1], backs[3]))
    rest = complex_difference(backs[0], backs[2])
    unfolded = (
        complex_sum(even, odd),
        complex_difference(rest, skew),
        complex_difference(even, odd),
        complex_sum(rest, skew),
    )
    for j, (real, imag) in enumerate(unfolded):
        own = slice(j * blocks, (j + 1) * blocks)
        real, imag = real * weight, imag * weight
        low = jnp.where(first, real, swap_halves(imag)).astype(jnp.bfloat16)
        high = jnp.where(first, swap_halves(real), imag).astype(jnp.bfloat16)
        low = low.reshape(blocks, local_modes, lanes)
        high = high.reshape(blocks, local_modes, lanes)
        skip = 0
        for out_ref in out_refs:
            count = out_ref.shape[3]
            out_ref[0, own, 0] = low[:, skip : skip + count]
            out_ref[1, own, 0] = high[:, skip : skip + count]
            skip += count


def analysis_kernel(skip, first, last, cutoff_ref, fields_ref, basis_ref, *refs):
    out_ref, stage = refs[-2:]
    block, radii, degrees = basis_ref.shape
    local = skip + pl.program_id(0) * block
    step = pl.program_id(1)
    stage[...] = fields_ref[...].astype(jnp.float32).reshape(stage.shape)

    def add_to(held_ref):
        for i in range(block):
            field = stage[pl.ds(i, radii, stride=block), :].astype(jnp.bfloat16)
            part = lax.dot_general(
                field, basis_ref[i], (((0,), (0,)), ((), ())), preferred_element_type=jnp.float32
            )
            out_ref[i] = part if held_ref is None else part + held_ref[i]

    @pl.when(step == 0)
    def _():
        add_to(None if first else refs[0])

    @pl.when(step > 0)
    def _():
        add_to(out_ref)

    if last:

        @pl.when(step == pl.num_programs(1) - 1)
        def _():
            degree_ids = lax.broadcasted_iota(jnp.int32, (1, degrees), 1)
            for i in range(block):
                kept = (degree_ids < cutoff_ref[local + i]).astype(jnp.float32)
                out_ref[i] = out_ref[i] * kept


def params(grid_rank=1):
    return pltpu.CompilerParams(
        vmem_limit_bytes=VMEM_LIMIT, dimension_semantics=("arbitrary",) * grid_rank
    )


def row_parts(row_count):
    parts, done = [], 0
    for share in np.cumsum(ROW_SHARES):
        upto = row_count * int(share) // int(np.sum(ROW_SHARES))
        if upto > done:
            parts.append((done, upto - done))
            done = upto
    return parts


def mode_parts(local_modes, block):
    if local_modes < 2 * block:
        return [(0, local_modes)]
    return [(0, local_modes - block), (local_modes - block, block)]


def on_device(spectrum, radial_basis, cutoff, couplings, trap_potential, weights):
    local_modes, planes, degrees = spectrum.shape[1], spectrum.shape[3], spectrum.shape[4]
    radius_count = radial_basis.shape[1]
    axes = ("comp", "mr")
    components, mode_width = lax.axis_size("comp"), lax.axis_size("mr")
    device_count = components * mode_width
    mode_total = local_modes * mode_width
    lanes = 2 * planes
    block = math.gcd(local_modes, MODE_BLOCK)

    first_mode = (lax.axis_index("mr") * local_modes).reshape(1).astype(jnp.int32)
    mode_phases, degree_phases = kinetic_tables(mode_total, degrees)
    table, back_table = spectral_tables(mode_total)
    to_turns = TIMESTEP / (2.0 * math.pi)
    lane_strength = jnp.repeat(couplings.T * to_turns, planes, axis=1)

    me = lax.axis_index(axes)
    parts = row_parts(radius_count // device_count)

    in_smem = pl.BlockSpec(memory_space=pltpu.SMEM)

    def synthesis(start, rows):
        radii = rows * device_count
        part = math.gcd(block, MODE_PART)
        per_block = block // part
        return pl.pallas_call(
            functools.partial(synthesis_kernel, planes),
            grid=(local_modes // block, per_block),
            out_shape=jax.ShapeDtypeStruct((radii, local_modes, lanes), jnp.bfloat16),
            in_specs=[
                in_smem,
                in_smem,
                in_smem,
                pl.BlockSpec((2, degrees), lambda i, j: (0, 0)),
                pl.BlockSpec(
                    (None, part, 2, planes, degrees), lambda i, j: (0, i * per_block + j, 0, 0, 0)
                ),
                pl.BlockSpec(
                    (pl.Element(part), pl.Element(radii), pl.Element(degrees)),
                    lambda i, j: ((i * per_block + j) * part, start * device_count, 0),
                ),
            ],
            out_specs=pl.BlockSpec((radii, block, lanes), lambda i, j: (0, i, 0)),
            scratch_shapes=[pltpu.VMEM((radii * block, lanes), jnp.float32)],
            compiler_params=params(2),
            cost_estimate=pl.CostEstimate(
                flops=2 * local_modes * radii * degrees * lanes,
                bytes_accessed=4 * local_modes * lanes * degrees
                + 2 * local_modes * radii * (degrees + lanes),
                transcendentals=0,
            ),
            name="synthesis",
        )(first_mode, cutoff, mode_phases, degree_phases, spectrum, radial_basis)

    def physical(radial, start, rows, groups):
        first_radius = start * device_count + me * rows
        trap = lax.dynamic_slice_in_dim(trap_potential, first_radius, rows) * to_turns
        weight = lax.dynamic_slice_in_dim(weights, first_radius, rows)
        quarter = mode_total // 4

        def shape(count):
            return (components, mode_width, rows, count, lanes)

        def spec(count):
            return pl.BlockSpec(
                (components, mode_width, 1, count, lanes), lambda i: (0, 0, i, 0, 0)
            )

        counts = [count for _, count in groups]
        kicked = pl.pallas_call(
            physical_kernel,
            grid=(rows,),
            out_shape=[jax.ShapeDtypeStruct(shape(count), jnp.bfloat16) for count in counts],
            in_specs=[
                in_smem,
                in_smem,
                pl.BlockSpec((2, lanes), lambda i: (0, 0)),
                pl.BlockSpec((4, quarter, 2 * quarter), lambda i: (0, 0, 0)),
                pl.BlockSpec((4, quarter, 2 * quarter), lambda i: (0, 0, 0)),
                spec(local_modes),
            ],
            out_specs=[spec(count) for count in counts],
            scratch_shapes=[
                pltpu.VMEM((4, 2 * quarter, 2 * lanes), jnp.bfloat16),
                pltpu.VMEM((4, 2 * quarter, 2 * lanes), jnp.bfloat16),
            ],
            compiler_params=params(),
            cost_estimate=pl.CostEstimate(
                flops=4 * rows * mode_total * mode_total * lanes,
                bytes_accessed=8 * rows * mode_total * lanes + 2 * mode_total * mode_total,
                transcendentals=0,
            ),
            name="physical",
        )(trap, weight, lane_strength, table, back_table, radial.reshape(shape(local_modes)))
        return [
            value.reshape(rows * device_count, count, lanes)
            for value, count in zip(kicked, counts)
        ]

    def analysis(fields, held, start, rows, last, skip):
        radii, count = fields.shape[:2]
        shift = skip // block
        steps = max(d for d in (1, 2, 4) if radii % (16 * d) == 0 and (d == 1 or radii // d >= 384))
        part = radii // steps
        out_spec = pl.BlockSpec((block, lanes, degrees), lambda i, j: (shift + i, 0, 0))
        operands = [cutoff, fields, radial_basis]
        in_specs = [
            in_smem,
            pl.BlockSpec((part, block, lanes), lambda i, j: (j, i, 0)),
            pl.BlockSpec(
                (pl.Element(block), pl.Element(part), pl.Element(degrees)),
                lambda i, j: (
                    skip + i * block,
                    pl.multiple_of(start * device_count + j * part, 16),
                    0,
                ),
            ),
        ]
        if held is not None:
            operands.append(held)
            in_specs.append(out_spec)
        return pl.pallas_call(
            functools.partial(analysis_kernel, skip, held is None, last),
            grid=(count // block, steps),
            out_shape=jax.ShapeDtypeStruct((local_modes, lanes, degrees), jnp.float32),
            in_specs=in_specs,
            out_specs=out_spec,
            scratch_shapes=[pltpu.VMEM((part * block, lanes), jnp.float32)],
            input_output_aliases={} if held is None else {3: 0},
            compiler_params=params(2),
            cost_estimate=pl.CostEstimate(
                flops=2 * count * radii * degrees * lanes,
                bytes_accessed=2 * count * radii * (degrees + lanes)
                + 8 * count * lanes * degrees,
                transcendentals=0,
            ),
            name="analysis",
        )(*operands)

    def exchange(value):
        return lax.all_to_all(value, axes, split_axis=0, concat_axis=0, tiled=True)

    arrived = [exchange(synthesis(*part)) for part in parts]
    returned = []
    for k, part in enumerate(parts):
        last = k == len(parts) - 1
        groups = mode_parts(local_modes, block) if last else [(0, local_modes)]
        for (skip, _), kicked in zip(groups, physical(arrived[k], *part, groups)):
            returned.append((exchange(kicked), part, last, skip))
    evolved = None
    for fields, part, last, skip in returned:
        evolved = analysis(fields, evolved, *part, last, skip)
    return evolved.reshape(1, local_modes, 2, planes, degrees)


def solution(mesh):
    in_specs = (P("comp", "mr", None, None, None), P("mr", None, None), P("mr"), P(), P(), P())
    out_specs = P("comp", "mr", None, None, None)
    return jax.shard_map(
        on_device, mesh=mesh, in_specs=in_specs, out_specs=out_specs, check_vma=False
    )
```

time: 828 us -> 795 us (0.960)
  blocking collectives: 0 us -> 228 us
  waiting for transfers between devices: 526 us -> 362 us
  Pallas kernels: 245 us -> 169 us
  starting transfers between devices: 33 us -> 16.8 us
  other arithmetic: 22.9 us -> 13 us
    all_to_all x0 -> x1, blocking collectives: none -> 228 us  [exchange(): return lax.all_to_all(value, axes, split_axis=0, concat_axis=0, tiled=True)]
    all_to_all x8 -> x4, waiting for transfers between devices: 526 us -> 362 us  [exchange(): return lax.all_to_all(value, axes, split_axis=0, concat_axis=0, tiled=True)]
    pallas_call x12 -> x7, Pallas kernels: 245 us -> 169 us  [the longest x2 68 us: physical(): pl.pallas_call(physical_kernel, grid=(rows,), out_shape=[jax.ShapeDtypeSt...]
    all_to_all x8 -> x4, starting transfers between devices: 33 us -> 16.8 us  [exchange(): return lax.all_to_all(value, axes, split_axis=0, concat_axis=0, tiled=True)]
    convert_element_type x2 -> x1, other arithmetic: 17.9 us -> 8.89 us  [spectral_tables(): cosine = (jnp.cos(angles) * normalizer).astype(jnp.bfloat16)]
  transfers between devices with their start and end apart: 8 -> 4, of which waited for: 8 -> 4; matrix products, arithmetic and copies ran while one was open for 3% -> 2% of each run, Pallas kernels for 25% -> 18%
where the time goes in v2:
time: 795 us
  waiting for transfers between devices  362 us (46%)
  blocking collectives  228 us (29%)
  Pallas kernels  169 us (21%)
  starting transfers between devices  16.8 us (2%)
  other arithmetic  13 us (2%)
    all_to_all x4, waiting for transfers between devices, exchange(): return lax.all_to_all(value, axes, split_axis=0, concat_axis=0, tiled=True)  362 us
    all_to_all x1, blocking collectives, exchange(): return lax.all_to_all(value, axes, split_axis=0, concat_axis=0, tiled=True)  228 us
    pallas_call x2, Pallas kernels, physical(): pl.pallas_call(physical_kernel, grid=(rows,), out_shape=[jax.ShapeDtypeSt...  68 us
    pallas_call x3, Pallas kernels, analysis(): pl.pallas_call(functools.partial(analysis_kernel, skip, held is None, las...  56.3 us
    pallas_call x2, Pallas kernels, synthesis(): pl.pallas_call(functools.partial(synthesis_kernel, planes), grid=(local_m...  44.3 us
    all_to_all x4, starting transfers between devices, exchange(): return lax.all_to_all(value, axes, split_axis=0, concat_axis=0, tiled=True)  16.8 us
  transfers between devices with their start and end apart: 4, of which 4 were waited for; matrix products, arithmetic and copies ran while one was open for 2% of the time, Pallas kernels for 18%

profile of v2, /device:TPU:0, one launch (start us, length us, event | category | flops | bytes accessed | tf_op | source)
XLA Modules:
  0.0 794.8 jit_solution(15079786245996903019)
XLA Ops:
  0.0 12.8 %synthesis.3 = bf16[192,64,128]{2,1,0:T(8,128)(2,1)} custom-call(s32[1]{0:T(128)} %bitcast.1.first_ref, s32[64]{0:T(128)} %cutoff_ref.9, f32[2,1024]{1,0:T(2,128)} %constant.53.clone.mode_ref, f32[2,512]{1,0:T(2,128)} %constant.54.clone.degree_ref, f32[1,64,2,64,512]{4,3,2,1,0:T(8,128)} %spectrum_ref.3, bf16[64,1024,512]{2,1,0:T(8,128)(2,1)} %basis_ref.9), custom_call_target="tpu_custom_call" | custom-call | flops 1610612736 | bytes 32505856 | tf_op jit(solution)/shard_map/synthesis/pallas_call | solution.py:284
  12.8 7.3 all-to-all-start.3
  20.1 31.5 %synthesis.2 = bf16[832,64,128]{2,1,0:T(8,128)(2,1)} custom-call(s32[1]{0:T(128)} %bitcast.1.first_ref, s32[64]{0:T(128)} %cutoff_ref.9, f32[2,1024]{1,0:T(2,128)} %constant.53.clone.mode_ref, f32[2,512]{1,0:T(2,128)} %constant.54.clone.degree_ref, f32[1,64,2,64,512]{4,3,2,1,0:T(8,128)} %spectrum_ref.3, bf16[64,1024,512]{2,1,0:T(8,128)(2,1)} %basis_ref.9), custom_call_target="tpu_custom_call" | custom-call | flops 6979321856 | bytes 84934656 | tf_op jit(solution)/shard_map/synthesis/pallas_call | solution.py:284
  51.6 40.9 %all-to-all-done.3 = bf16[192,64,128]{2,1,0:T(8,128)(2,1)S(1)} async-done(((bf16[192,64,128]{2,1,0:T(8,128)(2,1)}), bf16[192,64,128]{2,1,0:T(8,128)(2,1)S(1)}, u32[]{:S(2)}, u32[]{:S(2)}) %all-to-all-start.3) | async-done | bytes 3145760 | tf_op jit(solution)/shard_map/all_to_all | solution.py:399
  92.6 1.6 copy-done.2
  94.2 3.8 all-to-all-start
  98.8 1.3 dynamic_slice.15.weight_ref
  100.1 1.3 dynamic-slice_multiply_fusion.trap_ref
  101.4 8.9 %multiply_convert_fusion.1 = (bf16[4,256,256]{2,1,0:T(8,128)(2,1)S(1)}, bf16[4,256,256]{2,1,0:T(8,128)(2,1)S(1)}, bf16[4,256,256]{2,1,0:T(8,128)(2,1)S(1)}, bf16[4,256,256]{2,1,0:T(8,128)(2,1)S(1)}) fusion(s32[4,256]{1,0:T(4,128)S(1)} %iota_add_fusion), kind=kLoop, calls=%fused_computation.15 | loop fusion | flops 9437184 | bytes 2101248 | tf_op jit(solution)/shard_map/convert_element_type | solution.py:27
  110.3 1.5 pad_maximum_fusion
  111.8 14.3 %physical.3 = bf16[2,16,6,64,128]{4,3,2,1,0:T(8,128)(2,1)} custom-call(f32[6]{0:T(128)} %dynamic-slice_multiply_fusion.trap_ref, f32[6]{0:T(128)} %dynamic_slice.15.weight_ref, f32[2,128]{1,0:T(2,128)} %reshape.48.lanes_ref, bf16[4,256,512]{2,1,0:T(8,128)(2,1)} %get-tuple-element.13.table_ref, bf16[4,256,512]{2,1,0:T(8,128)(2,1)} %get-tuple-element.14.back_ref, ...), custom_call_target="tpu_custom_call" | custom-call | flops 3221225472 | bytes 8388608 | tf_op jit(solution)/shard_map/physical/pallas_call | solution.py:328
  126.1 270.0 %all-to-all-done = bf16[832,64,128]{2,1,0:T(8,128)(2,1)} async-done(((bf16[832,64,128]{2,1,0:T(8,128)(2,1)}), bf16[832,64,128]{2,1,0:T(8,128)(2,1)}, u32[]{:S(2)}, u32[]{:S(2)}) %all-to-all-start) | async-done | bytes 13631520 | tf_op jit(solution)/shard_map/all_to_all | solution.py:399
  396.1 2.8 all-to-all-start.4
  398.9 1.4 dynamic_slice.13.weight_ref
  400.3 1.3 dynamic-slice_multiply_fusion.1.trap_ref
  401.5 53.7 %physical.2 = (bf16[2,16,26,48,128]{4,3,2,1,0:T(8,128)(2,1)}, bf16[2,16,26,16,128]{4,3,2,1,0:T(8,128)(2,1)}) custom-call(f32[26]{0:T(128)} %dynamic-slice_multiply_fusion.1.trap_ref, f32[26]{0:T(128)} %dynamic_slice.13.weight_ref, f32[2,128]{1,0:T(2,128)} %reshape.48.lanes_ref, bf16[4,256,512]{2,1,0:T(8,128)(2,1)} %get-tuple-element.13.table_ref, ...), custom_call_target="tpu_custom_call" | custom-call | flops 13958643712 | bytes 29360128 | tf_op jit(solution)/shard_map/physical/pallas_call | solution.py:328
  455.2 16.2 %all-to-all-done.4.fields_ref = bf16[192,64,128]{2,1,0:T(8,128)(2,1)S(1)} async-done(((bf16[192,64,128]{2,1,0:T(8,128)(2,1)}), bf16[192,64,128]{2,1,0:T(8,128)(2,1)S(1)}, u32[]{:S(2)}, u32[]{:S(2)}) %all-to-all-start.4) | async-done | bytes 3145760 | tf_op jit(solution)/shard_map/all_to_all | solution.py:399
  471.4 228.0 %all_to_all.25.fields_ref = bf16[832,48,128]{2,1,0:T(8,128)(2,1)} all-to-all(bf16[832,48,128]{2,1,0:T(8,128)(2,1)} %bitcast.9), channel_id=1, replica_groups=mesh['comp'=2,'mr'=16] {'comp','mr'}, dimensions={0} | all-to-all | bytes 20447232 | tf_op jit(solution)/shard_map/all_to_all | solution.py:399
  699.4 3.0 all-to-all-start.1
  702.3 13.1 %analysis.3.refs_0_ = f32[64,128,512]{2,1,0:T(8,128)} custom-call(s32[64]{0:T(128)} %cutoff_ref.9, bf16[192,64,128]{2,1,0:T(8,128)(2,1)} %copy-done.1, bf16[64,1024,512]{2,1,0:T(8,128)(2,1)} %basis_ref.9), custom_call_target="tpu_custom_call" | custom-call | flops 1610612736 | bytes 49283072 | tf_op jit(solution)/shard_map/analysis/pallas_call | solution.py:380
  715.4 30.3 %analysis.4.refs_0_ = f32[64,128,512]{2,1,0:T(8,128)} custom-call(s32[64]{0:T(128)} %cutoff_ref.9, bf16[832,48,128]{2,1,0:T(8,128)(2,1)} %all_to_all.25.fields_ref, bf16[64,1024,512]{2,1,0:T(8,128)(2,1)} %basis_ref.9, f32[64,128,512]{2,1,0:T(8,128)} %analysis.3.refs_0_), custom_call_target="tpu_custom_call", output_to_operand_aliasing={{}: (3, {})} | custom-call | flops 5234491392 | bytes 76283904 | tf_op jit(solution)/shard_map/analysis/pallas_call | solution.py:380
  745.7 34.5 %all-to-all-done.1.fields_ref = bf16[832,16,128]{2,1,0:T(8,128)(2,1)S(1)} async-done(((bf16[832,16,128]{2,1,0:T(8,128)(2,1)}), bf16[832,16,128]{2,1,0:T(8,128)(2,1)S(1)}, u32[]{:S(2)}, u32[]{:S(2)}) %all-to-all-start.1) | async-done | bytes 3407904 | tf_op jit(solution)/shard_map/all_to_all | solution.py:399
  780.2 1.7 copy-done
  781.9 13.0 %analysis.5 = f32[64,128,512]{2,1,0:T(8,128)} custom-call(s32[64]{0:T(128)} %cutoff_ref.9, bf16[832,16,128]{2,1,0:T(8,128)(2,1)} %copy-done, bf16[64,1024,512]{2,1,0:T(8,128)(2,1)} %basis_ref.9, f32[64,128,512]{2,1,0:T(8,128)} %analysis.4.refs_0_), custom_call_target="tpu_custom_call", output_to_operand_aliasing={{}: (3, {})} | custom-call | flops 1744830464 | bytes 25427968 | tf_op jit(solution)/shard_map/analysis/pallas_call | solution.py:380
  (12 shorter events, 0.8 us)
Async XLA Ops:
  12.8 79.7 %all-to-all-start.3 = ((bf16[192,64,128]{2,1,0:T(8,128)(2,1)}), bf16[192,64,128]{2,1,0:T(8,128)(2,1)S(1)}, u32[]{:S(2)}, u32[]{:S(2)}) async-start(bf16[192,64,128]{2,1,0:T(8,128)(2,1)} %synthesis.3), calls=%async_computation.3 | async-start | bytes 6291456 | tf_op jit(solution)/shard_map/all_to_all | solution.py:399
  51.6 46.4 %copy-start.3 = (f32[2,2]{1,0:T(2,128)S(1)}, f32[2,2]{1,0:T(2,128)}, u32[]{:S(2)}) copy-start(f32[2,2]{1,0:T(2,128)} %param.11) | copy-start | bytes 52
  92.6 1.6 copy-start.2
  94.2 302.0 %all-to-all-start = ((bf16[832,64,128]{2,1,0:T(8,128)(2,1)}), bf16[832,64,128]{2,1,0:T(8,128)(2,1)}, u32[]{:S(2)}, u32[]{:S(2)}) async-start(bf16[832,64,128]{2,1,0:T(8,128)(2,1)} %synthesis.2), calls=%async_computation | async-start | bytes 27262976 | tf_op jit(solution)/shard_map/all_to_all | solution.py:399
  396.1 75.3 %all-to-all-start.4 = ((bf16[192,64,128]{2,1,0:T(8,128)(2,1)}), bf16[192,64,128]{2,1,0:T(8,128)(2,1)S(1)}, u32[]{:S(2)}, u32[]{:S(2)}) async-start(bf16[192,64,128]{2,1,0:T(8,128)(2,1)} %bitcast.12), calls=%async_computation.4 | async-start | bytes 6291456 | tf_op jit(solution)/shard_map/all_to_all | solution.py:399
  471.4 228.0 %copy-start.1 = (bf16[192,64,128]{2,1,0:T(8,128)(2,1)}, bf16[192,64,128]{2,1,0:T(8,128)(2,1)S(1)}, u32[]{:S(2)}) copy-start(bf16[192,64,128]{2,1,0:T(8,128)(2,1)S(1)} %all-to-all-done.4.fields_ref) | copy-start | bytes 9437188
  699.4 80.8 %all-to-all-start.1 = ((bf16[832,16,128]{2,1,0:T(8,128)(2,1)}), bf16[832,16,128]{2,1,0:T(8,128)(2,1)S(1)}, u32[]{:S(2)}, u32[]{:S(2)}) async-start(bf16[832,16,128]{2,1,0:T(8,128)(2,1)} %bitcast.10), calls=%async_computation.1 | async-start | bytes 6815744 | tf_op jit(solution)/shard_map/all_to_all | solution.py:399
  780.2 1.7 copy-start

commit v3 on v2

--- a/solution.py
+++ b/solution.py
@@ -11,10 +11,9 @@
 
 TIMESTEP = 0.5
 ROTATION = 0.7
-VMEM_LIMIT = 60 * 1024 * 1024
-ROW_SHARES = (6, 26)
+ROW_SHARES = (5, 27)
 MODE_BLOCK = 16
-MODE_PART = 16
+LAST_MODES = 8
 
 
 def spectral_tables(mode_total):
@@ -83,12 +82,10 @@
 def synthesis_kernel(
     planes, first_ref, cutoff_ref, mode_ref, degree_ref, spectrum_ref, basis_ref, out_ref, stage
 ):
-    part, radii, degrees = basis_ref.shape
-    block = out_ref.shape[1]
-    inner = pl.program_id(1)
-    local = pl.program_id(0) * block + inner * part
+    block, radii, degrees = basis_ref.shape
+    local = pl.program_id(0) * block
     degree_ids = lax.broadcasted_iota(jnp.int32, (1, degrees), 1)
-    for i in range(part):
+    for i in range(block):
         mode = first_ref[0] + local + i
         mode_cos, mode_sin = mode_ref[0, mode], mode_ref[1, mode]
         degree_cos, degree_sin = degree_ref[0:1, :], degree_ref[1:2, :]
@@ -100,13 +97,10 @@
         coeffs = jnp.concatenate(
             [real * cosine + imag * sine, imag * cosine - real * sine], axis=0
         ).astype(jnp.bfloat16)
-        stage[pl.ds(inner * part + i, radii, stride=block), :] = lax.dot_general(
+        stage[pl.ds(i, radii, stride=block), :] = lax.dot_general(
             basis_ref[i], coeffs, (((1,), (1,)), ((), ())), preferred_element_type=jnp.float32
         )
-
-    @pl.when(inner == pl.num_programs(1) - 1)
-    def _():
-        out_ref[...] = stage[...].reshape(out_ref.shape).astype(jnp.bfloat16)
+    out_ref[...] = stage[...].reshape(out_ref.shape).astype(jnp.bfloat16)
 
 
 def complex_sum(left, right):
@@ -189,15 +183,13 @@
     for j, (real, imag) in enumerate(unfolded):
         own = slice(j * blocks, (j + 1) * blocks)
         real, imag = real * weight, imag * weight
-        low = jnp.where(first, real, swap_halves(imag)).astype(jnp.bfloat16)
-        high = jnp.where(first, swap_halves(real), imag).astype(jnp.bfloat16)
-        low = low.reshape(blocks, local_modes, lanes)
-        high = high.reshape(blocks, local_modes, lanes)
+        low = jnp.where(first, real, swap_halves(imag)).reshape(blocks, local_modes, lanes)
+        high = jnp.where(first, swap_halves(real), imag).reshape(blocks, local_modes, lanes)
         skip = 0
         for out_ref in out_refs:
             count = out_ref.shape[3]
-            out_ref[0, own, 0] = low[:, skip : skip + count]
-            out_ref[1, own, 0] = high[:, skip : skip + count]
+            out_ref[0, own, 0] = low[:, skip : skip + count].astype(jnp.bfloat16)
+            out_ref[1, own, 0] = high[:, skip : skip + count].astype(jnp.bfloat16)
             skip += count
 
 
@@ -234,9 +226,25 @@
                 out_ref[i] = out_ref[i] * kept
 
 
-def params(grid_rank=1):
+def hold_kernel(*refs):
+    del refs
+
+
+def hold(value, after):
+    anywhere = pl.BlockSpec(memory_space=pl.ANY)
+    return pl.pallas_call(
+        hold_kernel,
+        out_shape=jax.ShapeDtypeStruct(value.shape, value.dtype),
+        in_specs=[anywhere] * (1 + len(after)),
+        out_specs=anywhere,
+        input_output_aliases={0: 0},
+        name="hold",
+    )(value, *after)
+
+
+def params(grid_rank=1, mebibytes=60):
     return pltpu.CompilerParams(
-        vmem_limit_bytes=VMEM_LIMIT, dimension_semantics=("arbitrary",) * grid_rank
+        vmem_limit_bytes=mebibytes * 1024 * 1024, dimension_semantics=("arbitrary",) * grid_rank
     )
 
 
@@ -253,7 +261,7 @@
 def mode_parts(local_modes, block):
     if local_modes < 2 * block:
         return [(0, local_modes)]
-    return [(0, local_modes - block), (local_modes - block, block)]
+    return [(0, local_modes - LAST_MODES), (local_modes - LAST_MODES, LAST_MODES)]
 
 
 def on_device(spectrum, radial_basis, cutoff, couplings, trap_potential, weights):
@@ -279,28 +287,24 @@
 
     def synthesis(start, rows):
         radii = rows * device_count
-        part = math.gcd(block, MODE_PART)
-        per_block = block // part
         return pl.pallas_call(
             functools.partial(synthesis_kernel, planes),
-            grid=(local_modes // block, per_block),
+            grid=(local_modes // block,),
             out_shape=jax.ShapeDtypeStruct((radii, local_modes, lanes), jnp.bfloat16),
             in_specs=[
                 in_smem,
                 in_smem,
                 in_smem,
-                pl.BlockSpec((2, degrees), lambda i, j: (0, 0)),
+                pl.BlockSpec((2, degrees), lambda i: (0, 0)),
+                pl.BlockSpec((None, block, 2, planes, degrees), lambda i: (0, i, 0, 0, 0)),
                 pl.BlockSpec(
-                    (None, part, 2, planes, degrees), lambda i, j: (0, i * per_block + j, 0, 0, 0)
-                ),
-                pl.BlockSpec(
-                    (pl.Element(part), pl.Element(radii), pl.Element(degrees)),
-                    lambda i, j: ((i * per_block + j) * part, start * device_count, 0),
+                    (pl.Element(block), pl.Element(radii), pl.Element(degrees)),
+                    lambda i: (i * block, start * device_count, 0),
                 ),
             ],
-            out_specs=pl.BlockSpec((radii, block, lanes), lambda i, j: (0, i, 0)),
+            out_specs=pl.BlockSpec((radii, block, lanes), lambda i: (0, i, 0)),
             scratch_shapes=[pltpu.VMEM((radii * block, lanes), jnp.float32)],
-            compiler_params=params(2),
+            compiler_params=params(),
             cost_estimate=pl.CostEstimate(
                 flops=2 * local_modes * radii * degrees * lanes,
                 bytes_accessed=4 * local_modes * lanes * degrees
@@ -342,7 +346,7 @@
                 pltpu.VMEM((4, 2 * quarter, 2 * lanes), jnp.bfloat16),
                 pltpu.VMEM((4, 2 * quarter, 2 * lanes), jnp.bfloat16),
             ],
-            compiler_params=params(),
+            compiler_params=params(1, 48),
             cost_estimate=pl.CostEstimate(
                 flops=4 * rows * mode_total * mode_total * lanes,
                 bytes_accessed=8 * rows * mode_total * lanes + 2 * mode_total * mode_total,
@@ -357,6 +361,7 @@
 
     def analysis(fields, held, start, rows, last, skip):
         radii, count = fields.shape[:2]
+        block = math.gcd(count, MODE_BLOCK)
         shift = skip // block
         steps = max(d for d in (1, 2, 4) if radii % (16 * d) == 0 and (d == 1 or radii // d >= 384))
         part = radii // steps
@@ -385,7 +390,7 @@
             out_specs=out_spec,
             scratch_shapes=[pltpu.VMEM((part * block, lanes), jnp.float32)],
             input_output_aliases={} if held is None else {3: 0},
-            compiler_params=params(2),
+            compiler_params=params(2, 50),
             cost_estimate=pl.CostEstimate(
                 flops=2 * count * radii * degrees * lanes,
                 bytes_accessed=2 * count * radii * (degrees + lanes)
@@ -399,15 +404,21 @@
         return lax.all_to_all(value, axes, split_axis=0, concat_axis=0, tiled=True)
 
     arrived = [exchange(synthesis(*part)) for part in parts]
-    returned = []
+    kicked = []
     for k, part in enumerate(parts):
         last = k == len(parts) - 1
         groups = mode_parts(local_modes, block) if last else [(0, local_modes)]
-        for (skip, _), kicked in zip(groups, physical(arrived[k], *part, groups)):
-            returned.append((exchange(kicked), part, last, skip))
-    evolved = None
-    for fields, part, last, skip in returned:
-        evolved = analysis(fields, evolved, *part, last, skip)
+        for (skip, _), values in zip(groups, physical(arrived[k], *part, groups)):
+            kicked.append((values, part, last, skip))
+    evolved, before, waiting = None, None, None
+    for values, part, last, skip in kicked:
+        if before is not None:
+            values = hold(values, [before])
+        fields = exchange(values)
+        if waiting is not None:
+            before = evolved = analysis(waiting[0], evolved, *waiting[1:])
+        waiting = (fields, *part, last, skip)
+    evolved = analysis(waiting[0], evolved, *waiting[1:])
     return evolved.reshape(1, local_modes, 2, planes, degrees)
 
 

time: 795 us -> 788 us (level)
  blocking collectives: 228 us -> 0 us
  waiting for transfers between devices: 362 us -> 583 us
    all_to_all x1 -> x0, blocking collectives: 228 us -> none  [exchange(): return lax.all_to_all(value, axes, split_axis=0, concat_axis=0, tiled=True)]
    all_to_all x4 -> x5, waiting for transfers between devices: 362 us -> 583 us  [exchange(): return lax.all_to_all(value, axes, split_axis=0, concat_axis=0, tiled=True)]
    all_to_all x4 -> x5, starting transfers between devices: 16.8 us -> 21 us  [exchange(): return lax.all_to_all(value, axes, split_axis=0, concat_axis=0, tiled=True)]
  transfers between devices with their start and end apart: 4 -> 5, of which waited for: 4 -> 5; matrix products, arithmetic and copies ran while one was open for 2% -> 2% of each run, Pallas kernels for 18% -> 18%
where the time goes in v3:
time: 788 us; the launch traced here: 787 us
  waiting for transfers between devices  583 us (74%)
  Pallas kernels  163 us (21%)
  starting transfers between devices  21 us (3%)
  other arithmetic  10.6 us (1%)
  local copies, waits for them, and re-layouts  10.4 us (1%)
    all_to_all x5, waiting for transfers between devices, exchange(): return lax.all_to_all(value, axes, split_axis=0, concat_axis=0, tiled=True)  583 us
    pallas_call x2, Pallas kernels, physical(): pl.pallas_call(physical_kernel, grid=(rows,), out_shape=[jax.ShapeDtypeSt...  65.4 us
    pallas_call x3, Pallas kernels, analysis(): pl.pallas_call(functools.partial(analysis_kernel, skip, held is None, las...  52.6 us
    pallas_call x2, Pallas kernels, synthesis(): pl.pallas_call(functools.partial(synthesis_kernel, planes), grid=(local_m...  44.5 us
    all_to_all x5, starting transfers between devices, exchange(): return lax.all_to_all(value, axes, split_axis=0, concat_axis=0, tiled=True)  21 us
  transfers between devices with their start and end apart: 5, of which 5 were waited for; matrix products, arithmetic and copies ran while one was open for 2% of the time, Pallas kernels for 18%

profile of v3, /device:TPU:0, one launch (start us, length us, event | category | flops | bytes accessed | tf_op | source)
XLA Modules:
  0.0 787.2 jit_solution(6979995470350823413)
XLA Ops:
  0.0 11.9 %synthesis.3 = bf16[160,64,128]{2,1,0:T(8,128)(2,1)} custom-call(s32[1]{0:T(128)} %bitcast.1.first_ref, s32[64]{0:T(128)} %cutoff_ref.9, f32[2,1024]{1,0:T(2,128)} %constant.53.clone.mode_ref, f32[2,512]{1,0:T(2,128)} %constant.54.clone.degree_ref, f32[1,64,2,64,512]{4,3,2,1,0:T(8,128)} %spectrum_ref.3, bf16[64,1024,512]{2,1,0:T(8,128)(2,1)} %basis_ref.9), custom_call_target="tpu_custom_call" | custom-call | flops 1342177280 | bytes 29884416 | tf_op jit(solution)/shard_map/synthesis/pallas_call | solution.py:290
  11.9 7.3 all-to-all-start.1
  19.2 32.6 %synthesis.2 = bf16[864,64,128]{2,1,0:T(8,128)(2,1)} custom-call(s32[1]{0:T(128)} %bitcast.1.first_ref, s32[64]{0:T(128)} %cutoff_ref.9, f32[2,1024]{1,0:T(2,128)} %constant.53.clone.mode_ref, f32[2,512]{1,0:T(2,128)} %constant.54.clone.degree_ref, f32[1,64,2,64,512]{4,3,2,1,0:T(8,128)} %spectrum_ref.3, bf16[64,1024,512]{2,1,0:T(8,128)(2,1)} %basis_ref.9), custom_call_target="tpu_custom_call" | custom-call | flops 7247757312 | bytes 87556096 | tf_op jit(solution)/shard_map/synthesis/pallas_call | solution.py:290
  51.8 28.8 %all-to-all-done.1 = bf16[160,64,128]{2,1,0:T(8,128)(2,1)S(1)} async-done(((bf16[160,64,128]{2,1,0:T(8,128)(2,1)}), bf16[160,64,128]{2,1,0:T(8,128)(2,1)S(1)}, u32[]{:S(2)}, u32[]{:S(2)}) %all-to-all-start.1) | async-done | bytes 2621472 | tf_op jit(solution)/shard_map/all_to_all | solution.py:404
  80.6 1.5 copy-done.7
  82.0 3.8 all-to-all-start
  87.7 8.9 %multiply_convert_fusion.1 = (bf16[4,256,256]{2,1,0:T(8,128)(2,1)S(1)}, bf16[4,256,256]{2,1,0:T(8,128)(2,1)S(1)}, bf16[4,256,256]{2,1,0:T(8,128)(2,1)S(1)}, bf16[4,256,256]{2,1,0:T(8,128)(2,1)S(1)}) fusion(s32[4,256]{1,0:T(4,128)S(1)} %iota_add_fusion), kind=kLoop, calls=%fused_computation.15 | loop fusion | flops 9437184 | bytes 2101248 | tf_op jit(solution)/shard_map/convert_element_type | solution.py:26
  96.8 10.9 %physical.3 = bf16[2,16,5,64,128]{4,3,2,1,0:T(8,128)(2,1)S(1)} custom-call(f32[5]{0:T(128)S(1)} %dynamic-slice_multiply_fusion.trap_ref, f32[5]{0:T(128)S(1)} %dynamic_slice.15.weight_ref, f32[2,128]{1,0:T(2,128)S(1)} %reshape.48.lanes_ref, bf16[4,256,512]{2,1,0:T(8,128)(2,1)S(1)} %get-tuple-element.13.table_ref, ...), custom_call_target="tpu_custom_call" | custom-call | flops 2684354560 | bytes 7340032 | tf_op jit(solution)/shard_map/physical/pallas_call | solution.py:332
  107.6 1.5 copy-done.1
  110.1 1.0 copy-done.4
  111.1 284.3 %all-to-all-done = bf16[864,64,128]{2,1,0:T(8,128)(2,1)} async-done(((bf16[864,64,128]{2,1,0:T(8,128)(2,1)}), bf16[864,64,128]{2,1,0:T(8,128)(2,1)}, u32[]{:S(2)}, u32[]{:S(2)}) %all-to-all-start) | async-done | bytes 14155808 | tf_op jit(solution)/shard_map/all_to_all | solution.py:404
  395.4 3.0 all-to-all-start.2
  399.9 1.2 copy-done.3
  401.1 1.2 copy-done.5
  402.3 54.5 %physical.2 = (bf16[2,16,27,56,128]{4,3,2,1,0:T(8,128)(2,1)}, bf16[2,16,27,8,128]{4,3,2,1,0:T(8,128)(2,1)S(1)}) custom-call(f32[27]{0:T(128)S(1)} %dynamic-slice_multiply_fusion.1.trap_ref, f32[27]{0:T(128)S(1)} %dynamic_slice.13.weight_ref, f32[2,128]{1,0:T(2,128)S(1)} %reshape.48.lanes_ref, bf16[4,256,512]{2,1,0:T(8,128)(2,1)S(1)} %copy-done.3, ...), custom_call_target="tpu_custom_call" | custom-call | flops 14495514624 | bytes 30408704 | tf_op jit(solution)/shard_map/physical/pallas_call | solution.py:332
  456.8 1.2 copy-done
  458.1 1.5 all-to-all-done.2.fields_ref
  459.6 4.3 all-to-all-start.4
  463.9 11.4 %analysis.3.refs_1_.refs_0_ = f32[64,128,512]{2,1,0:T(8,128)} custom-call(s32[64]{0:T(128)S(1)} %copy-done.6, bf16[160,64,128]{2,1,0:T(8,128)(2,1)S(1)} %all-to-all-done.2.fields_ref, bf16[64,1024,512]{2,1,0:T(8,128)(2,1)} %basis_ref.9), custom_call_target="tpu_custom_call" | custom-call | flops 1342177280 | bytes 46661632 | tf_op jit(solution)/shard_map/analysis/pallas_call | solution.py:385
  475.2 260.1 %all-to-all-done.4.fields_ref = bf16[864,56,128]{2,1,0:T(8,128)(2,1)} async-done(((bf16[864,56,128]{2,1,0:T(8,128)(2,1)}), bf16[864,56,128]{2,1,0:T(8,128)(2,1)}, u32[]{:S(2)}, u32[]{:S(2)}) %all-to-all-start.4) | async-done | bytes 12386336 | tf_op jit(solution)/shard_map/all_to_all | solution.py:404
  735.4 2.7 all-to-all-start.3
  738.1 35.1 %analysis.4.refs_0_ = f32[64,128,512]{2,1,0:T(8,128)} custom-call(s32[64]{0:T(128)S(1)} %copy-done.6, bf16[864,56,128]{2,1,0:T(8,128)(2,1)} %all-to-all-done.4.fields_ref, bf16[64,1024,512]{2,1,0:T(8,128)(2,1)} %basis_ref.9, f32[64,128,512]{2,1,0:T(8,128)} %analysis.3.refs_1_.refs_0_), custom_call_target="tpu_custom_call", output_to_operand_aliasing={{}: (3, {})} | custom-call | flops 6341787648 | bytes 91291648 | tf_op jit(solution)/shard_map/analysis/pallas_call | solution.py:385
  773.2 7.8 all-to-all-done.3.fields_ref
  781.1 6.1 analysis.5
  (24 shorter events, 4.5 us)
Async XLA Ops:
  11.9 68.7 %all-to-all-start.1 = ((bf16[160,64,128]{2,1,0:T(8,128)(2,1)}), bf16[160,64,128]{2,1,0:T(8,128)(2,1)S(1)}, u32[]{:S(2)}, u32[]{:S(2)}) async-start(bf16[160,64,128]{2,1,0:T(8,128)(2,1)} %synthesis.3), calls=%async_computation.1 | async-start | bytes 5242880 | tf_op jit(solution)/shard_map/all_to_all | solution.py:404
  51.8 34.1 %copy-start.8 = (f32[2,2]{1,0:T(2,128)S(1)}, f32[2,2]{1,0:T(2,128)}, u32[]{:S(2)}) copy-start(f32[2,2]{1,0:T(2,128)} %param.11) | copy-start | bytes 52
  80.6 1.5 copy-start.7
  82.0 313.3 %all-to-all-start = ((bf16[864,64,128]{2,1,0:T(8,128)(2,1)}), bf16[864,64,128]{2,1,0:T(8,128)(2,1)}, u32[]{:S(2)}, u32[]{:S(2)}) async-start(bf16[864,64,128]{2,1,0:T(8,128)(2,1)} %synthesis.2), calls=%async_computation | async-start | bytes 28311552 | tf_op jit(solution)/shard_map/all_to_all | solution.py:404
  107.6 1.5 copy-start.1
  109.1 1.0 copy-start.2
  110.1 1.0 copy-start.4
  395.4 64.2 %all-to-all-start.2 = ((bf16[160,64,128]{2,1,0:T(8,128)(2,1)}), bf16[160,64,128]{2,1,0:T(8,128)(2,1)S(1)}, u32[]{:S(2)}, u32[]{:S(2)}) async-start(bf16[160,64,128]{2,1,0:T(8,128)(2,1)} %bitcast.10), calls=%async_computation.2 | async-start | bytes 5242880 | tf_op jit(solution)/shard_map/all_to_all | solution.py:404
  399.9 1.2 copy-start.3
  401.1 1.2 copy-start.5
  456.8 1.2 copy-start
  459.6 4.3 copy-start.6
  459.6 275.8 %all-to-all-start.4 = ((bf16[864,56,128]{2,1,0:T(8,128)(2,1)}), bf16[864,56,128]{2,1,0:T(8,128)(2,1)}, u32[]{:S(2)}, u32[]{:S(2)}) async-start(bf16[864,56,128]{2,1,0:T(8,128)(2,1)} %bitcast.11), calls=%async_computation.4 | async-start | bytes 24772608 | tf_op jit(solution)/shard_map/all_to_all | solution.py:404
  735.4 45.7 %all-to-all-start.3 = ((bf16[864,8,128]{2,1,0:T(8,128)(2,1)}), bf16[864,8,128]{2,1,0:T(8,128)(2,1)S(1)}, u32[]{:S(2)}, u32[]{:S(2)}) async-start(bf16[864,8,128]{2,1,0:T(8,128)(2,1)} %hold.1), calls=%async_computation.3 | async-start | bytes 3538944 | tf_op jit(solution)/shard_map/all_to_all | solution.py:404

commit v4 on v3

--- a/solution.py
+++ b/solution.py
@@ -7,6 +7,7 @@
 from jax import lax
 from jax.experimental import pallas as pl
 from jax.experimental.pallas import tpu as pltpu
+from jax.sharding import Mesh
 from jax.sharding import PartitionSpec as P
 
 TIMESTEP = 0.5
@@ -79,9 +80,26 @@
     return pltpu.roll(value, value.shape[-1] // 2, value.ndim - 1)
 
 
+def relative_rows(place_ref, outer, group, size):
+    for step in range(outer):
+        for turn in range(group):
+            device = (place_ref[0] ^ step) * group + (place_ref[1] ^ turn)
+            yield step, turn, pl.multiple_of(device * size, size)
+
+
 def synthesis_kernel(
-    planes, first_ref, cutoff_ref, mode_ref, degree_ref, spectrum_ref, basis_ref, out_ref, stage
+    planes,
+    outs,
+    place_ref,
+    first_ref,
+    cutoff_ref,
+    mode_ref,
+    degree_ref,
+    spectrum_ref,
+    basis_ref,
+    *refs,
 ):
+    out_refs, stage = refs[-outs - 1 : -1], refs[-1]
     block, radii, degrees = basis_ref.shape
     local = pl.program_id(0) * block
     degree_ids = lax.broadcasted_iota(jnp.int32, (1, degrees), 1)
@@ -100,7 +118,14 @@
         stage[pl.ds(i, radii, stride=block), :] = lax.dot_general(
             basis_ref[i], coeffs, (((1,), (1,)), ((), ())), preferred_element_type=jnp.float32
         )
-    out_ref[...] = stage[...].reshape(out_ref.shape).astype(jnp.bfloat16)
+    if outs == 1:
+        out_refs[0][...] = stage[...].reshape(out_refs[0].shape).astype(jnp.bfloat16)
+        return
+    group, rows, _, lanes = out_refs[0].shape
+    size = rows * block
+    for step, turn, start in relative_rows(place_ref, outs, group, size):
+        piece = stage[pl.ds(start, size), :].astype(jnp.bfloat16)
+        out_refs[step][turn] = piece.reshape(rows, block, lanes)
 
 
 def complex_sum(left, right):
@@ -115,19 +140,38 @@
     return -value[1], value[0]
 
 
-def physical_kernel(trap_ref, weight_ref, lanes_ref, table_ref, back_ref, x_ref, *refs):
-    *out_refs, work, kick = refs
+def physical_kernel(
+    relative,
+    inner,
+    outs,
+    place_ref,
+    trap_ref,
+    weight_ref,
+    lanes_ref,
+    table_ref,
+    back_ref,
+    x_ref,
+    *refs,
+):
+    out_refs, (work, kick) = refs[-outs - 2 : -2], refs[-2:]
     row = pl.program_id(0)
-    width, local_modes, lanes = x_ref.shape[1], x_ref.shape[3], x_ref.shape[4]
-    quarter = width * local_modes // 4
-    blocks = width // 4
+    local_modes, lanes = x_ref.shape[3:]
+    quarter = inner * local_modes
+
+    def block_at(component, j, i):
+        if relative:
+            return place_ref[1] ^ (component * inner + i), place_ref[0] ^ j
+        return component, j * inner + i
+
+    def field(component, j):
+        pieces = [x_ref[(*block_at(component, j, i), 0)] for i in range(inner)]
+        return jnp.concatenate(pieces, axis=0).astype(jnp.float32)
+
     first = lax.broadcasted_iota(jnp.int32, (quarter, lanes), 1) < lanes // 2
 
     parts = []
     for j in range(4):
-        own = slice(j * blocks, (j + 1) * blocks)
-        low = x_ref[0, own, 0].reshape(quarter, lanes).astype(jnp.float32)
-        high = x_ref[1, own, 0].reshape(quarter, lanes).astype(jnp.float32)
+        low, high = field(0, j), field(1, j)
         parts.append(
             (
                 jnp.where(first, low, swap_halves(high)),
@@ -181,24 +225,40 @@
         complex_sum(rest, skew),
     )
     for j, (real, imag) in enumerate(unfolded):
-        own = slice(j * blocks, (j + 1) * blocks)
         real, imag = real * weight, imag * weight
-        low = jnp.where(first, real, swap_halves(imag)).reshape(blocks, local_modes, lanes)
-        high = jnp.where(first, swap_halves(real), imag).reshape(blocks, local_modes, lanes)
-        skip = 0
-        for out_ref in out_refs:
-            count = out_ref.shape[3]
-            out_ref[0, own, 0] = low[:, skip : skip + count].astype(jnp.bfloat16)
-            out_ref[1, own, 0] = high[:, skip : skip + count].astype(jnp.bfloat16)
-            skip += count
-
-
-def analysis_kernel(skip, first, last, cutoff_ref, fields_ref, basis_ref, *refs):
-    out_ref, stage = refs[-2:]
+        values = (
+            jnp.where(first, real, swap_halves(imag)),
+            jnp.where(first, swap_halves(real), imag),
+        )
+        for component, value in enumerate(values):
+            for i in range(inner):
+                skip = i * local_modes
+                for out_ref in out_refs:
+                    count = out_ref.shape[3]
+                    out_ref[(*block_at(component, j, i), 0)] = value[skip : skip + count].astype(
+                        jnp.bfloat16
+                    )
+                    skip += count
+
+
+def analysis_kernel(skip, first, last, ins, place_ref, cutoff_ref, *refs):
+    fields_refs, basis_ref, held_ref, (out_ref, stage) = (
+        refs[:ins],
+        refs[ins],
+        refs[ins + 1],
+        refs[-2:],
+    )
     block, radii, degrees = basis_ref.shape
     local = skip + pl.program_id(0) * block
     step = pl.program_id(1)
-    stage[...] = fields_ref[...].astype(jnp.float32).reshape(stage.shape)
+    if ins == 1:
+        stage[...] = fields_refs[0][...].astype(jnp.float32).reshape(stage.shape)
+    else:
+        group, rows = fields_refs[0].shape[:2]
+        size = rows * block
+        for distance, turn, start in relative_rows(place_ref, ins, group, size):
+            piece = fields_refs[distance][turn].astype(jnp.float32)
+            stage[pl.ds(start, size), :] = piece.reshape(size, stage.shape[1])
 
     def add_to(held_ref):
         for i in range(block):
@@ -210,7 +270,7 @@
 
     @pl.when(step == 0)
     def _():
-        add_to(None if first else refs[0])
+        add_to(None if first else held_ref)
 
     @pl.when(step > 0)
     def _():
@@ -267,31 +327,40 @@
 def on_device(spectrum, radial_basis, cutoff, couplings, trap_potential, weights):
     local_modes, planes, degrees = spectrum.shape[1], spectrum.shape[3], spectrum.shape[4]
     radius_count = radial_basis.shape[1]
-    axes = ("comp", "mr")
-    components, mode_width = lax.axis_size("comp"), lax.axis_size("mr")
+    axes = ("comp", "hi", "lo")
+    components, outer, inner = (lax.axis_size(name) for name in axes)
+    mode_width, group = outer * inner, components * inner
     device_count = components * mode_width
     mode_total = local_modes * mode_width
     lanes = 2 * planes
     block = math.gcd(local_modes, MODE_BLOCK)
 
-    first_mode = (lax.axis_index("mr") * local_modes).reshape(1).astype(jnp.int32)
+    first_mode = (lax.axis_index(("hi", "lo")) * local_modes).reshape(1).astype(jnp.int32)
+    place = jnp.stack([lax.axis_index("hi"), lax.axis_index(("comp", "lo"))]).astype(jnp.int32)
     mode_phases, degree_phases = kinetic_tables(mode_total, degrees)
     table, back_table = spectral_tables(mode_total)
     to_turns = TIMESTEP / (2.0 * math.pi)
     lane_strength = jnp.repeat(couplings.T * to_turns, planes, axis=1)
 
-    me = lax.axis_index(axes)
+    anywhere = pl.BlockSpec(memory_space=pl.ANY)
     parts = row_parts(radius_count // device_count)
 
     in_smem = pl.BlockSpec(memory_space=pltpu.SMEM)
 
-    def synthesis(start, rows):
+    def synthesis(start, rows, relative, after):
         radii = rows * device_count
+        if relative:
+            shape, outs = (group, rows, local_modes, lanes), outer
+            out_spec = pl.BlockSpec((group, rows, block, lanes), lambda i: (0, 0, i, 0))
+        else:
+            shape, outs = (radii, local_modes, lanes), 1
+            out_spec = pl.BlockSpec((radii, block, lanes), lambda i: (0, i, 0))
         return pl.pallas_call(
-            functools.partial(synthesis_kernel, planes),
+            functools.partial(synthesis_kernel, planes, outs),
             grid=(local_modes // block,),
-            out_shape=jax.ShapeDtypeStruct((radii, local_modes, lanes), jnp.bfloat16),
+            out_shape=[jax.ShapeDtypeStruct(shape, jnp.bfloat16)] * outs,
             in_specs=[
+                in_smem,
                 in_smem,
                 in_smem,
                 in_smem,
@@ -301,8 +370,9 @@
                     (pl.Element(block), pl.Element(radii), pl.Element(degrees)),
                     lambda i: (i * block, start * device_count, 0),
                 ),
+                *[anywhere] * len(after),
             ],
-            out_specs=pl.BlockSpec((radii, block, lanes), lambda i: (0, i, 0)),
+            out_specs=[out_spec] * outs,
             scratch_shapes=[pltpu.VMEM((radii * block, lanes), jnp.float32)],
             compiler_params=params(),
             cost_estimate=pl.CostEstimate(
@@ -312,64 +382,81 @@
                 transcendentals=0,
             ),
             name="synthesis",
-        )(first_mode, cutoff, mode_phases, degree_phases, spectrum, radial_basis)
-
-    def physical(radial, start, rows, groups):
+        )(
+            place, first_mode, cutoff, mode_phases, degree_phases, spectrum, radial_basis, *after
+        )
+
+    def physical(radial, start, rows, groups, relative, after):
+        me = lax.axis_index(("hi", "comp", "lo") if relative else axes)
         first_radius = start * device_count + me * rows
         trap = lax.dynamic_slice_in_dim(trap_potential, first_radius, rows) * to_turns
         weight = lax.dynamic_slice_in_dim(weights, first_radius, rows)
         quarter = mode_total // 4
+        lead = (group, outer) if relative else (components, mode_width)
 
         def shape(count):
-            return (components, mode_width, rows, count, lanes)
+            return (*lead, rows, count, lanes)
 
         def spec(count):
-            return pl.BlockSpec(
-                (components, mode_width, 1, count, lanes), lambda i: (0, 0, i, 0, 0)
-            )
+            return pl.BlockSpec((*lead, 1, count, lanes), lambda i: (0, 0, i, 0, 0))
 
         counts = [count for _, count in groups]
-        kicked = pl.pallas_call(
-            physical_kernel,
+        table_spec = pl.BlockSpec((4, quarter, 2 * quarter), lambda i: (0, 0, 0))
+        return pl.pallas_call(
+            functools.partial(physical_kernel, relative, inner, len(counts)),
             grid=(rows,),
             out_shape=[jax.ShapeDtypeStruct(shape(count), jnp.bfloat16) for count in counts],
             in_specs=[
                 in_smem,
                 in_smem,
+                in_smem,
                 pl.BlockSpec((2, lanes), lambda i: (0, 0)),
-                pl.BlockSpec((4, quarter, 2 * quarter), lambda i: (0, 0, 0)),
-                pl.BlockSpec((4, quarter, 2 * quarter), lambda i: (0, 0, 0)),
+                table_spec,
+                table_spec,
                 spec(local_modes),
+                *[anywhere] * len(after),
             ],
             out_specs=[spec(count) for count in counts],
             scratch_shapes=[
                 pltpu.VMEM((4, 2 * quarter, 2 * lanes), jnp.bfloat16),
                 pltpu.VMEM((4, 2 * quarter, 2 * lanes), jnp.bfloat16),
             ],
-            compiler_params=params(1, 48),
+            compiler_params=params(),
             cost_estimate=pl.CostEstimate(
                 flops=4 * rows * mode_total * mode_total * lanes,
                 bytes_accessed=8 * rows * mode_total * lanes + 2 * mode_total * mode_total,
                 transcendentals=0,
             ),
             name="physical",
-        )(trap, weight, lane_strength, table, back_table, radial.reshape(shape(local_modes)))
-        return [
-            value.reshape(rows * device_count, count, lanes)
-            for value, count in zip(kicked, counts)
-        ]
+        )(
+            place,
+            trap,
+            weight,
+            lane_strength,
+            table,
+            back_table,
+            radial.reshape(shape(local_modes)),
+            *after,
+        )
 
     def analysis(fields, held, start, rows, last, skip):
-        radii, count = fields.shape[:2]
+        relative = len(fields) > 1
+        radii, count = rows * device_count, fields[0].shape[-2]
         block = math.gcd(count, MODE_BLOCK)
         shift = skip // block
-        steps = max(d for d in (1, 2, 4) if radii % (16 * d) == 0 and (d == 1 or radii // d >= 384))
+        halves = not relative and radii % 32 == 0 and radii >= 768
+        steps = 2 if halves else 1
         part = radii // steps
         out_spec = pl.BlockSpec((block, lanes, degrees), lambda i, j: (shift + i, 0, 0))
-        operands = [cutoff, fields, radial_basis]
+        if relative:
+            field_spec = pl.BlockSpec((group, rows, block, lanes), lambda i, j: (0, 0, i, 0))
+        else:
+            field_spec = pl.BlockSpec((part, block, lanes), lambda i, j: (j, i, 0))
+        operands = [place, cutoff, *fields, radial_basis]
         in_specs = [
             in_smem,
-            pl.BlockSpec((part, block, lanes), lambda i, j: (j, i, 0)),
+            in_smem,
+            *[field_spec] * len(fields),
             pl.BlockSpec(
                 (pl.Element(block), pl.Element(part), pl.Element(degrees)),
                 lambda i, j: (
@@ -383,13 +470,13 @@
             operands.append(held)
             in_specs.append(out_spec)
         return pl.pallas_call(
-            functools.partial(analysis_kernel, skip, held is None, last),
+            functools.partial(analysis_kernel, skip, held is None, last, len(fields)),
             grid=(count // block, steps),
             out_shape=jax.ShapeDtypeStruct((local_modes, lanes, degrees), jnp.float32),
             in_specs=in_specs,
             out_specs=out_spec,
             scratch_shapes=[pltpu.VMEM((part * block, lanes), jnp.float32)],
-            input_output_aliases={} if held is None else {3: 0},
+            input_output_aliases={} if held is None else {len(operands) - 1: 0},
             compiler_params=params(2, 50),
             cost_estimate=pl.CostEstimate(
                 flops=2 * count * radii * degrees * lanes,
@@ -403,28 +490,59 @@
     def exchange(value):
         return lax.all_to_all(value, axes, split_axis=0, concat_axis=0, tiled=True)
 
-    arrived = [exchange(synthesis(*part)) for part in parts]
-    kicked = []
-    for k, part in enumerate(parts):
-        last = k == len(parts) - 1
-        groups = mode_parts(local_modes, block) if last else [(0, local_modes)]
-        for (skip, _), values in zip(groups, physical(arrived[k], *part, groups)):
-            kicked.append((values, part, last, skip))
-    evolved, before, waiting = None, None, None
-    for values, part, last, skip in kicked:
-        if before is not None:
-            values = hold(values, [before])
-        fields = exchange(values)
-        if waiting is not None:
-            before = evolved = analysis(waiting[0], evolved, *waiting[1:])
-        waiting = (fields, *part, last, skip)
+    def across(pieces):
+        return [
+            lax.ppermute(piece, "hi", [(i, i ^ step) for i in range(outer)]) if step else piece
+            for step, piece in enumerate(pieces)
+        ]
+
+    def within(pieces):
+        return [
+            lax.ppermute(piece, ("comp", "lo"), [(i, i ^ turn) for i in range(group)])
+            if turn
+            else piece
+            for turn, piece in enumerate(pieces)
+        ]
+
+    def swap_order(pieces):
+        return [
+            jnp.stack([piece[i] for piece in pieces]) for i in range(pieces[0].shape[0])
+        ]
+
+    small, large = parts
+    all_modes = [(0, local_modes)]
+    sent = synthesis(*small, True, [])
+    synthesized = synthesis(*large, False, sent[:1])[0]
+    arrived = across(sent)
+    radial = exchange(hold(synthesized, arrived[1:]))
+    near = jnp.stack(within(swap_order(arrived)))
+    kicked = physical(near, *small, all_modes, True, [])[0]
+    near = within([kicked[turn] for turn in range(group)])
+
+    groups = mode_parts(local_modes, block)
+    kicked = physical(radial, *large, groups, False, near[1:])
+    sent = swap_order(near)
+    sent = sent[:1] + [hold(piece, [radial]) for piece in sent[1:]]
+    arrived = across(sent)
+
+    evolved, waiting, after = None, (arrived, *small, False, 0), arrived[1:]
+    for (skip, count), values in zip(groups, kicked):
+        fields = exchange(hold(values.reshape(-1, count, lanes), after))
+        evolved = analysis(waiting[0], evolved, *waiting[1:])
+        waiting, after = ([fields], *large, True, skip), [evolved]
     evolved = analysis(waiting[0], evolved, *waiting[1:])
     return evolved.reshape(1, local_modes, 2, planes, degrees)
 
 
 def solution(mesh):
-    in_specs = (P("comp", "mr", None, None, None), P("mr", None, None), P("mr"), P(), P(), P())
-    out_specs = P("comp", "mr", None, None, None)
+    components, width = mesh.shape["comp"], mesh.shape["mr"]
+    outer = math.gcd(width, 4)
+    split_mesh = Mesh(
+        mesh.devices.reshape(components, outer, width // outer), ("comp", "hi", "lo")
+    )
+    modes = ("hi", "lo")
+    in_specs = (P("comp", modes, None, None, None), P(modes, None, None), P(modes), P(), P(), P())
+    out_specs = P("comp", modes, None, None, None)
     return jax.shard_map(
-        on_device, mesh=mesh, in_specs=in_specs, out_specs=out_specs, check_vma=False
-    )
+        on_device, mesh=split_mesh, in_specs=in_specs, out_specs=out_specs, check_vma=False
+    )

time: 788 us -> 780 us (0.990)
  waiting for transfers between devices: 583 us -> 535 us
  starting transfers between devices: 21 us -> 51.3 us
    all_to_all x5 -> x3, waiting for transfers between devices: 583 us -> 360 us  [exchange(): return lax.all_to_all(value, axes, split_axis=0, concat_axis=0, tiled=True)]
    ppermute x0 -> x20, waiting for transfers between devices: none -> 175 us  [the longest x14 163 us: within(): lax.ppermute(piece, ('comp', 'lo'), [(i, i ^ turn) for i in range(group)])]
    ppermute x0 -> x20, starting transfers between devices: none -> 28.5 us  [the longest x14 18.5 us: within(): lax.ppermute(piece, ('comp', 'lo'), [(i, i ^ turn) for i in range(group)])]
    all_to_all x5 -> x3, starting transfers between devices: 21 us -> 22.8 us  [exchange(): return lax.all_to_all(value, axes, split_axis=0, concat_axis=0, tiled=True)]
  transfers between devices with their start and end apart: 5 -> 23, of which waited for: 5 -> 13; matrix products, arithmetic and copies ran while one was open for 2% -> 3% of each run, Pallas kernels for 18% -> 19%
where the time goes in v4:
time: 780 us
  waiting for transfers between devices  535 us (69%)
  Pallas kernels  165 us (21%)
  starting transfers between devices  51.3 us (7%)
  other arithmetic  14.1 us (2%)
  local copies, waits for them, and re-layouts  13.7 us (2%)
    all_to_all x3, waiting for transfers between devices, exchange(): return lax.all_to_all(value, axes, split_axis=0, concat_axis=0, tiled=True)  360 us
    ppermute x14, waiting for transfers between devices, within(): lax.ppermute(piece, ('comp', 'lo'), [(i, i ^ turn) for i in range(group)])  163 us
    pallas_call x2, Pallas kernels, physical(): pl.pallas_call(functools.partial(physical_kernel, relative, inner, len(co...  68.1 us
    pallas_call x3, Pallas kernels, analysis(): pl.pallas_call(functools.partial(analysis_kernel, skip, held is None, las...  52.6 us
    pallas_call x2, Pallas kernels, synthesis(): pl.pallas_call(functools.partial(synthesis_kernel, planes, outs), grid=(l...  44.5 us
    all_to_all x3, starting transfers between devices, exchange(): return lax.all_to_all(value, axes, split_axis=0, concat_axis=0, tiled=True)  22.8 us
    ppermute x14, starting transfers between devices, within(): lax.ppermute(piece, ('comp', 'lo'), [(i, i ^ turn) for i in range(group)])  18.5 us
  transfers between devices with their start and end apart: 23, of which 13 were waited for; matrix products, arithmetic and copies ran while one was open for 3% of the time, Pallas kernels for 19%

profile of v4, /device:TPU:0, one launch (start us, length us, event | category | flops | bytes accessed | tf_op | source)
XLA Modules:
  0.0 779.7 jit_solution(1734637373470321014)
XLA Ops:
  0.6 11.9 %synthesis.2 = (bf16[8,5,64,128]{3,2,1,0:T(8,128)(2,1)}, bf16[8,5,64,128]{3,2,1,0:T(8,128)(2,1)}, bf16[8,5,64,128]{3,2,1,0:T(8,128)(2,1)}, bf16[8,5,64,128]{3,2,1,0:T(8,128)(2,1)}) custom-call(s32[2]{0:T(128)} %pad_add_fusion.place_ref, s32[1]{0:T(128)} %bitcast.3.first_ref, s32[64]{0:T(128)} %cutoff_ref.9, f32[2,1024]{1,0:T(2,128)} %constant.60.clone.mode_ref, ...), custom_call_target="tpu_custom_call" | custom-call | flops 1342177280 | bytes 29884416 | tf_op jit(solution)/shard_map/synthesis/pallas_call | solution.py:358
  18.2 32.6 %synthesis.3.refs_0_ = bf16[864,64,128]{2,1,0:T(8,128)(2,1)} custom-call(s32[2]{0:T(128)} %pad_add_fusion.place_ref, s32[1]{0:T(128)} %bitcast.3.first_ref, s32[64]{0:T(128)} %cutoff_ref.9, f32[2,1024]{1,0:T(2,128)} %constant.60.clone.mode_ref, f32[2,512]{1,0:T(2,128)} %constant.61.clone.degree_ref, f32[1,64,2,64,512]{4,3,2,1,0:T(8,128)} %spectrum_ref.3, ...), custom_call_target="tpu_custom_call" | custom-call | flops 7247757312 | bytes 87556096 | tf_op jit(solution)/shard_map/synthesis/pallas_call | solution.py:358
  50.8 11.7 %collective-permute-done.1.refs_2_ = bf16[8,5,64,128]{3,2,1,0:T(8,128)(2,1)S(1)} collective-permute-done((bf16[8,5,64,128]{3,2,1,0:T(8,128)(2,1)}, bf16[8,5,64,128]{3,2,1,0:T(8,128)(2,1)S(1)}, u32[]{:S(2)}, u32[]{:S(2)}) %collective-permute-start.1) | collective-permute-done | bytes 655392 | tf_op jit(solution)/shard_map/ppermute | solution.py:495
  64.2 15.9 %all-to-all-start = ((bf16[864,64,128]{2,1,0:T(8,128)(2,1)}), bf16[864,64,128]{2,1,0:T(8,128)(2,1)}, u32[]{:S(2)}, u32[]{:S(2)}) async-start(bf16[864,64,128]{2,1,0:T(8,128)(2,1)} %hold.6), calls=%async_computation | async-start | bytes 28311552 | tf_op jit(solution)/shard_map/all_to_all | solution.py:491
  84.9 8.9 %multiply_convert_fusion.1 = (bf16[4,256,256]{2,1,0:T(8,128)(2,1)S(1)}, bf16[4,256,256]{2,1,0:T(8,128)(2,1)S(1)}, bf16[4,256,256]{2,1,0:T(8,128)(2,1)S(1)}, bf16[4,256,256]{2,1,0:T(8,128)(2,1)S(1)}) fusion(s32[4,256]{1,0:T(4,128)S(1)} %iota_add_fusion), kind=kLoop, calls=%fused_computation.15 | loop fusion | flops 9437184 | bytes 2101248 | tf_op jit(solution)/shard_map/convert_element_type | solution.py:27
  103.5 72.2 %collective-permute-done.4 = bf16[4,5,64,128]{3,2,1,0:T(8,128)(2,1)S(1)} collective-permute-done((bf16[4,5,64,128]{3,2,1,0:T(8,128)(2,1)S(1)}, bf16[4,5,64,128]{3,2,1,0:T(8,128)(2,1)S(1)}, u32[]{:S(2)}, u32[]{:S(2)}) %collective-permute-start.4) | collective-permute-done | bytes 327712 | tf_op jit(solution)/shard_map/ppermute | solution.py:501
  178.4 7.2 collective-permute-done.5
  185.7 3.8 collective-permute-done.6
  189.5 7.2 collective-permute-done.7
  196.7 17.2 %collective-permute-done.8 = bf16[4,5,64,128]{3,2,1,0:T(8,128)(2,1)S(1)} collective-permute-done((bf16[4,5,64,128]{3,2,1,0:T(8,128)(2,1)S(1)}, bf16[4,5,64,128]{3,2,1,0:T(8,128)(2,1)S(1)}, u32[]{:S(2)}, u32[]{:S(2)}) %collective-permute-start.8) | collective-permute-done | bytes 327712 | tf_op jit(solution)/shard_map/ppermute | solution.py:501
  214.0 18.6 %collective-permute-done.9 = bf16[4,5,64,128]{3,2,1,0:T(8,128)(2,1)S(1)} collective-permute-done((bf16[4,5,64,128]{3,2,1,0:T(8,128)(2,1)S(1)}, bf16[4,5,64,128]{3,2,1,0:T(8,128)(2,1)S(1)}, u32[]{:S(2)}, u32[]{:S(2)}) %collective-permute-start.9) | collective-permute-done | bytes 327712 | tf_op jit(solution)/shard_map/ppermute | solution.py:501
  234.1 12.3 %physical.2 = bf16[8,4,5,64,128]{4,3,2,1,0:T(8,128)(2,1)} custom-call(s32[2]{0:T(128)} %pad_add_fusion.place_ref, f32[5]{0:T(128)} %dynamic-slice_multiply_fusion.trap_ref, f32[5]{0:T(128)} %dynamic_slice.15.weight_ref, f32[2,128]{1,0:T(2,128)} %reshape.46.lanes_ref, bf16[4,256,512]{2,1,0:T(8,128)(2,1)} %get-tuple-element.92.table_ref, ...), custom_call_target="tpu_custom_call" | custom-call | flops 2684354560 | bytes 7340032 | tf_op jit(solution)/shard_map/physical/pallas_call | solution.py:405
  250.7 5.2 collective-permute-start.11
  260.3 28.8 %collective-permute-done.11.refs_1_ = bf16[4,5,64,128]{3,2,1,0:T(8,128)(2,1)S(1)} collective-permute-done((bf16[4,5,64,128]{3,2,1,0:T(8,128)(2,1)S(1)}, bf16[4,5,64,128]{3,2,1,0:T(8,128)(2,1)S(1)}, u32[]{:S(2)}, u32[]{:S(2)}) %collective-permute-start.11) | collective-permute-done | bytes 327712 | tf_op jit(solution)/shard_map/ppermute | solution.py:501
  289.1 5.7 collective-permute-done.12.refs_2_
  298.8 92.3 %all-to-all-done.refs_1_ = bf16[864,64,128]{2,1,0:T(8,128)(2,1)} async-done(((bf16[864,64,128]{2,1,0:T(8,128)(2,1)}), bf16[864,64,128]{2,1,0:T(8,128)(2,1)}, u32[]{:S(2)}, u32[]{:S(2)}) %all-to-all-start) | async-done | bytes 14155808 | tf_op jit(solution)/shard_map/all_to_all | solution.py:491
  391.2 4.3 collective-permute-start.19
  395.5 55.7 %physical.3 = (bf16[2,16,27,56,128]{4,3,2,1,0:T(8,128)(2,1)}, bf16[2,16,27,8,128]{4,3,2,1,0:T(8,128)(2,1)}) custom-call(s32[2]{0:T(128)} %pad_add_fusion.place_ref, f32[27]{0:T(128)} %dynamic-slice_multiply_fusion.1.trap_ref, f32[27]{0:T(128)} %dynamic_slice.13.weight_ref, f32[2,128]{1,0:T(2,128)} %reshape.46.lanes_ref, ...), custom_call_target="tpu_custom_call" | custom-call | flops 14495514624 | bytes 30408704 | tf_op jit(solution)/shard_map/physical/pallas_call | solution.py:405
  452.5 3.9 all-to-all-start.2
  456.5 11.3 %analysis.3.refs_1_.refs_2_ = f32[64,128,512]{2,1,0:T(8,128)} custom-call(s32[2]{0:T(128)S(1)} %copy-done.7, s32[64]{0:T(128)S(1)} %copy-done.6, bf16[8,5,64,128]{3,2,1,0:T(8,128)(2,1)S(1)} %get-tuple-element.63.refs_0_, bf16[8,5,64,128]{3,2,1,0:T(8,128)(2,1)S(1)} %copy-done.1, bf16[8,5,64,128]{3,2,1,0:T(8,128)(2,1)S(1)} %copy-done.3, ...), custom_call_target="tpu_custom_call" | custom-call | flops 1342177280 | bytes 46661632 | tf_op jit(solution)/shard_map/analysis/pallas_call | solution.py:472
  467.9 260.1 %all-to-all-done.2.refs_0_ = bf16[864,56,128]{2,1,0:T(8,128)(2,1)} async-done(((bf16[864,56,128]{2,1,0:T(8,128)(2,1)}), bf16[864,56,128]{2,1,0:T(8,128)(2,1)}, u32[]{:S(2)}, u32[]{:S(2)}) %all-to-all-start.2) | async-done | bytes 12386336 | tf_op jit(solution)/shard_map/all_to_all | solution.py:491
  730.9 35.1 %analysis.4.refs_2_ = f32[64,128,512]{2,1,0:T(8,128)} custom-call(s32[2]{0:T(128)S(1)} %copy-done.7, s32[64]{0:T(128)S(1)} %copy-done.6, bf16[864,56,128]{2,1,0:T(8,128)(2,1)} %all-to-all-done.2.refs_0_, bf16[64,1024,512]{2,1,0:T(8,128)(2,1)} %refs_1_.3, f32[64,128,512]{2,1,0:T(8,128)} %analysis.3.refs_1_.refs_2_), custom_call_target="tpu_custom_call", output_to_operand_aliasing={{}: (4, {})} | custom-call | flops 6341787648 | bytes 91291648 | tf_op jit(solution)/shard_map/analysis/pallas_call | solution.py:472
  766.0 7.6 all-to-all-done.1.refs_0_
  773.6 6.1 analysis.5
  (130 shorter events, 43.6 us)
Async XLA Ops:
  12.6 38.2 %collective-permute-start = (bf16[8,5,64,128]{3,2,1,0:T(8,128)(2,1)}, bf16[8,5,64,128]{3,2,1,0:T(8,128)(2,1)S(1)}, u32[]{:S(2)}, u32[]{:S(2)}) collective-permute-start(bf16[8,5,64,128]{3,2,1,0:T(8,128)(2,1)} %get-tuple-element.12), channel_id=1, source_target_pairs={{0,4},{4,0},{8,12},{12,8},{1,5},{5,1},{9,13},{13,9},{2,6},{6,2},{1... | collective-permute-start | bytes 1966088 | tf_op jit(solution)/shard_map/ppermute | solution.py:495
  15.6 46.9 %collective-permute-start.1 = (bf16[8,5,64,128]{3,2,1,0:T(8,128)(2,1)}, bf16[8,5,64,128]{3,2,1,0:T(8,128)(2,1)S(1)}, u32[]{:S(2)}, u32[]{:S(2)}) collective-permute-start(bf16[8,5,64,128]{3,2,1,0:T(8,128)(2,1)} %get-tuple-element.13), channel_id=1, source_target_pairs={{0,8},{4,12},{8,0},{12,4},{1,9},{5,13},{9,1},{13,5},{2,10},{6,14},... | collective-permute-start | bytes 1966088 | tf_op jit(solution)/shard_map/ppermute | solution.py:495
  18.2 44.3 %collective-permute-start.2 = (bf16[8,5,64,128]{3,2,1,0:T(8,128)(2,1)}, bf16[8,5,64,128]{3,2,1,0:T(8,128)(2,1)S(1)}, u32[]{:S(2)}, u32[]{:S(2)}) collective-permute-start(bf16[8,5,64,128]{3,2,1,0:T(8,128)(2,1)} %get-tuple-element.14), channel_id=1, source_target_pairs={{0,12},{4,8},{8,4},{12,0},{1,13},{5,9},{9,5},{13,1},{2,14},{6,10},... | collective-permute-start | bytes 1966088 | tf_op jit(solution)/shard_map/ppermute | solution.py:495
  64.2 326.9 %all-to-all-start = ((bf16[864,64,128]{2,1,0:T(8,128)(2,1)}), bf16[864,64,128]{2,1,0:T(8,128)(2,1)}, u32[]{:S(2)}, u32[]{:S(2)}) async-start(bf16[864,64,128]{2,1,0:T(8,128)(2,1)} %hold.6), calls=%async_computation | async-start | bytes 28311552 | tf_op jit(solution)/shard_map/all_to_all | solution.py:491
  96.7 4.2 collective-permute-start.3
  96.8 78.9 %collective-permute-start.4 = (bf16[4,5,64,128]{3,2,1,0:T(8,128)(2,1)S(1)}, bf16[4,5,64,128]{3,2,1,0:T(8,128)(2,1)S(1)}, u32[]{:S(2)}, u32[]{:S(2)}) collective-permute-start(bf16[4,5,64,128]{3,2,1,0:T(8,128)(2,1)S(1)} %pad_maximum_fusion.3), channel_id=1, source_target_pairs={{0,2},{1,3},{2,0},{3,1},{16,18},{17,19},{18,16},{19,17},{4,6},{5,7... | collective-permute-start | bytes 983048 | tf_op jit(solution)/shard_map/ppermute | solution.py:501
  98.6 87.0 %collective-permute-start.5 = (bf16[4,5,64,128]{3,2,1,0:T(8,128)(2,1)S(1)}, bf16[4,5,64,128]{3,2,1,0:T(8,128)(2,1)S(1)}, u32[]{:S(2)}, u32[]{:S(2)}) collective-permute-start(bf16[4,5,64,128]{3,2,1,0:T(8,128)(2,1)S(1)} %pad_maximum_fusion.4), channel_id=1, source_target_pairs={{0,3},{1,2},{2,1},{3,0},{16,19},{17,18},{18,17},{19,16},{4,7},{5,6... | collective-permute-start | bytes 983048 | tf_op jit(solution)/shard_map/ppermute | solution.py:501
  98.9 90.6 %collective-permute-start.6 = (bf16[4,5,64,128]{3,2,1,0:T(8,128)(2,1)S(1)}, bf16[4,5,64,128]{3,2,1,0:T(8,128)(2,1)S(1)}, u32[]{:S(2)}, u32[]{:S(2)}) collective-permute-start(bf16[4,5,64,128]{3,2,1,0:T(8,128)(2,1)S(1)} %pad_maximum_fusion.5), channel_id=1, source_target_pairs={{0,16},{1,17},{2,18},{3,19},{16,0},{17,1},{18,2},{19,3},{4,20},{5,... | collective-permute-start | bytes 983048 | tf_op jit(solution)/shard_map/ppermute | solution.py:501
  100.5 96.2 %collective-permute-start.7 = (bf16[4,5,64,128]{3,2,1,0:T(8,128)(2,1)S(1)}, bf16[4,5,64,128]{3,2,1,0:T(8,128)(2,1)S(1)}, u32[]{:S(2)}, u32[]{:S(2)}) collective-permute-start(bf16[4,5,64,128]{3,2,1,0:T(8,128)(2,1)S(1)} %pad_maximum_fusion.6), channel_id=1, source_target_pairs={{0,17},{1,16},{2,19},{3,18},{16,1},{17,0},{18,3},{19,2},{4,21},{5,... | collective-permute-start | bytes 983048 | tf_op jit(solution)/shard_map/ppermute | solution.py:501
  100.8 113.1 %collective-permute-start.8 = (bf16[4,5,64,128]{3,2,1,0:T(8,128)(2,1)S(1)}, bf16[4,5,64,128]{3,2,1,0:T(8,128)(2,1)S(1)}, u32[]{:S(2)}, u32[]{:S(2)}) collective-permute-start(bf16[4,5,64,128]{3,2,1,0:T(8,128)(2,1)S(1)} %pad_maximum_fusion.7), channel_id=1, source_target_pairs={{0,18},{1,19},{2,16},{3,17},{16,2},{17,3},{18,0},{19,1},{4,22},{5,... | collective-permute-start | bytes 983048 | tf_op jit(solution)/shard_map/ppermute | solution.py:501
  175.7 56.8 %collective-permute-start.9 = (bf16[4,5,64,128]{3,2,1,0:T(8,128)(2,1)S(1)}, bf16[4,5,64,128]{3,2,1,0:T(8,128)(2,1)S(1)}, u32[]{:S(2)}, u32[]{:S(2)}) collective-permute-start(bf16[4,5,64,128]{3,2,1,0:T(8,128)(2,1)S(1)} %pad_maximum_fusion.8), channel_id=1, source_target_pairs={{0,19},{1,18},{2,17},{3,16},{16,3},{17,2},{18,1},{19,0},{4,23},{5,... | collective-permute-start | bytes 983048 | tf_op jit(solution)/shard_map/ppermute | solution.py:501
  248.5 10.7 %collective-permute-start.10 = (bf16[4,5,64,128]{3,2,1,0:T(8,128)(2,1)S(1)}, bf16[4,5,64,128]{3,2,1,0:T(8,128)(2,1)S(1)}, u32[]{:S(2)}, u32[]{:S(2)}) collective-permute-start(bf16[4,5,64,128]{3,2,1,0:T(8,128)(2,1)S(1)} %get-tuple-element.27), channel_id=1, source_target_pairs={{0,1},{1,0},{2,3},{3,2},{16,17},{17,16},{18,19},{19,18},{4,5},{5,4... | collective-permute-start | bytes 983048 | tf_op jit(solution)/shard_map/ppermute | solution.py:501
  250.7 38.4 %collective-permute-start.11 = (bf16[4,5,64,128]{3,2,1,0:T(8,128)(2,1)S(1)}, bf16[4,5,64,128]{3,2,1,0:T(8,128)(2,1)S(1)}, u32[]{:S(2)}, u32[]{:S(2)}) collective-permute-start(bf16[4,5,64,128]{3,2,1,0:T(8,128)(2,1)S(1)} %get-tuple-element.26), channel_id=1, source_target_pairs={{0,2},{1,3},{2,0},{3,1},{16,18},{17,19},{18,16},{19,17},{4,6},{5,7... | collective-permute-start | bytes 983048 | tf_op jit(solution)/shard_map/ppermute | solution.py:501
  256.8 40.9 %collective-permute-start.16 = (bf16[4,5,64,128]{3,2,1,0:T(8,128)(2,1)S(1)}, bf16[4,5,64,128]{3,2,1,0:T(8,128)(2,1)S(1)}, u32[]{:S(2)}, u32[]{:S(2)}) collective-permute-start(bf16[4,5,64,128]{3,2,1,0:T(8,128)(2,1)S(1)} %get-tuple-element.21), channel_id=1, source_target_pairs={{0,19},{1,18},{2,17},{3,16},{16,3},{17,2},{18,1},{19,0},{4,23},{5,... | collective-permute-start | bytes 983048 | tf_op jit(solution)/shard_map/ppermute | solution.py:501
  256.9 40.8 %collective-permute-start.15 = (bf16[4,5,64,128]{3,2,1,0:T(8,128)(2,1)S(1)}, bf16[4,5,64,128]{3,2,1,0:T(8,128)(2,1)S(1)}, u32[]{:S(2)}, u32[]{:S(2)}) collective-permute-start(bf16[4,5,64,128]{3,2,1,0:T(8,128)(2,1)S(1)} %get-tuple-element.22), channel_id=1, source_target_pairs={{0,18},{1,19},{2,16},{3,17},{16,2},{17,3},{18,0},{19,1},{4,22},{5,... | collective-permute-start | bytes 983048 | tf_op jit(solution)/shard_map/ppermute | solution.py:501
  259.2 38.4 %collective-permute-start.14 = (bf16[4,5,64,128]{3,2,1,0:T(8,128)(2,1)S(1)}, bf16[4,5,64,128]{3,2,1,0:T(8,128)(2,1)S(1)}, u32[]{:S(2)}, u32[]{:S(2)}) collective-permute-start(bf16[4,5,64,128]{3,2,1,0:T(8,128)(2,1)S(1)} %get-tuple-element.23), channel_id=1, source_target_pairs={{0,17},{1,16},{2,19},{3,18},{16,1},{17,0},{18,3},{19,2},{4,21},{5,... | collective-permute-start | bytes 983048 | tf_op jit(solution)/shard_map/ppermute | solution.py:501
  259.2 35.7 %collective-permute-start.12 = (bf16[4,5,64,128]{3,2,1,0:T(8,128)(2,1)S(1)}, bf16[4,5,64,128]{3,2,1,0:T(8,128)(2,1)S(1)}, u32[]{:S(2)}, u32[]{:S(2)}) collective-permute-start(bf16[4,5,64,128]{3,2,1,0:T(8,128)(2,1)S(1)} %get-tuple-element.25), channel_id=1, source_target_pairs={{0,3},{1,2},{2,1},{3,0},{16,19},{17,18},{18,17},{19,16},{4,7},{5,6... | collective-permute-start | bytes 983048 | tf_op jit(solution)/shard_map/ppermute | solution.py:501
  289.1 8.5 %collective-permute-start.13 = (bf16[4,5,64,128]{3,2,1,0:T(8,128)(2,1)S(1)}, bf16[4,5,64,128]{3,2,1,0:T(8,128)(2,1)S(1)}, u32[]{:S(2)}, u32[]{:S(2)}) collective-permute-start(bf16[4,5,64,128]{3,2,1,0:T(8,128)(2,1)S(1)} %get-tuple-element.24), channel_id=1, source_target_pairs={{0,16},{1,17},{2,18},{3,19},{16,0},{17,1},{18,2},{19,3},{4,20},{5,... | collective-permute-start | bytes 983048 | tf_op jit(solution)/shard_map/ppermute | solution.py:501
  298.7 92.3 %copy-start.17 = (bf16[8,5,64,128]{3,2,1,0:T(8,128)(2,1)}, bf16[8,5,64,128]{3,2,1,0:T(8,128)(2,1)S(1)}, u32[]{:S(2)}) copy-start(bf16[8,5,64,128]{3,2,1,0:T(8,128)(2,1)S(1)} %get-tuple-element.62.refs_0_) | copy-start | bytes 1966084
  391.1 60.2 %collective-permute-start.17 = (bf16[8,5,64,128]{3,2,1,0:T(8,128)(2,1)}, bf16[8,5,64,128]{3,2,1,0:T(8,128)(2,1)S(1)}, u32[]{:S(2)}, u32[]{:S(2)}) collective-permute-start(bf16[8,5,64,128]{3,2,1,0:T(8,128)(2,1)} %hold.7), channel_id=1, source_target_pairs={{0,4},{4,0},{8,12},{12,8},{1,5},{5,1},{9,13},{13,9},{2,6},{6,2},{1... | collective-permute-start | bytes 1966088 | tf_op jit(solution)/shard_map/ppermute | solution.py:495
  391.2 60.1 %collective-permute-start.18 = (bf16[8,5,64,128]{3,2,1,0:T(8,128)(2,1)}, bf16[8,5,64,128]{3,2,1,0:T(8,128)(2,1)S(1)}, u32[]{:S(2)}, u32[]{:S(2)}) collective-permute-start(bf16[8,5,64,128]{3,2,1,0:T(8,128)(2,1)} %hold.8), channel_id=1, source_target_pairs={{0,8},{4,12},{8,0},{12,4},{1,9},{5,13},{9,1},{13,5},{2,10},{6,14},... | collective-permute-start | bytes 1966088 | tf_op jit(solution)/shard_map/ppermute | solution.py:495
  391.2 60.1 %collective-permute-start.19 = (bf16[8,5,64,128]{3,2,1,0:T(8,128)(2,1)}, bf16[8,5,64,128]{3,2,1,0:T(8,128)(2,1)S(1)}, u32[]{:S(2)}, u32[]{:S(2)}) collective-permute-start(bf16[8,5,64,128]{3,2,1,0:T(8,128)(2,1)} %hold.9), channel_id=1, source_target_pairs={{0,12},{4,8},{8,4},{12,0},{1,13},{5,9},{9,5},{13,1},{2,14},{6,10},... | collective-permute-start | bytes 1966088 | tf_op jit(solution)/shard_map/ppermute | solution.py:495
  452.5 275.4 %all-to-all-start.2 = ((bf16[864,56,128]{2,1,0:T(8,128)(2,1)}), bf16[864,56,128]{2,1,0:T(8,128)(2,1)}, u32[]{:S(2)}, u32[]{:S(2)}) async-start(bf16[864,56,128]{2,1,0:T(8,128)(2,1)} %hold.11), calls=%async_computation.2 | async-start | bytes 24772608 | tf_op jit(solution)/shard_map/all_to_all | solution.py:491
  727.9 45.7 %all-to-all-start.1 = ((bf16[864,8,128]{2,1,0:T(8,128)(2,1)}), bf16[864,8,128]{2,1,0:T(8,128)(2,1)S(1)}, u32[]{:S(2)}, u32[]{:S(2)}) async-start(bf16[864,8,128]{2,1,0:T(8,128)(2,1)} %hold.10), calls=%async_computation.1 | async-start | bytes 3538944 | tf_op jit(solution)/shard_map/all_to_all | solution.py:491
  (26 other events, 301.2 us)

commit v5 on v4

--- a/solution.py
+++ b/solution.py
@@ -80,10 +80,14 @@
     return pltpu.roll(value, value.shape[-1] // 2, value.ndim - 1)
 
 
-def relative_rows(place_ref, outer, group, size):
+def relative_rows(place_ref, outer, group, size, inner=None):
     for step in range(outer):
         for turn in range(group):
-            device = (place_ref[0] ^ step) * group + (place_ref[1] ^ turn)
+            outer_at, group_at = place_ref[0] ^ step, place_ref[1] ^ turn
+            device = outer_at * group + group_at
+            if inner is not None:
+                device = lax.div(group_at, inner) * outer + outer_at
+                device = device * inner + lax.rem(group_at, inner)
             yield step, turn, pl.multiple_of(device * size, size)
 
 
@@ -142,8 +146,8 @@
 
 def physical_kernel(
     relative,
+    relative_outs,
     inner,
-    outs,
     place_ref,
     trap_ref,
     weight_ref,
@@ -153,18 +157,18 @@
     x_ref,
     *refs,
 ):
-    out_refs, (work, kick) = refs[-outs - 2 : -2], refs[-2:]
+    out_refs, (work, kick) = refs[-len(relative_outs) - 2 : -2], refs[-2:]
     row = pl.program_id(0)
     local_modes, lanes = x_ref.shape[3:]
     quarter = inner * local_modes
 
-    def block_at(component, j, i):
-        if relative:
+    def block_at(component, j, i, by_distance):
+        if by_distance:
             return place_ref[1] ^ (component * inner + i), place_ref[0] ^ j
         return component, j * inner + i
 
     def field(component, j):
-        pieces = [x_ref[(*block_at(component, j, i), 0)] for i in range(inner)]
+        pieces = [x_ref[(*block_at(component, j, i, relative), 0)] for i in range(inner)]
         return jnp.concatenate(pieces, axis=0).astype(jnp.float32)
 
     first = lax.broadcasted_iota(jnp.int32, (quarter, lanes), 1) < lanes // 2
@@ -233,15 +237,14 @@
         for component, value in enumerate(values):
             for i in range(inner):
                 skip = i * local_modes
-                for out_ref in out_refs:
+                for out_ref, by_distance in zip(out_refs, relative_outs):
                     count = out_ref.shape[3]
-                    out_ref[(*block_at(component, j, i), 0)] = value[skip : skip + count].astype(
-                        jnp.bfloat16
-                    )
+                    at = (*block_at(component, j, i, by_distance), 0)
+                    out_ref[at] = value[skip : skip + count].astype(jnp.bfloat16)
                     skip += count
 
 
-def analysis_kernel(skip, first, last, ins, place_ref, cutoff_ref, *refs):
+def analysis_kernel(skip, first, last, ins, inner, place_ref, cutoff_ref, *refs):
     fields_refs, basis_ref, held_ref, (out_ref, stage) = (
         refs[:ins],
         refs[ins],
@@ -256,7 +259,7 @@
     else:
         group, rows = fields_refs[0].shape[:2]
         size = rows * block
-        for distance, turn, start in relative_rows(place_ref, ins, group, size):
+        for distance, turn, start in relative_rows(place_ref, ins, group, size, inner):
             piece = fields_refs[distance][turn].astype(jnp.float32)
             stage[pl.ds(start, size), :] = piece.reshape(size, stage.shape[1])
 
@@ -386,26 +389,28 @@
             place, first_mode, cutoff, mode_phases, degree_phases, spectrum, radial_basis, *after
         )
 
-    def physical(radial, start, rows, groups, relative, after):
+    def physical(radial, start, rows, groups, relative, relative_outs, after):
         me = lax.axis_index(("hi", "comp", "lo") if relative else axes)
         first_radius = start * device_count + me * rows
         trap = lax.dynamic_slice_in_dim(trap_potential, first_radius, rows) * to_turns
         weight = lax.dynamic_slice_in_dim(weights, first_radius, rows)
         quarter = mode_total // 4
-        lead = (group, outer) if relative else (components, mode_width)
-
-        def shape(count):
-            return (*lead, rows, count, lanes)
-
-        def spec(count):
-            return pl.BlockSpec((*lead, 1, count, lanes), lambda i: (0, 0, i, 0, 0))
-
-        counts = [count for _, count in groups]
+        leads = {True: (group, outer), False: (components, mode_width)}
+
+        def shape(count, by_distance):
+            return (*leads[by_distance], rows, count, lanes)
+
+        def spec(count, by_distance):
+            return pl.BlockSpec(
+                (*leads[by_distance], 1, count, lanes), lambda i: (0, 0, i, 0, 0)
+            )
+
+        outs = [(count, flag) for (_, count), flag in zip(groups, relative_outs)]
         table_spec = pl.BlockSpec((4, quarter, 2 * quarter), lambda i: (0, 0, 0))
         return pl.pallas_call(
-            functools.partial(physical_kernel, relative, inner, len(counts)),
+            functools.partial(physical_kernel, relative, relative_outs, inner),
             grid=(rows,),
-            out_shape=[jax.ShapeDtypeStruct(shape(count), jnp.bfloat16) for count in counts],
+            out_shape=[jax.ShapeDtypeStruct(shape(*out), jnp.bfloat16) for out in outs],
             in_specs=[
                 in_smem,
                 in_smem,
@@ -413,10 +418,10 @@
                 pl.BlockSpec((2, lanes), lambda i: (0, 0)),
                 table_spec,
                 table_spec,
-                spec(local_modes),
+                spec(local_modes, relative),
                 *[anywhere] * len(after),
             ],
-            out_specs=[spec(count) for count in counts],
+            out_specs=[spec(*out) for out in outs],
             scratch_shapes=[
                 pltpu.VMEM((4, 2 * quarter, 2 * lanes), jnp.bfloat16),
                 pltpu.VMEM((4, 2 * quarter, 2 * lanes), jnp.bfloat16),
@@ -435,11 +440,11 @@
             lane_strength,
             table,
             back_table,
-            radial.reshape(shape(local_modes)),
+            radial.reshape(shape(local_modes, relative)),
             *after,
         )
 
-    def analysis(fields, held, start, rows, last, skip):
+    def analysis(fields, held, start, rows, last, skip, inner_order=None, after=()):
         relative = len(fields) > 1
         radii, count = rows * device_count, fields[0].shape[-2]
         block = math.gcd(count, MODE_BLOCK)
@@ -469,14 +474,19 @@
         if held is not None:
             operands.append(held)
             in_specs.append(out_spec)
+        aliases = {} if held is None else {len(operands) - 1: 0}
+        operands += after
+        in_specs += [anywhere] * len(after)
         return pl.pallas_call(
-            functools.partial(analysis_kernel, skip, held is None, last, len(fields)),
+            functools.partial(
+                analysis_kernel, skip, held is None, last, len(fields), inner_order
+            ),
             grid=(count // block, steps),
             out_shape=jax.ShapeDtypeStruct((local_modes, lanes, degrees), jnp.float32),
             in_specs=in_specs,
             out_specs=out_spec,
             scratch_shapes=[pltpu.VMEM((part * block, lanes), jnp.float32)],
-            input_output_aliases={} if held is None else {len(operands) - 1: 0},
+            input_output_aliases=aliases,
             compiler_params=params(2, 50),
             cost_estimate=pl.CostEstimate(
                 flops=2 * count * radii * degrees * lanes,
@@ -516,21 +526,25 @@
     arrived = across(sent)
     radial = exchange(hold(synthesized, arrived[1:]))
     near = jnp.stack(within(swap_order(arrived)))
-    kicked = physical(near, *small, all_modes, True, [])[0]
+    kicked = physical(near, *small, all_modes, True, [True], [])[0]
     near = within([kicked[turn] for turn in range(group)])
 
     groups = mode_parts(local_modes, block)
-    kicked = physical(radial, *large, groups, False, near[1:])
+    kicked = physical(radial, *large, groups, False, [False, True][: len(groups)], near[1:])
     sent = swap_order(near)
     sent = sent[:1] + [hold(piece, [radial]) for piece in sent[1:]]
     arrived = across(sent)
 
-    evolved, waiting, after = None, (arrived, *small, False, 0), arrived[1:]
-    for (skip, count), values in zip(groups, kicked):
-        fields = exchange(hold(values.reshape(-1, count, lanes), after))
-        evolved = analysis(waiting[0], evolved, *waiting[1:])
-        waiting, after = ([fields], *large, True, skip), [evolved]
-    evolved = analysis(waiting[0], evolved, *waiting[1:])
+    late = []
+    if len(groups) > 1:
+        late = within([kicked[1][turn] for turn in range(group)])
+    fields = exchange(hold(kicked[0].reshape(-1, groups[0][1], lanes), arrived[1:]))
+    evolved = analysis(arrived, None, *small, False, 0, None, late[1:])
+    evolved = analysis([fields], evolved, *large, True, 0)
+    if len(groups) > 1:
+        sent = swap_order(late)
+        arrived = across(sent[:1] + [hold(piece, [fields]) for piece in sent[1:]])
+        evolved = analysis(arrived, evolved, *large, True, groups[1][0], inner)
     return evolved.reshape(1, local_modes, 2, planes, degrees)
 
 

time: 780 us -> 775 us (level)
  waiting for transfers between devices: 535 us -> 517 us
  starting transfers between devices: 51.3 us -> 60.5 us
    all_to_all x3 -> x2, waiting for transfers between devices: 360 us -> 229 us  [exchange(): return lax.all_to_all(value, axes, split_axis=0, concat_axis=0, tiled=True)]
    ppermute x14 -> x21, waiting for transfers between devices: 163 us -> 276 us  [within(): lax.ppermute(piece, ('comp', 'lo'), [(i, i ^ turn) for i in range(group)])]
    ppermute x14 -> x21, starting transfers between devices: 18.5 us -> 26.1 us  [within(): lax.ppermute(piece, ('comp', 'lo'), [(i, i ^ turn) for i in range(group)])]
    all_to_all x3 -> x2, starting transfers between devices: 22.8 us -> 20 us  [exchange(): return lax.all_to_all(value, axes, split_axis=0, concat_axis=0, tiled=True)]
  transfers between devices with their start and end apart: 23 -> 32, of which waited for: 13 -> 16; matrix products, arithmetic and copies ran while one was open for 3% -> 3% of each run, Pallas kernels for 19% -> 19%
where the time goes in v5:
time: 775 us; the launch traced here: 774 us
  waiting for transfers between devices  517 us (67%)
  Pallas kernels  166 us (21%)
  starting transfers between devices  60.5 us (8%)
  local copies, waits for them, and re-layouts  15.5 us (2%)
  other arithmetic  14.1 us (2%)
    ppermute x21, waiting for transfers between devices, within(): lax.ppermute(piece, ('comp', 'lo'), [(i, i ^ turn) for i in range(group)])  276 us
    all_to_all x2, waiting for transfers between devices, exchange(): return lax.all_to_all(value, axes, split_axis=0, concat_axis=0, tiled=True)  229 us
    pallas_call x2, Pallas kernels, physical(): pl.pallas_call(functools.partial(physical_kernel, relative, relative_outs...  68.2 us
    pallas_call x3, Pallas kernels, analysis(): pl.pallas_call(functools.partial(analysis_kernel, skip, held is None, las...  53.4 us
    pallas_call x2, Pallas kernels, synthesis(): pl.pallas_call(functools.partial(synthesis_kernel, planes, outs), grid=(l...  44.5 us
    ppermute x21, starting transfers between devices, within(): lax.ppermute(piece, ('comp', 'lo'), [(i, i ^ turn) for i in range(group)])  26.1 us
    all_to_all x2, starting transfers between devices, exchange(): return lax.all_to_all(value, axes, split_axis=0, concat_axis=0, tiled=True)  20 us
  transfers between devices with their start and end apart: 32, of which 16 were waited for; matrix products, arithmetic and copies ran while one was open for 3% of the time, Pallas kernels for 19%

profile of v5, /device:TPU:0, one launch (start us, length us, event | category | flops | bytes accessed | tf_op | source)
XLA Modules:
  0.0 774.0 jit_solution(10209428890591199734)
XLA Ops:
  0.7 11.9 %synthesis.2 = (bf16[8,5,64,128]{3,2,1,0:T(8,128)(2,1)}, bf16[8,5,64,128]{3,2,1,0:T(8,128)(2,1)}, bf16[8,5,64,128]{3,2,1,0:T(8,128)(2,1)}, bf16[8,5,64,128]{3,2,1,0:T(8,128)(2,1)}) custom-call(s32[2]{0:T(128)} %pad_add_fusion.place_ref, s32[1]{0:T(128)} %bitcast.3.first_ref, s32[64]{0:T(128)} %cutoff_ref.9, f32[2,1024]{1,0:T(2,128)} %constant.60.clone.mode_ref, ...), custom_call_target="tpu_custom_call" | custom-call | flops 1342177280 | bytes 29884416 | tf_op jit(solution)/shard_map/synthesis/pallas_call | solution.py:361
  18.2 32.6 %synthesis.3.refs_0_ = bf16[864,64,128]{2,1,0:T(8,128)(2,1)} custom-call(s32[2]{0:T(128)} %pad_add_fusion.place_ref, s32[1]{0:T(128)} %bitcast.3.first_ref, s32[64]{0:T(128)} %cutoff_ref.9, f32[2,1024]{1,0:T(2,128)} %constant.60.clone.mode_ref, f32[2,512]{1,0:T(2,128)} %constant.61.clone.degree_ref, f32[1,64,2,64,512]{4,3,2,1,0:T(8,128)} %spectrum_ref.3, ...), custom_call_target="tpu_custom_call" | custom-call | flops 7247757312 | bytes 87556096 | tf_op jit(solution)/shard_map/synthesis/pallas_call | solution.py:361
  50.8 11.7 %collective-permute-done.1.refs_2_ = bf16[8,5,64,128]{3,2,1,0:T(8,128)(2,1)S(1)} collective-permute-done((bf16[8,5,64,128]{3,2,1,0:T(8,128)(2,1)}, bf16[8,5,64,128]{3,2,1,0:T(8,128)(2,1)S(1)}, u32[]{:S(2)}, u32[]{:S(2)}) %collective-permute-start.1) | collective-permute-done | bytes 655392 | tf_op jit(solution)/shard_map/ppermute | solution.py:505
  64.2 15.9 %all-to-all-start = ((bf16[864,64,128]{2,1,0:T(8,128)(2,1)}), bf16[864,64,128]{2,1,0:T(8,128)(2,1)}, u32[]{:S(2)}, u32[]{:S(2)}) async-start(bf16[864,64,128]{2,1,0:T(8,128)(2,1)} %hold.8), calls=%async_computation | async-start | bytes 28311552 | tf_op jit(solution)/shard_map/all_to_all | solution.py:501
  85.0 8.9 %multiply_convert_fusion.1 = (bf16[4,256,256]{2,1,0:T(8,128)(2,1)S(1)}, bf16[4,256,256]{2,1,0:T(8,128)(2,1)S(1)}, bf16[4,256,256]{2,1,0:T(8,128)(2,1)S(1)}, bf16[4,256,256]{2,1,0:T(8,128)(2,1)S(1)}) fusion(s32[4,256]{1,0:T(4,128)S(1)} %iota_add_fusion), kind=kLoop, calls=%fused_computation.15 | loop fusion | flops 9437184 | bytes 2101248 | tf_op jit(solution)/shard_map/convert_element_type | solution.py:27
  103.6 72.1 %collective-permute-done.4 = bf16[4,5,64,128]{3,2,1,0:T(8,128)(2,1)S(1)} collective-permute-done((bf16[4,5,64,128]{3,2,1,0:T(8,128)(2,1)S(1)}, bf16[4,5,64,128]{3,2,1,0:T(8,128)(2,1)S(1)}, u32[]{:S(2)}, u32[]{:S(2)}) %collective-permute-start.4) | collective-permute-done | bytes 327712 | tf_op jit(solution)/shard_map/ppermute | solution.py:511
  178.4 7.2 collective-permute-done.5
  189.5 7.2 collective-permute-done.7
  196.8 17.2 %collective-permute-done.8 = bf16[4,5,64,128]{3,2,1,0:T(8,128)(2,1)S(1)} collective-permute-done((bf16[4,5,64,128]{3,2,1,0:T(8,128)(2,1)S(1)}, bf16[4,5,64,128]{3,2,1,0:T(8,128)(2,1)S(1)}, u32[]{:S(2)}, u32[]{:S(2)}) %collective-permute-start.8) | collective-permute-done | bytes 327712 | tf_op jit(solution)/shard_map/ppermute | solution.py:511
  214.0 18.6 %collective-permute-done.9 = bf16[4,5,64,128]{3,2,1,0:T(8,128)(2,1)S(1)} collective-permute-done((bf16[4,5,64,128]{3,2,1,0:T(8,128)(2,1)S(1)}, bf16[4,5,64,128]{3,2,1,0:T(8,128)(2,1)S(1)}, u32[]{:S(2)}, u32[]{:S(2)}) %collective-permute-start.9) | collective-permute-done | bytes 327712 | tf_op jit(solution)/shard_map/ppermute | solution.py:511
  234.1 12.4 %physical.2 = bf16[8,4,5,64,128]{4,3,2,1,0:T(8,128)(2,1)} custom-call(s32[2]{0:T(128)} %pad_add_fusion.place_ref, f32[5]{0:T(128)} %dynamic-slice_multiply_fusion.trap_ref, f32[5]{0:T(128)} %dynamic_slice.15.weight_ref, f32[2,128]{1,0:T(2,128)} %reshape.47.lanes_ref, bf16[4,256,512]{2,1,0:T(8,128)(2,1)} %get-tuple-element.131.table_ref, ...), custom_call_target="tpu_custom_call" | custom-call | flops 2684354560 | bytes 7340032 | tf_op jit(solution)/shard_map/physical/pallas_call | solution.py:410
  250.7 5.2 collective-permute-start.11
  260.3 28.8 %collective-permute-done.11.refs_1_ = bf16[4,5,64,128]{3,2,1,0:T(8,128)(2,1)S(1)} collective-permute-done((bf16[4,5,64,128]{3,2,1,0:T(8,128)(2,1)S(1)}, bf16[4,5,64,128]{3,2,1,0:T(8,128)(2,1)S(1)}, u32[]{:S(2)}, u32[]{:S(2)}) %collective-permute-start.11) | collective-permute-done | bytes 327712 | tf_op jit(solution)/shard_map/ppermute | solution.py:511
  289.1 5.7 collective-permute-done.12.refs_2_
  298.7 92.3 %all-to-all-done.refs_1_ = bf16[864,64,128]{2,1,0:T(8,128)(2,1)} async-done(((bf16[864,64,128]{2,1,0:T(8,128)(2,1)}), bf16[864,64,128]{2,1,0:T(8,128)(2,1)}, u32[]{:S(2)}, u32[]{:S(2)}) %all-to-all-start) | async-done | bytes 14155808 | tf_op jit(solution)/shard_map/all_to_all | solution.py:501
  395.5 55.8 %physical.3 = (bf16[2,16,27,56,128]{4,3,2,1,0:T(8,128)(2,1)}, bf16[8,4,27,8,128]{4,3,2,1,0:T(8,128)(2,1)}) custom-call(s32[2]{0:T(128)} %pad_add_fusion.place_ref, f32[27]{0:T(128)} %dynamic-slice_multiply_fusion.1.trap_ref, f32[27]{0:T(128)} %dynamic_slice.13.weight_ref, f32[2,128]{1,0:T(2,128)} %reshape.47.lanes_ref, ...), custom_call_target="tpu_custom_call" | custom-call | flops 14495514624 | bytes 30408704 | tf_op jit(solution)/shard_map/physical/pallas_call | solution.py:410
  464.7 72.8 %collective-permute-done.18.refs_6_ = bf16[4,27,8,128]{3,2,1,0:T(8,128)(2,1)S(1)} collective-permute-done((bf16[4,27,8,128]{3,2,1,0:T(8,128)(2,1)S(1)}, bf16[4,27,8,128]{3,2,1,0:T(8,128)(2,1)S(1)}, u32[]{:S(2)}, u32[]{:S(2)}) %collective-permute-start.18) | collective-permute-done | bytes 221216 | tf_op jit(solution)/shard_map/ppermute | solution.py:511
  538.9 29.7 %collective-permute-done.19.refs_7_ = bf16[4,27,8,128]{3,2,1,0:T(8,128)(2,1)S(1)} collective-permute-done((bf16[4,27,8,128]{3,2,1,0:T(8,128)(2,1)S(1)}, bf16[4,27,8,128]{3,2,1,0:T(8,128)(2,1)S(1)}, u32[]{:S(2)}, u32[]{:S(2)}) %collective-permute-start.19) | collective-permute-done | bytes 221216 | tf_op jit(solution)/shard_map/ppermute | solution.py:511
  568.6 9.2 %collective-permute-done.20.refs_8_ = bf16[4,27,8,128]{3,2,1,0:T(8,128)(2,1)S(1)} collective-permute-done((bf16[4,27,8,128]{3,2,1,0:T(8,128)(2,1)S(1)}, bf16[4,27,8,128]{3,2,1,0:T(8,128)(2,1)S(1)}, u32[]{:S(2)}, u32[]{:S(2)}) %collective-permute-start.20) | collective-permute-done | bytes 221216 | tf_op jit(solution)/shard_map/ppermute | solution.py:511
  579.5 11.5 %analysis.3.refs_2_ = f32[64,128,512]{2,1,0:T(8,128)} custom-call(s32[2]{0:T(128)S(1)} %copy-done.5, s32[64]{0:T(128)S(1)} %copy-done.4, bf16[8,5,64,128]{3,2,1,0:T(8,128)(2,1)S(1)} %get-tuple-element.71.refs_0_, bf16[8,5,64,128]{3,2,1,0:T(8,128)(2,1)S(1)} %copy-done.1, bf16[8,5,64,128]{3,2,1,0:T(8,128)(2,1)S(1)} %copy-done.3, ...), custom_call_target="tpu_custom_call" | custom-call | flops 1342177280 | bytes 46661632 | tf_op jit(solution)/shard_map/analysis/pallas_call | solution.py:480
  591.0 136.7 %all-to-all-done.1.refs_1_.refs_0_ = bf16[864,56,128]{2,1,0:T(8,128)(2,1)} async-done(((bf16[864,56,128]{2,1,0:T(8,128)(2,1)}), bf16[864,56,128]{2,1,0:T(8,128)(2,1)}, u32[]{:S(2)}, u32[]{:S(2)}) %all-to-all-start.1) | async-done | bytes 12386336 | tf_op jit(solution)/shard_map/all_to_all | solution.py:501
  727.7 4.4 collective-permute-start.29
  732.1 35.1 %analysis.4.refs_5_ = f32[64,128,512]{2,1,0:T(8,128)} custom-call(s32[2]{0:T(128)S(1)} %copy-done.5, s32[64]{0:T(128)S(1)} %copy-done.4, bf16[864,56,128]{2,1,0:T(8,128)(2,1)} %all-to-all-done.1.refs_1_.refs_0_, bf16[64,1024,512]{2,1,0:T(8,128)(2,1)} %refs_4_.3, f32[64,128,512]{2,1,0:T(8,128)} %analysis.3.refs_2_), custom_call_target="tpu_custom_call", output_to_operand_aliasing={{}: (4, {})} | custom-call | flops 6341787648 | bytes 91291648 | tf_op jit(solution)/shard_map/analysis/pallas_call | solution.py:480
  767.2 6.8 analysis.5
  (165 shorter events, 63.8 us)
Async XLA Ops:
  15.6 46.9 %collective-permute-start.1 = (bf16[8,5,64,128]{3,2,1,0:T(8,128)(2,1)}, bf16[8,5,64,128]{3,2,1,0:T(8,128)(2,1)S(1)}, u32[]{:S(2)}, u32[]{:S(2)}) collective-permute-start(bf16[8,5,64,128]{3,2,1,0:T(8,128)(2,1)} %get-tuple-element.13), channel_id=1, source_target_pairs={{0,8},{4,12},{8,0},{12,4},{1,9},{5,13},{9,1},{13,5},{2,10},{6,14},... | collective-permute-start | bytes 1966088 | tf_op jit(solution)/shard_map/ppermute | solution.py:505
  18.2 44.3 %collective-permute-start.2 = (bf16[8,5,64,128]{3,2,1,0:T(8,128)(2,1)}, bf16[8,5,64,128]{3,2,1,0:T(8,128)(2,1)S(1)}, u32[]{:S(2)}, u32[]{:S(2)}) collective-permute-start(bf16[8,5,64,128]{3,2,1,0:T(8,128)(2,1)} %get-tuple-element.14), channel_id=1, source_target_pairs={{0,12},{4,8},{8,4},{12,0},{1,13},{5,9},{9,5},{13,1},{2,14},{6,10},... | collective-permute-start | bytes 1966088 | tf_op jit(solution)/shard_map/ppermute | solution.py:505
  64.2 326.9 %all-to-all-start = ((bf16[864,64,128]{2,1,0:T(8,128)(2,1)}), bf16[864,64,128]{2,1,0:T(8,128)(2,1)}, u32[]{:S(2)}, u32[]{:S(2)}) async-start(bf16[864,64,128]{2,1,0:T(8,128)(2,1)} %hold.8), calls=%async_computation | async-start | bytes 28311552 | tf_op jit(solution)/shard_map/all_to_all | solution.py:501
  96.9 78.9 %collective-permute-start.4 = (bf16[4,5,64,128]{3,2,1,0:T(8,128)(2,1)S(1)}, bf16[4,5,64,128]{3,2,1,0:T(8,128)(2,1)S(1)}, u32[]{:S(2)}, u32[]{:S(2)}) collective-permute-start(bf16[4,5,64,128]{3,2,1,0:T(8,128)(2,1)S(1)} %pad_maximum_fusion.3), channel_id=1, source_target_pairs={{0,2},{1,3},{2,0},{3,1},{16,18},{17,19},{18,16},{19,17},{4,6},{5,7... | collective-permute-start | bytes 983048 | tf_op jit(solution)/shard_map/ppermute | solution.py:511
  98.7 87.0 %collective-permute-start.5 = (bf16[4,5,64,128]{3,2,1,0:T(8,128)(2,1)S(1)}, bf16[4,5,64,128]{3,2,1,0:T(8,128)(2,1)S(1)}, u32[]{:S(2)}, u32[]{:S(2)}) collective-permute-start(bf16[4,5,64,128]{3,2,1,0:T(8,128)(2,1)S(1)} %pad_maximum_fusion.4), channel_id=1, source_target_pairs={{0,3},{1,2},{2,1},{3,0},{16,19},{17,18},{18,17},{19,16},{4,7},{5,6... | collective-permute-start | bytes 983048 | tf_op jit(solution)/shard_map/ppermute | solution.py:511
  98.9 90.5 %collective-permute-start.6 = (bf16[4,5,64,128]{3,2,1,0:T(8,128)(2,1)S(1)}, bf16[4,5,64,128]{3,2,1,0:T(8,128)(2,1)S(1)}, u32[]{:S(2)}, u32[]{:S(2)}) collective-permute-start(bf16[4,5,64,128]{3,2,1,0:T(8,128)(2,1)S(1)} %pad_maximum_fusion.5), channel_id=1, source_target_pairs={{0,16},{1,17},{2,18},{3,19},{16,0},{17,1},{18,2},{19,3},{4,20},{5,... | collective-permute-start | bytes 983048 | tf_op jit(solution)/shard_map/ppermute | solution.py:511
  100.6 96.1 %collective-permute-start.7 = (bf16[4,5,64,128]{3,2,1,0:T(8,128)(2,1)S(1)}, bf16[4,5,64,128]{3,2,1,0:T(8,128)(2,1)S(1)}, u32[]{:S(2)}, u32[]{:S(2)}) collective-permute-start(bf16[4,5,64,128]{3,2,1,0:T(8,128)(2,1)S(1)} %pad_maximum_fusion.6), channel_id=1, source_target_pairs={{0,17},{1,16},{2,19},{3,18},{16,1},{17,0},{18,3},{19,2},{4,21},{5,... | collective-permute-start | bytes 983048 | tf_op jit(solution)/shard_map/ppermute | solution.py:511
  100.9 113.0 %collective-permute-start.8 = (bf16[4,5,64,128]{3,2,1,0:T(8,128)(2,1)S(1)}, bf16[4,5,64,128]{3,2,1,0:T(8,128)(2,1)S(1)}, u32[]{:S(2)}, u32[]{:S(2)}) collective-permute-start(bf16[4,5,64,128]{3,2,1,0:T(8,128)(2,1)S(1)} %pad_maximum_fusion.7), channel_id=1, source_target_pairs={{0,18},{1,19},{2,16},{3,17},{16,2},{17,3},{18,0},{19,1},{4,22},{5,... | collective-permute-start | bytes 983048 | tf_op jit(solution)/shard_map/ppermute | solution.py:511
  175.7 56.8 %collective-permute-start.9 = (bf16[4,5,64,128]{3,2,1,0:T(8,128)(2,1)S(1)}, bf16[4,5,64,128]{3,2,1,0:T(8,128)(2,1)S(1)}, u32[]{:S(2)}, u32[]{:S(2)}) collective-permute-start(bf16[4,5,64,128]{3,2,1,0:T(8,128)(2,1)S(1)} %pad_maximum_fusion.8), channel_id=1, source_target_pairs={{0,19},{1,18},{2,17},{3,16},{16,3},{17,2},{18,1},{19,0},{4,23},{5,... | collective-permute-start | bytes 983048 | tf_op jit(solution)/shard_map/ppermute | solution.py:511
  256.9 40.9 %collective-permute-start.16 = (bf16[4,5,64,128]{3,2,1,0:T(8,128)(2,1)S(1)}, bf16[4,5,64,128]{3,2,1,0:T(8,128)(2,1)S(1)}, u32[]{:S(2)}, u32[]{:S(2)}) collective-permute-start(bf16[4,5,64,128]{3,2,1,0:T(8,128)(2,1)S(1)} %get-tuple-element.21), channel_id=1, source_target_pairs={{0,19},{1,18},{2,17},{3,16},{16,3},{17,2},{18,1},{19,0},{4,23},{5,... | collective-permute-start | bytes 983048 | tf_op jit(solution)/shard_map/ppermute | solution.py:511
  256.9 40.8 %collective-permute-start.15 = (bf16[4,5,64,128]{3,2,1,0:T(8,128)(2,1)S(1)}, bf16[4,5,64,128]{3,2,1,0:T(8,128)(2,1)S(1)}, u32[]{:S(2)}, u32[]{:S(2)}) collective-permute-start(bf16[4,5,64,128]{3,2,1,0:T(8,128)(2,1)S(1)} %get-tuple-element.22), channel_id=1, source_target_pairs={{0,18},{1,19},{2,16},{3,17},{16,2},{17,3},{18,0},{19,1},{4,22},{5,... | collective-permute-start | bytes 983048 | tf_op jit(solution)/shard_map/ppermute | solution.py:511
  259.2 38.4 %collective-permute-start.14 = (bf16[4,5,64,128]{3,2,1,0:T(8,128)(2,1)S(1)}, bf16[4,5,64,128]{3,2,1,0:T(8,128)(2,1)S(1)}, u32[]{:S(2)}, u32[]{:S(2)}) collective-permute-start(bf16[4,5,64,128]{3,2,1,0:T(8,128)(2,1)S(1)} %get-tuple-element.23), channel_id=1, source_target_pairs={{0,17},{1,16},{2,19},{3,18},{16,1},{17,0},{18,3},{19,2},{4,21},{5,... | collective-permute-start | bytes 983048 | tf_op jit(solution)/shard_map/ppermute | solution.py:511
  391.1 60.3 %collective-permute-start.24 = (bf16[8,5,64,128]{3,2,1,0:T(8,128)(2,1)}, bf16[8,5,64,128]{3,2,1,0:T(8,128)(2,1)S(1)}, u32[]{:S(2)}, u32[]{:S(2)}) collective-permute-start(bf16[8,5,64,128]{3,2,1,0:T(8,128)(2,1)} %hold.9), channel_id=1, source_target_pairs={{0,4},{4,0},{8,12},{12,8},{1,5},{5,1},{9,13},{13,9},{2,6},{6,2},{1... | collective-permute-start | bytes 1966088 | tf_op jit(solution)/shard_map/ppermute | solution.py:505
  391.2 60.2 %collective-permute-start.25 = (bf16[8,5,64,128]{3,2,1,0:T(8,128)(2,1)}, bf16[8,5,64,128]{3,2,1,0:T(8,128)(2,1)S(1)}, u32[]{:S(2)}, u32[]{:S(2)}) collective-permute-start(bf16[8,5,64,128]{3,2,1,0:T(8,128)(2,1)} %hold.10), channel_id=1, source_target_pairs={{0,8},{4,12},{8,0},{12,4},{1,9},{5,13},{9,1},{13,5},{2,10},{6,14},... | collective-permute-start | bytes 1966088 | tf_op jit(solution)/shard_map/ppermute | solution.py:505
  391.3 60.2 %collective-permute-start.26 = (bf16[8,5,64,128]{3,2,1,0:T(8,128)(2,1)}, bf16[8,5,64,128]{3,2,1,0:T(8,128)(2,1)S(1)}, u32[]{:S(2)}, u32[]{:S(2)}) collective-permute-start(bf16[8,5,64,128]{3,2,1,0:T(8,128)(2,1)} %hold.11), channel_id=1, source_target_pairs={{0,12},{4,8},{8,4},{12,0},{1,13},{5,9},{9,5},{13,1},{2,14},{6,10},... | collective-permute-start | bytes 1966088 | tf_op jit(solution)/shard_map/ppermute | solution.py:505
  452.7 275.1 %all-to-all-start.1 = ((bf16[864,56,128]{2,1,0:T(8,128)(2,1)}), bf16[864,56,128]{2,1,0:T(8,128)(2,1)}, u32[]{:S(2)}, u32[]{:S(2)}) async-start(bf16[864,56,128]{2,1,0:T(8,128)(2,1)} %hold.12), calls=%async_computation.1 | async-start | bytes 24772608 | tf_op jit(solution)/shard_map/all_to_all | solution.py:501
  457.0 120.9 %collective-permute-start.23 = (bf16[4,27,8,128]{3,2,1,0:T(8,128)(2,1)S(1)}, bf16[4,27,8,128]{3,2,1,0:T(8,128)(2,1)S(1)}, u32[]{:S(2)}, u32[]{:S(2)}) collective-permute-start(bf16[4,27,8,128]{3,2,1,0:T(8,128)(2,1)S(1)} %get-tuple-element.32), channel_id=1, source_target_pairs={{0,19},{1,18},{2,17},{3,16},{16,3},{17,2},{18,1},{19,0},{4,23},{5,... | collective-permute-start | bytes 663560 | tf_op jit(solution)/shard_map/ppermute | solution.py:511
  459.1 118.8 %collective-permute-start.22 = (bf16[4,27,8,128]{3,2,1,0:T(8,128)(2,1)S(1)}, bf16[4,27,8,128]{3,2,1,0:T(8,128)(2,1)S(1)}, u32[]{:S(2)}, u32[]{:S(2)}) collective-permute-start(bf16[4,27,8,128]{3,2,1,0:T(8,128)(2,1)S(1)} %get-tuple-element.33), channel_id=1, source_target_pairs={{0,18},{1,19},{2,16},{3,17},{16,2},{17,3},{18,0},{19,1},{4,22},{5,... | collective-permute-start | bytes 663560 | tf_op jit(solution)/shard_map/ppermute | solution.py:511
  459.4 118.4 %collective-permute-start.21 = (bf16[4,27,8,128]{3,2,1,0:T(8,128)(2,1)S(1)}, bf16[4,27,8,128]{3,2,1,0:T(8,128)(2,1)S(1)}, u32[]{:S(2)}, u32[]{:S(2)}) collective-permute-start(bf16[4,27,8,128]{3,2,1,0:T(8,128)(2,1)S(1)} %get-tuple-element.34), channel_id=1, source_target_pairs={{0,17},{1,16},{2,19},{3,18},{16,1},{17,0},{18,3},{19,2},{4,21},{5,... | collective-permute-start | bytes 663560 | tf_op jit(solution)/shard_map/ppermute | solution.py:511
  460.8 117.0 %collective-permute-start.20 = (bf16[4,27,8,128]{3,2,1,0:T(8,128)(2,1)S(1)}, bf16[4,27,8,128]{3,2,1,0:T(8,128)(2,1)S(1)}, u32[]{:S(2)}, u32[]{:S(2)}) collective-permute-start(bf16[4,27,8,128]{3,2,1,0:T(8,128)(2,1)S(1)} %get-tuple-element.35), channel_id=1, source_target_pairs={{0,16},{1,17},{2,18},{3,19},{16,0},{17,1},{18,2},{19,3},{4,20},{5,... | collective-permute-start | bytes 663560 | tf_op jit(solution)/shard_map/ppermute | solution.py:511
  462.9 74.6 %collective-permute-start.18 = (bf16[4,27,8,128]{3,2,1,0:T(8,128)(2,1)S(1)}, bf16[4,27,8,128]{3,2,1,0:T(8,128)(2,1)S(1)}, u32[]{:S(2)}, u32[]{:S(2)}) collective-permute-start(bf16[4,27,8,128]{3,2,1,0:T(8,128)(2,1)S(1)} %get-tuple-element.37), channel_id=1, source_target_pairs={{0,2},{1,3},{2,0},{3,1},{16,18},{17,19},{18,16},{19,17},{4,6},{5,7... | collective-permute-start | bytes 663560 | tf_op jit(solution)/shard_map/ppermute | solution.py:511
  727.7 39.5 %collective-permute-start.27 = (bf16[8,27,8,128]{3,2,1,0:T(8,128)(2,1)}, bf16[8,27,8,128]{3,2,1,0:T(8,128)(2,1)S(1)}, u32[]{:S(2)}, u32[]{:S(2)}) collective-permute-start(bf16[8,27,8,128]{3,2,1,0:T(8,128)(2,1)} %hold.13), channel_id=1, source_target_pairs={{0,4},{4,0},{8,12},{12,8},{1,5},{5,1},{9,13},{13,9},{2,6},{6,2},{1... | collective-permute-start | bytes 1327112 | tf_op jit(solution)/shard_map/ppermute | solution.py:505
  727.7 39.5 %collective-permute-start.28 = (bf16[8,27,8,128]{3,2,1,0:T(8,128)(2,1)}, bf16[8,27,8,128]{3,2,1,0:T(8,128)(2,1)S(1)}, u32[]{:S(2)}, u32[]{:S(2)}) collective-permute-start(bf16[8,27,8,128]{3,2,1,0:T(8,128)(2,1)} %hold.14), channel_id=1, source_target_pairs={{0,8},{4,12},{8,0},{12,4},{1,9},{5,13},{9,1},{13,5},{2,10},{6,14},... | collective-permute-start | bytes 1327112 | tf_op jit(solution)/shard_map/ppermute | solution.py:505
  727.7 39.5 %collective-permute-start.29 = (bf16[8,27,8,128]{3,2,1,0:T(8,128)(2,1)}, bf16[8,27,8,128]{3,2,1,0:T(8,128)(2,1)S(1)}, u32[]{:S(2)}, u32[]{:S(2)}) collective-permute-start(bf16[8,27,8,128]{3,2,1,0:T(8,128)(2,1)} %hold.15), channel_id=1, source_target_pairs={{0,12},{4,8},{8,4},{12,0},{1,13},{5,9},{9,5},{13,1},{2,14},{6,10},... | collective-permute-start | bytes 1327112 | tf_op jit(solution)/shard_map/ppermute | solution.py:505
  (38 other events, 1050.8 us)

commit v6 on v5

--- a/solution.py
+++ b/solution.py
@@ -49,7 +49,7 @@
     square = grid * grid
     cheb = np.polynomial.chebyshev.Chebyshev
     sine = cheb.fit(square, np.sin(np.pi * grid) / grid, 4, domain=[0.0, 0.25])
-    cosine = cheb.fit(square, np.cos(np.pi * grid), 5, domain=[0.0, 0.25])
+    cosine = cheb.fit(square, np.cos(np.pi * grid), 4, domain=[0.0, 0.25])
     poly = np.polynomial.polynomial.Polynomial
     return (
         [float(v) for v in sine.convert(kind=poly).coef],
@@ -449,7 +449,7 @@
         radii, count = rows * device_count, fields[0].shape[-2]
         block = math.gcd(count, MODE_BLOCK)
         shift = skip // block
-        halves = not relative and radii % 32 == 0 and radii >= 768
+        halves = not relative and radii % 32 == 0 and radii * block >= 768 * MODE_BLOCK
         steps = 2 if halves else 1
         part = radii // steps
         out_spec = pl.BlockSpec((block, lanes, degrees), lambda i, j: (shift + i, 0, 0))

time: 775 us -> 773 us (level)
  no operation moved by 1% of the time
where the time goes in v6:
time: 773 us; the launch traced here: 769 us
  waiting for transfers between devices  517 us (67%)
  Pallas kernels  161 us (21%)
  starting transfers between devices  60.6 us (8%)
  local copies, waits for them, and re-layouts  15.5 us (2%)
  other arithmetic  14.1 us (2%)
    ppermute x21, waiting for transfers between devices, within(): lax.ppermute(piece, ('comp', 'lo'), [(i, i ^ turn) for i in range(group)])  276 us
    all_to_all x2, waiting for transfers between devices, exchange(): return lax.all_to_all(value, axes, split_axis=0, concat_axis=0, tiled=True)  229 us
    pallas_call x2, Pallas kernels, physical(): pl.pallas_call(functools.partial(physical_kernel, relative, relative_outs...  67.5 us
    pallas_call x3, Pallas kernels, analysis(): pl.pallas_call(functools.partial(analysis_kernel, skip, held is None, las...  49 us
    pallas_call x2, Pallas kernels, synthesis(): pl.pallas_call(functools.partial(synthesis_kernel, planes, outs), grid=(l...  44.5 us
    ppermute x21, starting transfers between devices, within(): lax.ppermute(piece, ('comp', 'lo'), [(i, i ^ turn) for i in range(group)])  26.1 us
    all_to_all x2, starting transfers between devices, exchange(): return lax.all_to_all(value, axes, split_axis=0, concat_axis=0, tiled=True)  20 us
  transfers between devices with their start and end apart: 32, of which 16 were waited for; matrix products, arithmetic and copies ran while one was open for 3% of the time, Pallas kernels for 19%

profile of v6, /device:TPU:0, one launch (start us, length us, event | category | flops | bytes accessed | tf_op | source)
XLA Modules:
  0.0 769.1 jit_solution(15289612149674466270)
XLA Ops:
  0.7 11.9 %synthesis.2 = (bf16[8,5,64,128]{3,2,1,0:T(8,128)(2,1)}, bf16[8,5,64,128]{3,2,1,0:T(8,128)(2,1)}, bf16[8,5,64,128]{3,2,1,0:T(8,128)(2,1)}, bf16[8,5,64,128]{3,2,1,0:T(8,128)(2,1)}) custom-call(s32[2]{0:T(128)} %pad_add_fusion.place_ref, s32[1]{0:T(128)} %bitcast.3.first_ref, s32[64]{0:T(128)} %cutoff_ref.9, f32[2,1024]{1,0:T(2,128)} %constant.60.clone.mode_ref, ...), custom_call_target="tpu_custom_call" | custom-call | flops 1342177280 | bytes 29884416 | tf_op jit(solution)/shard_map/synthesis/pallas_call | solution.py:361
  18.2 32.6 %synthesis.3.refs_0_ = bf16[864,64,128]{2,1,0:T(8,128)(2,1)} custom-call(s32[2]{0:T(128)} %pad_add_fusion.place_ref, s32[1]{0:T(128)} %bitcast.3.first_ref, s32[64]{0:T(128)} %cutoff_ref.9, f32[2,1024]{1,0:T(2,128)} %constant.60.clone.mode_ref, f32[2,512]{1,0:T(2,128)} %constant.61.clone.degree_ref, f32[1,64,2,64,512]{4,3,2,1,0:T(8,128)} %spectrum_ref.3, ...), custom_call_target="tpu_custom_call" | custom-call | flops 7247757312 | bytes 87556096 | tf_op jit(solution)/shard_map/synthesis/pallas_call | solution.py:361
  50.8 11.7 %collective-permute-done.1.refs_2_ = bf16[8,5,64,128]{3,2,1,0:T(8,128)(2,1)S(1)} collective-permute-done((bf16[8,5,64,128]{3,2,1,0:T(8,128)(2,1)}, bf16[8,5,64,128]{3,2,1,0:T(8,128)(2,1)S(1)}, u32[]{:S(2)}, u32[]{:S(2)}) %collective-permute-start.1) | collective-permute-done | bytes 655392 | tf_op jit(solution)/shard_map/ppermute | solution.py:505
  64.2 15.9 %all-to-all-start = ((bf16[864,64,128]{2,1,0:T(8,128)(2,1)}), bf16[864,64,128]{2,1,0:T(8,128)(2,1)}, u32[]{:S(2)}, u32[]{:S(2)}) async-start(bf16[864,64,128]{2,1,0:T(8,128)(2,1)} %hold.8), calls=%async_computation | async-start | bytes 28311552 | tf_op jit(solution)/shard_map/all_to_all | solution.py:501
  85.0 8.9 %multiply_convert_fusion.1 = (bf16[4,256,256]{2,1,0:T(8,128)(2,1)S(1)}, bf16[4,256,256]{2,1,0:T(8,128)(2,1)S(1)}, bf16[4,256,256]{2,1,0:T(8,128)(2,1)S(1)}, bf16[4,256,256]{2,1,0:T(8,128)(2,1)S(1)}) fusion(s32[4,256]{1,0:T(4,128)S(1)} %iota_add_fusion), kind=kLoop, calls=%fused_computation.15 | loop fusion | flops 9437184 | bytes 2101248 | tf_op jit(solution)/shard_map/convert_element_type | solution.py:27
  103.6 72.1 %collective-permute-done.4 = bf16[4,5,64,128]{3,2,1,0:T(8,128)(2,1)S(1)} collective-permute-done((bf16[4,5,64,128]{3,2,1,0:T(8,128)(2,1)S(1)}, bf16[4,5,64,128]{3,2,1,0:T(8,128)(2,1)S(1)}, u32[]{:S(2)}, u32[]{:S(2)}) %collective-permute-start.4) | collective-permute-done | bytes 327712 | tf_op jit(solution)/shard_map/ppermute | solution.py:511
  178.4 7.2 collective-permute-done.5
  189.5 7.2 collective-permute-done.7
  196.8 17.2 %collective-permute-done.8 = bf16[4,5,64,128]{3,2,1,0:T(8,128)(2,1)S(1)} collective-permute-done((bf16[4,5,64,128]{3,2,1,0:T(8,128)(2,1)S(1)}, bf16[4,5,64,128]{3,2,1,0:T(8,128)(2,1)S(1)}, u32[]{:S(2)}, u32[]{:S(2)}) %collective-permute-start.8) | collective-permute-done | bytes 327712 | tf_op jit(solution)/shard_map/ppermute | solution.py:511
  214.0 18.6 %collective-permute-done.9 = bf16[4,5,64,128]{3,2,1,0:T(8,128)(2,1)S(1)} collective-permute-done((bf16[4,5,64,128]{3,2,1,0:T(8,128)(2,1)S(1)}, bf16[4,5,64,128]{3,2,1,0:T(8,128)(2,1)S(1)}, u32[]{:S(2)}, u32[]{:S(2)}) %collective-permute-start.9) | collective-permute-done | bytes 327712 | tf_op jit(solution)/shard_map/ppermute | solution.py:511
  234.1 12.3 %physical.2 = bf16[8,4,5,64,128]{4,3,2,1,0:T(8,128)(2,1)} custom-call(s32[2]{0:T(128)} %pad_add_fusion.place_ref, f32[5]{0:T(128)} %dynamic-slice_multiply_fusion.trap_ref, f32[5]{0:T(128)} %dynamic_slice.15.weight_ref, f32[2,128]{1,0:T(2,128)} %reshape.47.lanes_ref, bf16[4,256,512]{2,1,0:T(8,128)(2,1)} %get-tuple-element.131.table_ref, ...), custom_call_target="tpu_custom_call" | custom-call | flops 2684354560 | bytes 7340032 | tf_op jit(solution)/shard_map/physical/pallas_call | solution.py:410
  250.6 5.2 collective-permute-start.11
  260.1 28.8 %collective-permute-done.11.refs_1_ = bf16[4,5,64,128]{3,2,1,0:T(8,128)(2,1)S(1)} collective-permute-done((bf16[4,5,64,128]{3,2,1,0:T(8,128)(2,1)S(1)}, bf16[4,5,64,128]{3,2,1,0:T(8,128)(2,1)S(1)}, u32[]{:S(2)}, u32[]{:S(2)}) %collective-permute-start.11) | collective-permute-done | bytes 327712 | tf_op jit(solution)/shard_map/ppermute | solution.py:511
  289.0 5.7 collective-permute-done.12.refs_2_
  298.6 92.4 %all-to-all-done.refs_1_ = bf16[864,64,128]{2,1,0:T(8,128)(2,1)} async-done(((bf16[864,64,128]{2,1,0:T(8,128)(2,1)}), bf16[864,64,128]{2,1,0:T(8,128)(2,1)}, u32[]{:S(2)}, u32[]{:S(2)}) %all-to-all-start) | async-done | bytes 14155808 | tf_op jit(solution)/shard_map/all_to_all | solution.py:501
  395.5 55.3 %physical.3 = (bf16[2,16,27,56,128]{4,3,2,1,0:T(8,128)(2,1)}, bf16[8,4,27,8,128]{4,3,2,1,0:T(8,128)(2,1)}) custom-call(s32[2]{0:T(128)} %pad_add_fusion.place_ref, f32[27]{0:T(128)} %dynamic-slice_multiply_fusion.1.trap_ref, f32[27]{0:T(128)} %dynamic_slice.13.weight_ref, f32[2,128]{1,0:T(2,128)} %reshape.47.lanes_ref, ...), custom_call_target="tpu_custom_call" | custom-call | flops 14495514624 | bytes 30408704 | tf_op jit(solution)/shard_map/physical/pallas_call | solution.py:410
  464.1 72.8 %collective-permute-done.18.refs_6_ = bf16[4,27,8,128]{3,2,1,0:T(8,128)(2,1)S(1)} collective-permute-done((bf16[4,27,8,128]{3,2,1,0:T(8,128)(2,1)S(1)}, bf16[4,27,8,128]{3,2,1,0:T(8,128)(2,1)S(1)}, u32[]{:S(2)}, u32[]{:S(2)}) %collective-permute-start.18) | collective-permute-done | bytes 221216 | tf_op jit(solution)/shard_map/ppermute | solution.py:511
  538.3 29.7 %collective-permute-done.19.refs_7_ = bf16[4,27,8,128]{3,2,1,0:T(8,128)(2,1)S(1)} collective-permute-done((bf16[4,27,8,128]{3,2,1,0:T(8,128)(2,1)S(1)}, bf16[4,27,8,128]{3,2,1,0:T(8,128)(2,1)S(1)}, u32[]{:S(2)}, u32[]{:S(2)}) %collective-permute-start.19) | collective-permute-done | bytes 221216 | tf_op jit(solution)/shard_map/ppermute | solution.py:511
  568.0 9.2 %collective-permute-done.20.refs_8_ = bf16[4,27,8,128]{3,2,1,0:T(8,128)(2,1)S(1)} collective-permute-done((bf16[4,27,8,128]{3,2,1,0:T(8,128)(2,1)S(1)}, bf16[4,27,8,128]{3,2,1,0:T(8,128)(2,1)S(1)}, u32[]{:S(2)}, u32[]{:S(2)}) %collective-permute-start.20) | collective-permute-done | bytes 221216 | tf_op jit(solution)/shard_map/ppermute | solution.py:511
  578.9 11.5 %analysis.3.refs_2_ = f32[64,128,512]{2,1,0:T(8,128)} custom-call(s32[2]{0:T(128)S(1)} %copy-done.5, s32[64]{0:T(128)S(1)} %copy-done.4, bf16[8,5,64,128]{3,2,1,0:T(8,128)(2,1)S(1)} %get-tuple-element.71.refs_0_, bf16[8,5,64,128]{3,2,1,0:T(8,128)(2,1)S(1)} %copy-done.1, bf16[8,5,64,128]{3,2,1,0:T(8,128)(2,1)S(1)} %copy-done.3, ...), custom_call_target="tpu_custom_call" | custom-call | flops 1342177280 | bytes 46661632 | tf_op jit(solution)/shard_map/analysis/pallas_call | solution.py:480
  590.4 136.7 %all-to-all-done.1.refs_1_.refs_0_ = bf16[864,56,128]{2,1,0:T(8,128)(2,1)} async-done(((bf16[864,56,128]{2,1,0:T(8,128)(2,1)}), bf16[864,56,128]{2,1,0:T(8,128)(2,1)}, u32[]{:S(2)}, u32[]{:S(2)}) %all-to-all-start.1) | async-done | bytes 12386336 | tf_op jit(solution)/shard_map/all_to_all | solution.py:501
  727.2 4.4 collective-permute-start.29
  731.5 30.7 %analysis.4.refs_5_ = f32[64,128,512]{2,1,0:T(8,128)} custom-call(s32[2]{0:T(128)S(1)} %copy-done.5, s32[64]{0:T(128)S(1)} %copy-done.4, bf16[864,56,128]{2,1,0:T(8,128)(2,1)} %all-to-all-done.1.refs_1_.refs_0_, bf16[64,1024,512]{2,1,0:T(8,128)(2,1)} %refs_4_.3, f32[64,128,512]{2,1,0:T(8,128)} %analysis.3.refs_2_), custom_call_target="tpu_custom_call", output_to_operand_aliasing={{}: (4, {})} | custom-call | flops 6341787648 | bytes 91291648 | tf_op jit(solution)/shard_map/analysis/pallas_call | solution.py:480
  762.3 6.8 analysis.5
  (165 shorter events, 63.8 us)
Async XLA Ops:
  12.6 38.2 %collective-permute-start = (bf16[8,5,64,128]{3,2,1,0:T(8,128)(2,1)}, bf16[8,5,64,128]{3,2,1,0:T(8,128)(2,1)S(1)}, u32[]{:S(2)}, u32[]{:S(2)}) collective-permute-start(bf16[8,5,64,128]{3,2,1,0:T(8,128)(2,1)} %get-tuple-element.12), channel_id=1, source_target_pairs={{0,4},{4,0},{8,12},{12,8},{1,5},{5,1},{9,13},{13,9},{2,6},{6,2},{1... | collective-permute-start | bytes 1966088 | tf_op jit(solution)/shard_map/ppermute | solution.py:505
  15.6 46.9 %collective-permute-start.1 = (bf16[8,5,64,128]{3,2,1,0:T(8,128)(2,1)}, bf16[8,5,64,128]{3,2,1,0:T(8,128)(2,1)S(1)}, u32[]{:S(2)}, u32[]{:S(2)}) collective-permute-start(bf16[8,5,64,128]{3,2,1,0:T(8,128)(2,1)} %get-tuple-element.13), channel_id=1, source_target_pairs={{0,8},{4,12},{8,0},{12,4},{1,9},{5,13},{9,1},{13,5},{2,10},{6,14},... | collective-permute-start | bytes 1966088 | tf_op jit(solution)/shard_map/ppermute | solution.py:505
  18.2 44.3 %collective-permute-start.2 = (bf16[8,5,64,128]{3,2,1,0:T(8,128)(2,1)}, bf16[8,5,64,128]{3,2,1,0:T(8,128)(2,1)S(1)}, u32[]{:S(2)}, u32[]{:S(2)}) collective-permute-start(bf16[8,5,64,128]{3,2,1,0:T(8,128)(2,1)} %get-tuple-element.14), channel_id=1, source_target_pairs={{0,12},{4,8},{8,4},{12,0},{1,13},{5,9},{9,5},{13,1},{2,14},{6,10},... | collective-permute-start | bytes 1966088 | tf_op jit(solution)/shard_map/ppermute | solution.py:505
  64.2 326.9 %all-to-all-start = ((bf16[864,64,128]{2,1,0:T(8,128)(2,1)}), bf16[864,64,128]{2,1,0:T(8,128)(2,1)}, u32[]{:S(2)}, u32[]{:S(2)}) async-start(bf16[864,64,128]{2,1,0:T(8,128)(2,1)} %hold.8), calls=%async_computation | async-start | bytes 28311552 | tf_op jit(solution)/shard_map/all_to_all | solution.py:501
  96.9 78.9 %collective-permute-start.4 = (bf16[4,5,64,128]{3,2,1,0:T(8,128)(2,1)S(1)}, bf16[4,5,64,128]{3,2,1,0:T(8,128)(2,1)S(1)}, u32[]{:S(2)}, u32[]{:S(2)}) collective-permute-start(bf16[4,5,64,128]{3,2,1,0:T(8,128)(2,1)S(1)} %pad_maximum_fusion.3), channel_id=1, source_target_pairs={{0,2},{1,3},{2,0},{3,1},{16,18},{17,19},{18,16},{19,17},{4,6},{5,7... | collective-permute-start | bytes 983048 | tf_op jit(solution)/shard_map/ppermute | solution.py:511
  98.7 87.0 %collective-permute-start.5 = (bf16[4,5,64,128]{3,2,1,0:T(8,128)(2,1)S(1)}, bf16[4,5,64,128]{3,2,1,0:T(8,128)(2,1)S(1)}, u32[]{:S(2)}, u32[]{:S(2)}) collective-permute-start(bf16[4,5,64,128]{3,2,1,0:T(8,128)(2,1)S(1)} %pad_maximum_fusion.4), channel_id=1, source_target_pairs={{0,3},{1,2},{2,1},{3,0},{16,19},{17,18},{18,17},{19,16},{4,7},{5,6... | collective-permute-start | bytes 983048 | tf_op jit(solution)/shard_map/ppermute | solution.py:511
  98.9 90.5 %collective-permute-start.6 = (bf16[4,5,64,128]{3,2,1,0:T(8,128)(2,1)S(1)}, bf16[4,5,64,128]{3,2,1,0:T(8,128)(2,1)S(1)}, u32[]{:S(2)}, u32[]{:S(2)}) collective-permute-start(bf16[4,5,64,128]{3,2,1,0:T(8,128)(2,1)S(1)} %pad_maximum_fusion.5), channel_id=1, source_target_pairs={{0,16},{1,17},{2,18},{3,19},{16,0},{17,1},{18,2},{19,3},{4,20},{5,... | collective-permute-start | bytes 983048 | tf_op jit(solution)/shard_map/ppermute | solution.py:511
  100.6 96.1 %collective-permute-start.7 = (bf16[4,5,64,128]{3,2,1,0:T(8,128)(2,1)S(1)}, bf16[4,5,64,128]{3,2,1,0:T(8,128)(2,1)S(1)}, u32[]{:S(2)}, u32[]{:S(2)}) collective-permute-start(bf16[4,5,64,128]{3,2,1,0:T(8,128)(2,1)S(1)} %pad_maximum_fusion.6), channel_id=1, source_target_pairs={{0,17},{1,16},{2,19},{3,18},{16,1},{17,0},{18,3},{19,2},{4,21},{5,... | collective-permute-start | bytes 983048 | tf_op jit(solution)/shard_map/ppermute | solution.py:511
  100.9 113.0 %collective-permute-start.8 = (bf16[4,5,64,128]{3,2,1,0:T(8,128)(2,1)S(1)}, bf16[4,5,64,128]{3,2,1,0:T(8,128)(2,1)S(1)}, u32[]{:S(2)}, u32[]{:S(2)}) collective-permute-start(bf16[4,5,64,128]{3,2,1,0:T(8,128)(2,1)S(1)} %pad_maximum_fusion.7), channel_id=1, source_target_pairs={{0,18},{1,19},{2,16},{3,17},{16,2},{17,3},{18,0},{19,1},{4,22},{5,... | collective-permute-start | bytes 983048 | tf_op jit(solution)/shard_map/ppermute | solution.py:511
  175.7 56.8 %collective-permute-start.9 = (bf16[4,5,64,128]{3,2,1,0:T(8,128)(2,1)S(1)}, bf16[4,5,64,128]{3,2,1,0:T(8,128)(2,1)S(1)}, u32[]{:S(2)}, u32[]{:S(2)}) collective-permute-start(bf16[4,5,64,128]{3,2,1,0:T(8,128)(2,1)S(1)} %pad_maximum_fusion.8), channel_id=1, source_target_pairs={{0,19},{1,18},{2,17},{3,16},{16,3},{17,2},{18,1},{19,0},{4,23},{5,... | collective-permute-start | bytes 983048 | tf_op jit(solution)/shard_map/ppermute | solution.py:511
  250.6 38.4 %collective-permute-start.11 = (bf16[4,5,64,128]{3,2,1,0:T(8,128)(2,1)S(1)}, bf16[4,5,64,128]{3,2,1,0:T(8,128)(2,1)S(1)}, u32[]{:S(2)}, u32[]{:S(2)}) collective-permute-start(bf16[4,5,64,128]{3,2,1,0:T(8,128)(2,1)S(1)} %get-tuple-element.26), channel_id=1, source_target_pairs={{0,2},{1,3},{2,0},{3,1},{16,18},{17,19},{18,16},{19,17},{4,6},{5,7... | collective-permute-start | bytes 983048 | tf_op jit(solution)/shard_map/ppermute | solution.py:511
  256.7 40.9 %collective-permute-start.16 = (bf16[4,5,64,128]{3,2,1,0:T(8,128)(2,1)S(1)}, bf16[4,5,64,128]{3,2,1,0:T(8,128)(2,1)S(1)}, u32[]{:S(2)}, u32[]{:S(2)}) collective-permute-start(bf16[4,5,64,128]{3,2,1,0:T(8,128)(2,1)S(1)} %get-tuple-element.21), channel_id=1, source_target_pairs={{0,19},{1,18},{2,17},{3,16},{16,3},{17,2},{18,1},{19,0},{4,23},{5,... | collective-permute-start | bytes 983048 | tf_op jit(solution)/shard_map/ppermute | solution.py:511
  256.8 40.8 %collective-permute-start.15 = (bf16[4,5,64,128]{3,2,1,0:T(8,128)(2,1)S(1)}, bf16[4,5,64,128]{3,2,1,0:T(8,128)(2,1)S(1)}, u32[]{:S(2)}, u32[]{:S(2)}) collective-permute-start(bf16[4,5,64,128]{3,2,1,0:T(8,128)(2,1)S(1)} %get-tuple-element.22), channel_id=1, source_target_pairs={{0,18},{1,19},{2,16},{3,17},{16,2},{17,3},{18,0},{19,1},{4,22},{5,... | collective-permute-start | bytes 983048 | tf_op jit(solution)/shard_map/ppermute | solution.py:511
  259.1 38.4 %collective-permute-start.14 = (bf16[4,5,64,128]{3,2,1,0:T(8,128)(2,1)S(1)}, bf16[4,5,64,128]{3,2,1,0:T(8,128)(2,1)S(1)}, u32[]{:S(2)}, u32[]{:S(2)}) collective-permute-start(bf16[4,5,64,128]{3,2,1,0:T(8,128)(2,1)S(1)} %get-tuple-element.23), channel_id=1, source_target_pairs={{0,17},{1,16},{2,19},{3,18},{16,1},{17,0},{18,3},{19,2},{4,21},{5,... | collective-permute-start | bytes 983048 | tf_op jit(solution)/shard_map/ppermute | solution.py:511
  259.1 35.7 %collective-permute-start.12 = (bf16[4,5,64,128]{3,2,1,0:T(8,128)(2,1)S(1)}, bf16[4,5,64,128]{3,2,1,0:T(8,128)(2,1)S(1)}, u32[]{:S(2)}, u32[]{:S(2)}) collective-permute-start(bf16[4,5,64,128]{3,2,1,0:T(8,128)(2,1)S(1)} %get-tuple-element.25), channel_id=1, source_target_pairs={{0,3},{1,2},{2,1},{3,0},{16,19},{17,18},{18,17},{19,16},{4,7},{5,6... | collective-permute-start | bytes 983048 | tf_op jit(solution)/shard_map/ppermute | solution.py:511
  391.1 59.7 %collective-permute-start.24 = (bf16[8,5,64,128]{3,2,1,0:T(8,128)(2,1)}, bf16[8,5,64,128]{3,2,1,0:T(8,128)(2,1)S(1)}, u32[]{:S(2)}, u32[]{:S(2)}) collective-permute-start(bf16[8,5,64,128]{3,2,1,0:T(8,128)(2,1)} %hold.9), channel_id=1, source_target_pairs={{0,4},{4,0},{8,12},{12,8},{1,5},{5,1},{9,13},{13,9},{2,6},{6,2},{1... | collective-permute-start | bytes 1966088 | tf_op jit(solution)/shard_map/ppermute | solution.py:505
  391.2 59.7 %collective-permute-start.25 = (bf16[8,5,64,128]{3,2,1,0:T(8,128)(2,1)}, bf16[8,5,64,128]{3,2,1,0:T(8,128)(2,1)S(1)}, u32[]{:S(2)}, u32[]{:S(2)}) collective-permute-start(bf16[8,5,64,128]{3,2,1,0:T(8,128)(2,1)} %hold.10), channel_id=1, source_target_pairs={{0,8},{4,12},{8,0},{12,4},{1,9},{5,13},{9,1},{13,5},{2,10},{6,14},... | collective-permute-start | bytes 1966088 | tf_op jit(solution)/shard_map/ppermute | solution.py:505
  391.3 59.6 %collective-permute-start.26 = (bf16[8,5,64,128]{3,2,1,0:T(8,128)(2,1)}, bf16[8,5,64,128]{3,2,1,0:T(8,128)(2,1)S(1)}, u32[]{:S(2)}, u32[]{:S(2)}) collective-permute-start(bf16[8,5,64,128]{3,2,1,0:T(8,128)(2,1)} %hold.11), channel_id=1, source_target_pairs={{0,12},{4,8},{8,4},{12,0},{1,13},{5,9},{9,5},{13,1},{2,14},{6,10},... | collective-permute-start | bytes 1966088 | tf_op jit(solution)/shard_map/ppermute | solution.py:505
  452.1 275.1 %all-to-all-start.1 = ((bf16[864,56,128]{2,1,0:T(8,128)(2,1)}), bf16[864,56,128]{2,1,0:T(8,128)(2,1)}, u32[]{:S(2)}, u32[]{:S(2)}) async-start(bf16[864,56,128]{2,1,0:T(8,128)(2,1)} %hold.12), calls=%async_computation.1 | async-start | bytes 24772608 | tf_op jit(solution)/shard_map/all_to_all | solution.py:501
  456.4 120.9 %collective-permute-start.23 = (bf16[4,27,8,128]{3,2,1,0:T(8,128)(2,1)S(1)}, bf16[4,27,8,128]{3,2,1,0:T(8,128)(2,1)S(1)}, u32[]{:S(2)}, u32[]{:S(2)}) collective-permute-start(bf16[4,27,8,128]{3,2,1,0:T(8,128)(2,1)S(1)} %get-tuple-element.32), channel_id=1, source_target_pairs={{0,19},{1,18},{2,17},{3,16},{16,3},{17,2},{18,1},{19,0},{4,23},{5,... | collective-permute-start | bytes 663560 | tf_op jit(solution)/shard_map/ppermute | solution.py:511
  458.5 118.8 %collective-permute-start.22 = (bf16[4,27,8,128]{3,2,1,0:T(8,128)(2,1)S(1)}, bf16[4,27,8,128]{3,2,1,0:T(8,128)(2,1)S(1)}, u32[]{:S(2)}, u32[]{:S(2)}) collective-permute-start(bf16[4,27,8,128]{3,2,1,0:T(8,128)(2,1)S(1)} %get-tuple-element.33), channel_id=1, source_target_pairs={{0,18},{1,19},{2,16},{3,17},{16,2},{17,3},{18,0},{19,1},{4,22},{5,... | collective-permute-start | bytes 663560 | tf_op jit(solution)/shard_map/ppermute | solution.py:511
  458.8 118.4 %collective-permute-start.21 = (bf16[4,27,8,128]{3,2,1,0:T(8,128)(2,1)S(1)}, bf16[4,27,8,128]{3,2,1,0:T(8,128)(2,1)S(1)}, u32[]{:S(2)}, u32[]{:S(2)}) collective-permute-start(bf16[4,27,8,128]{3,2,1,0:T(8,128)(2,1)S(1)} %get-tuple-element.34), channel_id=1, source_target_pairs={{0,17},{1,16},{2,19},{3,18},{16,1},{17,0},{18,3},{19,2},{4,21},{5,... | collective-permute-start | bytes 663560 | tf_op jit(solution)/shard_map/ppermute | solution.py:511
  460.2 117.0 %collective-permute-start.20 = (bf16[4,27,8,128]{3,2,1,0:T(8,128)(2,1)S(1)}, bf16[4,27,8,128]{3,2,1,0:T(8,128)(2,1)S(1)}, u32[]{:S(2)}, u32[]{:S(2)}) collective-permute-start(bf16[4,27,8,128]{3,2,1,0:T(8,128)(2,1)S(1)} %get-tuple-element.35), channel_id=1, source_target_pairs={{0,16},{1,17},{2,18},{3,19},{16,0},{17,1},{18,2},{19,3},{4,20},{5,... | collective-permute-start | bytes 663560 | tf_op jit(solution)/shard_map/ppermute | solution.py:511
  462.3 74.6 %collective-permute-start.18 = (bf16[4,27,8,128]{3,2,1,0:T(8,128)(2,1)S(1)}, bf16[4,27,8,128]{3,2,1,0:T(8,128)(2,1)S(1)}, u32[]{:S(2)}, u32[]{:S(2)}) collective-permute-start(bf16[4,27,8,128]{3,2,1,0:T(8,128)(2,1)S(1)} %get-tuple-element.37), channel_id=1, source_target_pairs={{0,2},{1,3},{2,0},{3,1},{16,18},{17,19},{18,16},{19,17},{4,6},{5,7... | collective-permute-start | bytes 663560 | tf_op jit(solution)/shard_map/ppermute | solution.py:511
  (38 other events, 1044.2 us)
